TPU v7x, 32 devices: a whole 2x2x4 slice. The times are simulated.
32 devices in a mesh: ctx: 32 (over z, y, x, core), tp: 1.
Axes of the slice: x: 2, y: 2, z: 4, core: 2. Of those that a mesh axis runs over, the one named last changes fastest.
Arguments:
- streams: bfloat16 [3, 4096, 8192], P(None, 'ctx', 'tp'), may hold values from -6 to 6
- short_filter: float32 [3, 7, 512], P(None, None, 'tp'), may hold values from -2.5 to 2.5
- residues: float32 [16, 512], P(None, 'tp'), may hold values from -0.125 to 0.125
- rates: float32 [16, 512], P(None, 'tp'), may hold values from 2.4414062e-06 to 0.04
- skip: float32 [8192], P('tp'), may hold values from 0.5 to 1.5
- out_weight: bfloat16 [4096, 8192], P('ctx', 'tp'), may hold values from -0.0625 to 0.0625
- out_cotangent: bfloat16 [4096, 4096], P('ctx', 'tp'), may hold values from -12 to 12
Outputs:
- output: bfloat16 [4096, 4096], P('ctx', 'tp')
- grad_streams: bfloat16 [3, 4096, 8192], P(None, 'ctx', 'tp')
- grad_short: float32 [3, 7, 512], P(None, None, 'tp')
- grad_skip: float32 [8192], P('tp')
- grad_weight: float32 [4096, 8192], P('ctx', 'tp')
All inputs are finite; a program needn't handle non-finite values.
Results may differ from a plain program's by a relative error of at most 0.034.
Values may be sent and summed in bfloat16 or wider, within the bound.
No kernel may reach another device: no remote copies, remote signals or barrier semaphores. Data moves between devices by JAX's collectives and lax.ppermute only.
A program may use at most 320 MiB of HBM per device.

v0:
```python
import jax
import jax.numpy as jnp
from jax import lax
from jax.sharding import PartitionSpec as P

BLOCK = 256


highest = lax.Precision.HIGHEST


def entering_2(part, axis, combine, identity, reverse):
    count = lax.axis_size(axis)
    place = lax.axis_index(axis)
    ahead = count - 1 - place if reverse else place
    gathered = jax.tree.map(lambda a: lax.all_gather(a, axis), part)
    state = jax.tree.map(lambda a, e: jnp.zeros_like(a) + jnp.asarray(e, a.dtype), part, identity)

    def one(hop, state):
        source = count - 1 - hop if reverse else hop
        return combine(
            state, jax.tree.map(lambda a: lax.dynamic_index_in_dim(a, source, 0, False), gathered)
        )

    return lax.fori_loop(0, ahead, one, state)


def passed_along(block, axis, distance):
    devices = range(lax.axis_size(axis))
    route = [(i - distance, i) for i in devices if i - distance in devices]
    return lax.ppermute(block, axis, route)


def modal_tables(residues, rates, length, row_count):
    positions = jnp.arange(length, dtype=jnp.float32)
    profile = jnp.sum(
        residues[:, None, :] * jnp.exp(-rates[:, None, :] * positions[None, :, None]), axis=0
    )
    counter = jnp.arange(length, dtype=jnp.int32)
    offset = counter[:, None] - counter[None, :]
    toeplitz = jnp.where(
        (offset >= 0)[:, :, None], jnp.take(profile, jnp.maximum(offset, 0), axis=0), 0.0
    )
    inflow = jnp.exp(-rates[None] * (length - 1.0 - positions)[:, None, None])
    carried = residues[None] * jnp.exp(-rates[None] * (positions + 1.0)[:, None, None])
    block_decay = jnp.exp(-rates * length)
    places = jnp.arange(row_count, dtype=jnp.float32)
    entering = residues[None] * jnp.exp(-rates[None] * (places + 1.0)[:, None, None])
    device_decay = jnp.exp(-rates * row_count)
    return (toeplitz, inflow, carried, block_decay, entering, device_decay)


def local_pass(source, toeplitz, inflow, carried, block_decay):
    state = jnp.zeros((inflow.shape[1],) + source.shape[1:], jnp.float32)
    local = jnp.einsum("tsg,sgc->tgc", toeplitz, source, precision=highest)
    local = local + jnp.einsum("tmg,mgc->tgc", carried, state, precision=highest)
    state = block_decay[:, :, None] * state + jnp.einsum(
        "smg,sgc->mgc", inflow, source, precision=highest
    )
    return (local, state)


def combine(earlier, later):
    return (earlier[0] * later[0], later[0][:, :, None] * earlier[1] + later[1])


def states_before(ending, device_decay):
    neutral = (jnp.ones_like(device_decay), jnp.zeros_like(ending))
    result = entering_2((device_decay, ending), "ctx", combine, neutral, False)[1]
    return result


def states_after(ending, device_decay):
    neutral = (jnp.ones_like(device_decay), jnp.zeros_like(ending))
    result = entering_2((device_decay, ending), "ctx", combine, neutral, True)[1]
    return result


def shards(streams, short_filter, residues, rates, skip, out_weight, out_cotangent):
    row_count = streams.shape[1]
    channels = streams.shape[2]
    groups = residues.shape[1]
    members = channels // groups
    reach = short_filter.shape[1] - 1
    length = min(BLOCK, row_count)
    taps = jnp.repeat(short_filter, members, axis=2)
    rim = passed_along(streams[:, row_count - reach :, :], "ctx", 1)
    padded = jnp.concatenate([rim, streams], axis=1)
    smoothed = jnp.zeros(streams.shape, jnp.float32)
    for lag in range(reach + 1):
        smoothed = smoothed + taps[:, lag, None, :] * padded[
            :, reach - lag : reach - lag + row_count, :
        ].astype(jnp.float32)
    mixed = lax.optimization_barrier((smoothed[1] * smoothed[2]).astype(jnp.bfloat16)).astype(
        jnp.float32
    )
    toeplitz, inflow, carried, block_decay, entering, device_decay = modal_tables(
        residues, rates, length, row_count
    )
    local, ending = local_pass(
        mixed.reshape(row_count, groups, members), toeplitz, inflow, carried, block_decay
    )
    before = states_before(ending, device_decay)
    long_part = local + jnp.einsum("tmg,mgc->tgc", entering, before, precision=highest)
    field = long_part.reshape(row_count, channels) + skip * mixed
    gated = (smoothed[0] * field).astype(jnp.bfloat16)
    weights = lax.all_gather(out_weight, "ctx", axis=0, tiled=True)
    partial_value = lax.dot_general(
        gated, weights, (((1,), (1,)), ((), ())), preferred_element_type=jnp.float32
    )
    output = lax.psum_scatter(
        partial_value.astype(jnp.bfloat16), "tp", scatter_dimension=1, tiled=True
    )
    cotangent = lax.all_gather(out_cotangent, "tp", axis=1, tiled=True)
    upstream = jnp.dot(cotangent, weights, preferred_element_type=jnp.float32)
    grad_weight = lax.psum_scatter(
        lax.dot_general(
            cotangent, gated, (((0,), (0,)), ((), ())), preferred_element_type=jnp.float32
        ).astype(jnp.bfloat16),
        "ctx",
        scatter_dimension=0,
        tiled=True,
    ).astype(jnp.float32)
    grad_field = upstream * smoothed[0]
    skip_part = jnp.sum(grad_field * mixed, axis=0)
    flipped = grad_field[::-1].reshape(row_count, groups, members)
    back_local, back_end = local_pass(flipped, toeplitz, inflow, carried, block_decay)
    after = states_after(back_end, device_decay)
    back_part = back_local + jnp.einsum("tmg,mgc->tgc", entering, after, precision=highest)
    grad_mixed = back_part.reshape(row_count, channels)[::-1] + skip * grad_field
    grad_smoothed = jnp.stack(
        [upstream * field, grad_mixed * smoothed[2], grad_mixed * smoothed[1]]
    )
    tap_rows = []
    for lag in range(reach + 1):
        product = grad_smoothed * padded[:, reach - lag : reach - lag + row_count, :].astype(
            jnp.float32
        )
        tap_rows.append(jnp.sum(product.reshape(3, row_count, groups, members), axis=(1, 3)))
    tap_part = jnp.stack(tap_rows, axis=1)
    grad_skip, grad_short = lax.psum((skip_part, tap_part), "ctx")
    rim_next = passed_along(grad_smoothed[:, :reach, :], "ctx", -1)
    padded_back = jnp.concatenate([grad_smoothed, rim_next], axis=1)
    grad_streams = jnp.zeros(streams.shape, jnp.float32)
    for lag in range(reach + 1):
        grad_streams = (
            grad_streams + taps[:, lag, None, :] * padded_back[:, lag : lag + row_count, :]
        )
    return (output, grad_streams.astype(jnp.bfloat16), grad_short, grad_skip, grad_weight)


def solution(mesh):
    return jax.shard_map(
        shards,
        mesh=mesh,
        in_specs=(
            P(None, "ctx", "tp"),
            P(None, None, "tp"),
            P(None, "tp"),
            P(None, "tp"),
            P("tp"),
            P("ctx", "tp"),
            P("ctx", "tp"),
        ),
        out_specs=(
            P("ctx", "tp"),
            P(None, "ctx", "tp"),
            P(None, None, "tp"),
            P("tp"),
            P("ctx", "tp"),
        ),
        check_vma=False,
    )
```

profile of v0, /device:TPU:0, one launch (start us, length us, event | category | flops | bytes accessed | tf_op | source)
XLA Modules:
  0.0 2029.5 jit_solution(11290992194605988770)
XLA Ops:
  8.4 2.4 collective-permute-start
  10.8 1.4 broadcast_multiply_fusion
  12.3 4.3 broadcast_in_dim.26
  16.5 5.2 reshape.102
  23.8 19.5 fusion.15
  43.3 4.5 copy-done.1
  47.9 1.8 multiply_convert_fusion.1
  49.6 3.2 copy.59
  52.9 6.2 bitcast_add_fusion.3
  59.1 3.6 copy.65
  65.4 64.3 %gather_fusion = f32[16384,512]{1,0:T(8,128)} fusion(f32[128,512]{1,0:T(8,128)S(1)} %multiply_reduce_fusion, s32[16384]{0:T(1024)S(1)} %bitcast_clamp_fusion), kind=kCustom, calls=%fused_computation | custom fusion | bytes 67174400 | tf_op jit(solution)/shard_map/jit(_take)/gather | solution.py:42
  129.7 35.7 %copy.60 = f32[128,128,512]{1,0,2:T(8,128)} copy(f32[128,128,512]{2,1,0:T(8,128)} %bitcast.107) | data formatting | bytes 67108864 | tf_op jit(solution)/shard_map/jit(_take)/gather | solution.py:42
  165.4 7.9 fusion.41
  173.3 31.4 %fusion.1 = f32[512,16,128]{2,1,0:T(8,128)} fusion(bf16[128,512,16]{0,2,1:T(8,128)(2,1)S(1)} %bitcast.111, f32[128,128,512]{1,0,2:T(8,128)} %copy.60, pred[128,128]{1,0:T(8,128)(4,1)S(1)} %get-tuple-element.220, pred[128,128]{1,0:T(8,128)(4,1)S(1)} %get-tuple-element.221), kind=kOutput, calls=%fused_computation.8 | convolution fusion | flops 1627389952 | bytes 39878656 | tf_op jit(solution)/shard_map/tsg,sgc->tgc/dot_general | solution.py:55
  205.2 3.7 copy.66
  209.0 9.9 add_add_fusion.1
  218.9 5.8 copy.67
  224.7 318.5 %all-gather.8.cloned.1.call-done = bf16[4096,8192]{1,0:T(8,128)(2,1)} async-done(((bf16[128,8192]{1,0:T(8,128)(2,1)}), bf16[4096,8192]{1,0:T(8,128)(2,1)}) %all-gather.8.cloned.1.call-update) | async-done | bytes 67108880 | tf_op jit(solution)/shard_map/all_gather | solution.py:107
  543.2 30.9 %fusion.36 = (f32[8192]{0:T(1024)}, f32[128,8192]{1,0:T(8,128)}, bf16[128,8192]{1,0:T(8,128)(2,1)}, f32[1,128,8192]{2,1,0:T(8,128)}) fusion(bf16[128,8192]{1,0:T(8,128)(2,1)S(1)} %copy-done.3, f32[3,128,8192]{2,1,0:T(8,128)} %copy-done.1, f32[128,8192]{1,0:T(8,128)} %copy.67, f32[8192]{0:T(1024)S(1)} %copy-done.26, bf16[128,4096]{1,0:T(8,128)(2,1)S(1)} %copy-done, ...), kind=kOutput, calls=%fused_computation.74 | convolution fusion | flops 8599363584 | bytes 89194496 | tf_op jit(solution)/shard_map/dot_general | solution.py:115
  574.1 32.7 %rev.6 = f32[128,8192]{1,0:T(8,128)} reverse(f32[128,8192]{1,0:T(8,128)} %get-tuple-element.195), dimensions={0} | reverse | bytes 8388608 | tf_op jit(solution)/shard_map/rev | solution.py:126
  606.8 5.6 copy.68
  612.4 10.0 bitcast_add_fusion.2
  622.4 3.6 copy.69
  626.3 57.1 %fusion = f32[512,16,128]{2,1,0:T(8,128)} fusion(f32[128,512,16]{0,2,1:T(8,128)} %bitcast.109, f32[128,128,512]{1,0,2:T(8,128)} %copy.60, pred[128,128]{1,0:T(8,128)(4,1)S(1)} %get-tuple-element.220, pred[128,128]{1,0:T(8,128)(4,1)S(1)} %get-tuple-element.221), kind=kOutput, calls=%fused_computation.7 | convolution fusion | flops 1627389952 | bytes 41975808 | tf_op jit(solution)/shard_map/tsg,sgc->tgc/dot_general | solution.py:55
  683.3 55.9 %all-gather.14.cloned.1.call-done = f32[512,512,16]{1,2,0:T(8,128)} async-done(((f32[16,512,16]{1,2,0:T(8,128)}), f32[512,512,16]{1,2,0:T(8,128)}) %all-gather.14.cloned.1.call-update) | async-done | bytes 16777232 | tf_op jit(solution)/shard_map/all_gather | solution.py:16
  739.3 64.5 %while.27 = (s32[]{:T(128)}, f32[16,512,16]{1,2,0:T(8,128)S(1)}, s32[]{:T(128)}, f32[32,16,512]{2,1,0:T(8,128)}, f32[32,16,512,16]{2,3,1,0:T(8,128)}, /*index=5*/s32[]{:T(128)}, s32[]{:T(128)}, s32[]{:T(128)}, s32[]{:T(128)}) while((s32[]{:T(128)}, f32[16,512,16]{1,2,0:T(8,128)S(1)}, s32[]{:T(128)}, f32[32,16,512]{2,1,0:T(8,128)}, ...), condition=%wide.region_4.5_spmd, body=%wide.region_3.4_spmd.sunk | while | flops 262150 | bytes 1671323 | solution.py:25
  740.1 1.3 bitcast_add_fusion.7
  742.2 1.3 bitcast_add_fusion.7
  744.3 1.3 bitcast_add_fusion.7
  746.3 1.3 bitcast_add_fusion.7
  748.4 1.3 bitcast_add_fusion.7
  750.5 1.3 bitcast_add_fusion.7
  765.0 1.3 bitcast_add_fusion.7
  767.1 1.3 bitcast_add_fusion.7
  769.1 1.3 bitcast_add_fusion.7
  771.2 1.3 bitcast_add_fusion.7
  803.8 3.7 copy.70
  807.5 9.9 add_add_fusion
  817.4 5.6 copy.71
  823.0 32.5 %rev.7 = f32[128,8192]{1,0:T(8,128)} reverse(f32[128,8192]{1,0:T(8,128)} %copy.71), dimensions={0} | reverse | bytes 8388608 | tf_op jit(solution)/shard_map/rev | solution.py:130
  855.5 11.0 multiply_bitcast_fusion.1
  866.5 23.6 %fusion.21 = (f32[3,8192]{1,0:T(4,128)S(1)}, f32[3,8192]{1,0:T(4,128)}, f32[3,8192]{1,0:T(4,128)S(1)}, f32[3,8192]{1,0:T(4,128)}, f32[3,8192]{1,0:T(4,128)}, /*index=5*/f32[3,8192]{1,0:T(4,128)}, f32[3,8192]{1,0:T(4,128)S(1)}) fusion(bf16[3,128,8192]{2,1,0:T(8,128)(2,1)} %param.11, bf16[3,6,8192]{2,1,0:T(8,128)(2,1)S(1)} %copy-done.11, ...), kind=kLoop, calls=%fused_computation.48 | loop fusion | flops 128802816 | bytes 19857408 | tf_op jit(solution)/shard_map/reduce_sum | solution.py:139
  890.1 2.2 reduce_sum.103
  892.4 1.4 reduce_sum.104
  894.4 2.1 reduce_sum.106
  896.5 2.1 reduce_sum.112
  898.5 2.1 reduce_sum.118
  904.2 1.4 reduce_sum.107
  906.2 1.4 reduce_sum.113
  908.2 1.4 reduce_sum.142
  910.2 1.4 reduce_sum.145
  912.2 1.4 reduce_sum.148
  914.3 1.4 reduce_sum.151
  916.6 25.4 %convert_bitcast_fusion = bf16[4096,8192]{0,1:T(8,128)(2,1)} fusion(bf16[128,8192]{1,0:T(8,128)(2,1)S(1)} %copy-done.2, bf16[128,4096]{1,0:T(8,128)(2,1)S(1)} %copy-done), kind=kOutput, calls=%fused_computation.5 | convolution fusion | flops 8623489024 | bytes 70254592 | tf_op jit(solution)/shard_map/dot_general | solution.py:117
  942.1 10.6 pad_maximum_fusion.1
  952.6 2.1 slice.134
  956.0 29.0 %convolution_convert_fusion = bf16[128,4096]{1,0:T(8,128)(2,1)} fusion(bf16[128,8192]{1,0:T(8,128)(2,1)S(1)} %copy-done.2, bf16[4096,8192]{1,0:T(8,128)(2,1)} %all-gather.8.cloned.1.call-done), kind=kOutput, calls=%fused_computation.72 | convolution fusion | flops 8590458880 | bytes 70254592 | tf_op jit(solution)/shard_map/dot_general | solution.py:108
  985.0 47.7 %all-reduce.7.cloned.1.call-done = (f32[3,7,512]{2,0,1:T(4,128)}, f32[8192]{0:T(1024)}) async-done(((f32[3,7,512]{2,0,1:T(4,128)}, f32[8192]{0:T(1024)}), (f32[3,7,512]{2,0,1:T(4,128)}, f32[8192]{0:T(1024)})) %all-reduce.7.cloned.1.call-update) | async-done | bytes 75792 | tf_op jit(solution)/shard_map/psum | solution.py:141
  1032.7 1.5 copy.72
  1034.2 10.0 pad_maximum_fusion
  1044.2 36.4 %fusion.24 = bf16[3,128,8192]{2,1,0:T(8,128)(2,1)} fusion(f32[3,134,8192]{2,1,0:T(8,128)} %pad_maximum_fusion, f32[3,8192]{1,0:T(4,128)S(1)} %copy-done.13, f32[3,8192]{1,0:T(4,128)S(1)} %copy-done.15, f32[3,8192]{1,0:T(4,128)S(1)} %copy-done.17, f32[3,8192]{1,0:T(4,128)S(1)} %copy-done.19, f32[3,8192]{1,0:T(4,128)S(1)} %copy-done.21, ...), kind=kLoop, calls=%fused_computation.52 | loop fusion | flops 50331648 | bytes 95059968 | tf_op jit(solution)/shard_map/convert_element_type | solution.py:149
  1080.6 931.5 %all-reduce.5.cloned.1.call-done = bf16[4096,8192]{0,1:T(8,128)(2,1)} async-done(((bf16[4096,8192]{0,1:T(8,128)(2,1)}), bf16[4096,8192]{0,1:T(8,128)(2,1)}) %all-reduce.5.cloned.1.call-update) | async-done | bytes 67108880
  2012.2 3.8 dynamic-slice_convert_fusion
  2016.0 5.6 copy.73
  (158 shorter events, 67.4 us)
Async XLA Ops:
  7.2 536.0 %copy-start = (bf16[128,4096]{1,0:T(8,128)(2,1)S(1)}, bf16[128,4096]{1,0:T(8,128)(2,1)}, u32[]{:S(2)}) copy-start(bf16[128,4096]{1,0:T(8,128)(2,1)} %param.17) | copy-start | bytes 3145732
  7.2 197.6 %all-gather.10.cloned.1.call-start = ((), (), s32[]{:S(2)}) async-start(), calls=%async_computation.1 | async-start | bytes 1081344 | tf_op jit(solution)/shard_map/all_gather | solution.py:16
  8.4 15.3 collective-permute-start
  12.2 192.5 %all-gather.12.cloned.1.call-start = ((), (), s32[]{:S(2)}) async-start(), calls=%async_computation.2 | async-start | bytes 17301504 | tf_op jit(solution)/shard_map/all_gather | solution.py:16
  22.3 21.0 %copy-start.12 = (f32[3,8192]{1,0:T(4,128)}, f32[3,8192]{1,0:T(4,128)S(1)}, u32[]{:S(2)}) copy-start(f32[3,8192]{1,0:T(4,128)S(1)} %get-tuple-element.214) | copy-start | bytes 294916
  22.3 21.0 %copy-start.14 = (f32[3,8192]{1,0:T(4,128)}, f32[3,8192]{1,0:T(4,128)S(1)}, u32[]{:S(2)}) copy-start(f32[3,8192]{1,0:T(4,128)S(1)} %get-tuple-element.215) | copy-start | bytes 294916
  22.5 20.8 %copy-start.16 = (f32[3,8192]{1,0:T(4,128)}, f32[3,8192]{1,0:T(4,128)S(1)}, u32[]{:S(2)}) copy-start(f32[3,8192]{1,0:T(4,128)S(1)} %get-tuple-element.216) | copy-start | bytes 294916
  22.5 20.8 %copy-start.18 = (f32[3,8192]{1,0:T(4,128)}, f32[3,8192]{1,0:T(4,128)S(1)}, u32[]{:S(2)}) copy-start(f32[3,8192]{1,0:T(4,128)S(1)} %get-tuple-element.217) | copy-start | bytes 294916
  22.6 20.7 %copy-start.20 = (f32[3,8192]{1,0:T(4,128)}, f32[3,8192]{1,0:T(4,128)S(1)}, u32[]{:S(2)}) copy-start(f32[3,8192]{1,0:T(4,128)S(1)} %get-tuple-element.218) | copy-start | bytes 294916
  22.6 20.7 %copy-start.22 = (f32[3,8192]{1,0:T(4,128)}, f32[3,8192]{1,0:T(4,128)S(1)}, u32[]{:S(2)}) copy-start(f32[3,8192]{1,0:T(4,128)S(1)} %get-tuple-element.219) | copy-start | bytes 294916
  22.7 20.6 %copy-start.24 = (f32[3,1,8192]{2,0,1:T(4,128)}, f32[3,1,8192]{2,0,1:T(4,128)S(1)}, u32[]{:S(2)}) copy-start(f32[3,1,8192]{2,0,1:T(4,128)S(1)} %copy.106) | copy-start | bytes 294916
  22.9 30.0 %copy-start.4 = (f32[16,512]{0,1:T(8,128)}, f32[16,512]{0,1:T(8,128)S(1)}, u32[]{:S(2)}) copy-start(f32[16,512]{0,1:T(8,128)S(1)} %copy.62) | copy-start | bytes 98308
  23.7 29.1 %copy-start.29 = (f32[128]{0:T(128)}, f32[128]{0:T(128)S(1)}, u32[]{:S(2)}) copy-start(f32[128]{0:T(128)S(1)} %iota_subtract_fusion.1) | copy-start | bytes 1540
  23.7 19.6 copy-start.10
  43.3 4.5 copy-start.1
  52.9 10.9 copy-start.27
  62.8 480.4 %all-gather.8.cloned.1.call-start = ((), (), s32[]{:S(2)}) async-start(), calls=%async_computation | async-start | bytes 69206016 | tf_op jit(solution)/shard_map/all_gather | solution.py:107
  63.5 675.7 %all-gather.14.cloned.1.call-start = ((), (), s32[]{:S(2)}) async-start(), calls=%async_computation.3 | async-start | bytes 17301504 | tf_op jit(solution)/shard_map/all_gather | solution.py:16
  129.7 35.8 %copy-start.5 = (f32[16,512]{0,1:T(8,128)S(1)}, f32[16,512]{0,1:T(8,128)}, u32[]{:S(2)}) copy-start(f32[16,512]{0,1:T(8,128)} %copy-done.4) | copy-start | bytes 98308
  204.8 4.2 copy-start.6
  204.8 4.2 copy-start.7
  218.9 324.3 %copy-start.3 = (bf16[128,8192]{1,0:T(8,128)(2,1)S(1)}, bf16[128,8192]{1,0:T(8,128)(2,1)}, u32[]{:S(2)}) copy-start(bf16[128,8192]{1,0:T(8,128)(2,1)} %multiply_convert_fusion.1) | copy-start | bytes 6291460
  218.9 324.3 %copy-start.26 = (f32[8192]{0:T(1024)S(1)}, f32[8192]{0:T(1024)}, u32[]{:S(2)}) copy-start(f32[8192]{0:T(1024)} %param.15) | copy-start | bytes 98308
  574.1 38.3 %copy-start.9 = (f32[16,512]{0,1:T(8,128)S(1)}, f32[16,512]{0,1:T(8,128)}, u32[]{:S(2)}) copy-start(f32[16,512]{0,1:T(8,128)} %copy.64) | copy-start | bytes 98308
  574.1 38.3 %copy-start.30 = (f32[128]{0:T(128)S(1)}, f32[128]{0:T(128)}, u32[]{:S(2)}) copy-start(f32[128]{0:T(128)} %copy-done.29) | copy-start | bytes 1540
  626.1 406.6 %all-reduce.7.cloned.1.call-start = ((), (), s32[]{:S(2)}) async-start(), calls=%async_computation.5 | async-start | bytes 180224 | tf_op jit(solution)/shard_map/psum | solution.py:141
  739.3 68.2 %copy-start.8 = (f32[16,512]{0,1:T(8,128)S(1)}, f32[16,512]{0,1:T(8,128)}, u32[]{:S(2)}) copy-start(f32[16,512]{0,1:T(8,128)} %copy.61) | copy-start | bytes 98308
  855.5 11.0 copy-start.11
  890.1 26.5 %copy-start.2 = (bf16[128,8192]{1,0:T(8,128)(2,1)S(1)}, bf16[128,8192]{1,0:T(8,128)(2,1)}, u32[]{:S(2)}) copy-start(bf16[128,8192]{1,0:T(8,128)(2,1)} %get-tuple-element.202) | copy-start | bytes 6291460
  916.3 1095.9 %all-reduce.5.cloned.1.call-start = ((), (), s32[]{:S(2)}) async-start(), calls=%async_computation.4 | async-start | bytes 134217728
  954.7 79.4 %collective-permute-start.1 = (f32[3,6,8192]{2,1,0:T(8,128)}, f32[3,6,8192]{2,1,0:T(8,128)}, u32[]{:S(2)}, u32[]{:S(2)}) collective-permute-start(f32[3,6,8192]{2,1,0:T(8,128)} %slice.134), channel_id=1, source_target_pairs={{1,0},{2,1},{3,2},{4,3},{5,4},{6,5},{7,6},{8,7},{9,8},{10,9},{11,1... | collective-permute-start | bytes 1769480 | tf_op jit(solution)/shard_map/ppermute | solution.py:31
  1034.1 10.1 copy-start.13
  1034.1 10.1 copy-start.15
  1034.1 10.1 copy-start.17
  1034.1 10.1 copy-start.19
  1034.1 10.1 copy-start.21
  1034.1 10.1 copy-start.23
  1034.1 10.1 copy-start.25
  1080.6 941.0 %copy-start.28 = (f32[8192]{0:T(1024)S(1)}, f32[8192]{0:T(1024)}, u32[]{:S(2)}) copy-start(f32[8192]{0:T(1024)} %get-tuple-element.340) | copy-start | bytes 98308
Sparse Core Ops, SparseCore 0:
  12.3 56.1 all-gather.9
  72.0 113.8 all-gather.11
  188.7 354.4 all-gather.7
  626.2 113.0 all-gather.13
  916.4 116.1 all-reduce.6
  1038.9 973.1 all-reduce.4
where the time goes:
time: 2050 us; the launch traced here: 2030 us
  waiting for transfers between devices  1350 us (66%)
  local copies, waits for them, and re-layouts  268 us (13%)
  matrix products  218 us (11%)
  other arithmetic  168 us (8%)
    unnamed x7, waiting for transfers between devices  932 us
    all_gather x1, waiting for transfers between devices, shards(): weights = lax.all_gather(out_weight, 'ctx', axis=0, tiled=True)  318 us
    gather x2, local copies, waits for them, and re-layouts, modal_tables(): jnp.take(profile, jnp.maximum(offset, 0), axis=0)  100 us
    dot_general x2, matrix products, local_pass(): local = jnp.einsum('tsg,sgc->tgc', toeplitz, source, precision=highest)  88.4 us
    all_gather x3, waiting for transfers between devices, entering_2(): gathered = jax.tree.map(lambda a: lax.all_gather(a, axis), part)  55.9 us
    psum x1, waiting for transfers between devices, shards(): grad_skip, grad_short = lax.psum((skip_part, tap_part), 'ctx')  47.7 us
  transfers between devices with their start and end apart: 8, of which 4 were waited for; matrix products, arithmetic and copies ran while one was open for 19% of the time, Pallas kernels for 0%

commit v1 on v0

v1 whole, which is shorter than its diff:
```python
import functools
import math

import jax
import jax.numpy as jnp
from jax import lax
from jax.experimental import pallas as pl
from jax.experimental.pallas import tpu as pltpu
from jax.sharding import Mesh, PartitionSpec as P

LANES = 128
EDGE = 8
STEP = 8
VMEM = 48 * 1024 * 1024


def at(token, rows):
    start = token * rows
    return pl.ds(start if isinstance(start, int) else pl.multiple_of(start, rows), rows)


def total_of(terms):
    while len(terms) > 1:
        terms = [
            terms[k] + terms[k + 1] if k + 1 < len(terms) else terms[k]
            for k in range(0, len(terms), 2)
        ]
    return terms[0]


def to_token_rows(ref, first, value, rows):
    count = value.shape[0]
    for j in range(rows):
        ref[pl.ds(first * rows + j, count, stride=rows), :] = value[
            :, j * LANES : (j + 1) * LANES
        ].astype(jnp.float32)


def smooth_kernel(
    rows, tok, x_ref, rim_ref, taps_ref, decay_ref, sm_ref, mixed_ref, xt_ref, end_ref, pad, state
):
    modes, lags = decay_ref.shape[0], taps_ref.shape[1]
    first = pl.program_id(0) == 0

    @pl.when(first)
    def _():
        for i in range(3):
            to_token_rows(pad.at[i], 0, rim_ref[i], rows)
        state[...] = jnp.zeros_like(state)

    @pl.when(jnp.logical_not(first))
    def _():
        for i in range(3):
            pad[i, pl.ds(0, EDGE * rows), :] = pad[i, pl.ds(tok * rows, EDGE * rows), :]

    for i in range(3):
        to_token_rows(pad.at[i], EDGE, x_ref[0, i], rows)
        xt_ref[i] = pad[i, pl.ds(EDGE * rows, tok * rows), :]

    def smooth(n, carry):
        base = n * STEP
        results = []
        for i in range(3):
            taps = [taps_ref[i, j] for j in range(lags)]
            window = [
                pad[i, at(base + EDGE - (lags - 1) + k, rows), :] for k in range(STEP + lags - 1)
            ]
            results.append(
                [
                    total_of([taps[j] * window[u + lags - 1 - j] for j in range(lags)])
                    for u in range(STEP)
                ]
            )
            for u in range(STEP):
                sm_ref[i, at(base + u, rows), :] = results[i][u]
        for u in range(STEP):
            mixed_ref[at(base + u, rows), :] = (
                (results[1][u] * results[2][u]).astype(jnp.bfloat16).astype(jnp.float32)
            )
        return carry

    lax.fori_loop(0, tok // STEP, smooth, 0)
    decay = [decay_ref[m] for m in range(modes)]

    def advance(n, held):
        held = list(held)
        for u in range(STEP):
            x = mixed_ref[at(n * STEP + u, rows), :]
            held = [decay[m] * held[m] + x for m in range(modes)]
        return tuple(held)

    held = lax.fori_loop(0, tok // STEP, advance, tuple(state[m] for m in range(modes)))
    for m in range(modes):
        state[m] = held[m]
        end_ref[m] = held[m]


def field_kernel(
    rows,
    tok,
    mixed_ref,
    sm_ref,
    before_ref,
    decay_ref,
    residue_ref,
    skip_ref,
    field_ref,
    gated_ref,
    staged,
    state,
):
    modes = decay_ref.shape[0]

    @pl.when(pl.program_id(0) == 0)
    def _():
        state[...] = before_ref[...]

    decay = [decay_ref[m] for m in range(modes)]
    residue = [residue_ref[m] for m in range(modes)]
    skip = skip_ref[...]

    def advance(n, held):
        held = list(held)
        for u in range(STEP):
            place = at(n * STEP + u, rows)
            x = mixed_ref[place, :]
            held = [decay[m] * held[m] + x for m in range(modes)]
            field = total_of([residue[m] * held[m] for m in range(modes)] + [skip * x])
            field_ref[place, :] = field
            staged[place, :] = sm_ref[0, place, :] * field
        return tuple(held)

    held = lax.fori_loop(0, tok // STEP, advance, tuple(state[m] for m in range(modes)))
    for m in range(modes):
        state[m] = held[m]
    for j in range(rows):
        gated_ref[:, j * LANES : (j + 1) * LANES] = staged[
            pl.ds(j, tok, stride=rows), :
        ].astype(jnp.bfloat16)


def cotangent_kernel(
    rows, tok, up_ref, sm_ref, mixed_ref, decay_ref, upt_ref, end_ref, gskip_ref, state, total
):
    modes = decay_ref.shape[0]

    @pl.when(pl.program_id(0) == 0)
    def _():
        state[...] = jnp.zeros_like(state)
        total[...] = jnp.zeros_like(total)

    to_token_rows(upt_ref, 0, up_ref[...], rows)
    decay = [decay_ref[m] for m in range(modes)]

    def retreat(n, carry):
        held, summed = list(carry[:-1]), carry[-1]
        for u in range(STEP):
            place = at(tok - 1 - (n * STEP + u), rows)
            grad = upt_ref[place, :] * sm_ref[0, place, :]
            summed = summed + grad * mixed_ref[place, :]
            held = [decay[m] * held[m] + grad for m in range(modes)]
        return tuple(held) + (summed,)

    carry = lax.fori_loop(
        0, tok // STEP, retreat, tuple(state[m] for m in range(modes)) + (total[...],)
    )
    for m in range(modes):
        state[m] = carry[m]
        end_ref[m] = carry[m]
    total[...] = carry[-1]
    gskip_ref[...] = carry[-1]


def back_kernel(
    rows,
    tok,
    upt_ref,
    sm_ref,
    field_ref,
    xt_ref,
    after_ref,
    decay_ref,
    residue_ref,
    skip_ref,
    taps_ref,
    out_ref,
    gtaps_ref,
    head_ref,
    tail_ref,
    pad,
    staged,
    state,
    total,
):
    modes, lags = decay_ref.shape[0], taps_ref.shape[1]
    first = pl.program_id(0) == 0

    @pl.when(first)
    def _():
        state[...] = after_ref[...]
        total[...] = jnp.zeros_like(total)
        for i in range(3):
            pad[i, pl.ds(tok * rows, EDGE * rows), :] = jnp.zeros((EDGE * rows, LANES), jnp.float32)

    @pl.when(jnp.logical_not(first))
    def _():
        for i in range(3):
            pad[i, pl.ds(tok * rows, EDGE * rows), :] = pad[i, pl.ds(0, EDGE * rows), :]

    decay = [decay_ref[m] for m in range(modes)]
    residue = [residue_ref[m] for m in range(modes)]
    skip = skip_ref[...]

    def retreat(n, held):
        held = list(held)
        for u in range(STEP):
            place = at(tok - 1 - (n * STEP + u), rows)
            up = upt_ref[place, :]
            grad = up * sm_ref[0, place, :]
            held = [decay[m] * held[m] + grad for m in range(modes)]
            mixed = total_of([residue[m] * held[m] for m in range(modes)] + [skip * grad])
            pad[0, place, :] = up * field_ref[place, :]
            pad[1, place, :] = mixed * sm_ref[2, place, :]
            pad[2, place, :] = mixed * sm_ref[1, place, :]
        return tuple(held)

    held = lax.fori_loop(0, tok // STEP, retreat, tuple(state[m] for m in range(modes)))
    for m in range(modes):
        state[m] = held[m]

    @pl.when(first)
    def _():
        for i in range(3):
            tail_ref[i] = pad[i, pl.ds((tok - EDGE) * rows, EDGE * rows), :]

    for i in range(3):
        head_ref[i] = pad[i, pl.ds(0, EDGE * rows), :]
        taps = [taps_ref[i, j] for j in range(lags)]

        def spread(n, sums, i=i, taps=taps):
            base = n * STEP
            sums = list(sums)
            window = [pad[i, at(base + k, rows), :] for k in range(STEP + lags - 1)]
            for u in range(STEP):
                x = xt_ref[i, at(base + u, rows), :]
                for j in range(lags):
                    sums[j] = sums[j] + x * window[u + j]
                staged[at(base + u, rows), :] = total_of(
                    [taps[j] * window[u + j] for j in range(lags)]
                )
            return tuple(sums)

        sums = lax.fori_loop(
            0, tok // STEP, spread, tuple(total[i, j] for j in range(lags))
        )
        for j in range(lags):
            total[i, j] = sums[j]
            gtaps_ref[i, j] = sums[j]
        for j in range(rows):
            out_ref[0, i, :, j * LANES : (j + 1) * LANES] = staged[
                pl.ds(j, tok, stride=rows), :
            ].astype(jnp.bfloat16)


def whole(shape):
    return pl.BlockSpec(shape, lambda n: (0,) * len(shape))


def call(kernel, name, blocks, ins, in_specs, outs, out_specs, scratch, ops):
    size = sum(math.prod(a.shape) * a.dtype.itemsize for a in list(ins) + list(outs))
    return pl.pallas_call(
        kernel,
        grid=(blocks,),
        in_specs=in_specs,
        out_specs=out_specs,
        out_shape=outs,
        scratch_shapes=scratch,
        compiler_params=pltpu.CompilerParams(vmem_limit_bytes=VMEM),
        cost_estimate=pl.CostEstimate(flops=ops, bytes_accessed=size, transcendentals=0),
        name=name,
    )(*ins)


def shards(streams, short_filter, residues, rates, skip, out_weight, out_cotangent):
    hi, lo = lax.axis_size("hi"), lax.axis_size("lo")
    plane, place = lax.axis_index("hi"), lax.axis_index("lo")
    tok, channels = streams.shape[1:]
    modes, groups = residues.shape
    members = channels // groups
    lags = short_filter.shape[1]
    wide, near = channels // lo, groups // lo
    rows = wide // LANES
    length = tok * lo
    f32 = jnp.float32
    shape = jax.ShapeDtypeStruct

    def mine(a):
        a = lax.dynamic_slice_in_dim(a, place * near, near, a.ndim - 1)
        return jnp.repeat(a, members, axis=-1).reshape(a.shape[:-1] + (rows, LANES))

    taps, residue, rate = mine(short_filter), mine(residues), mine(rates)
    decay = jnp.exp(-rate)
    plane_decay = jnp.exp(-rate * length)
    direct = lax.dynamic_slice_in_dim(skip, place * wide, wide, 0).reshape(rows, LANES)

    own = lax.all_to_all(out_weight.reshape(out_weight.shape[0], lo, wide), "lo", 1, 0)
    weights = lax.all_gather(own.reshape(-1, wide), "hi", axis=0, tiled=True)
    cotangent = lax.all_gather(out_cotangent, "tp", axis=1, tiled=True)
    cotangent = lax.all_gather(cotangent, "lo", axis=0, tiled=True)
    x = lax.all_to_all(streams.reshape(3, tok, lo, wide), "lo", 2, 0)

    forward = [(i, i + 1) for i in range(hi - 1)]
    backward = [(i + 1, i) for i in range(hi - 1)]
    rim = lax.ppermute(x[lo - 1, :, tok - EDGE :, :], "hi", forward).astype(f32)

    flat = tok * rows
    up_blocks = pl.BlockSpec((flat, LANES), lambda n: (n, 0))
    up_three = pl.BlockSpec((3, flat, LANES), lambda n: (0, n, 0))
    up_one = pl.BlockSpec((1, flat, LANES), lambda n: (0, n, 0))
    down_blocks = pl.BlockSpec((flat, LANES), lambda n: (lo - 1 - n, 0))
    down_three = pl.BlockSpec((3, flat, LANES), lambda n: (0, lo - 1 - n, 0))
    down_one = pl.BlockSpec((1, flat, LANES), lambda n: (0, lo - 1 - n, 0))
    taps_spec = whole((3, lags, rows, LANES))
    mode_spec = whole((modes, rows, LANES))
    skip_spec = whole((rows, LANES))
    edge_spec = whole((3, EDGE * rows, LANES))
    states = pltpu.VMEM((modes, rows, LANES), f32)
    padded = pltpu.VMEM((3, (tok + EDGE) * rows, LANES), f32)
    work = length * wide

    smoothed, mixed, xt, ending = call(
        functools.partial(smooth_kernel, rows, tok),
        "smooth",
        lo,
        (x, rim, taps, decay),
        [
            pl.BlockSpec((1, 3, tok, wide), lambda n: (n, 0, 0, 0)),
            whole((3, EDGE, wide)),
            taps_spec,
            mode_spec,
        ],
        [
            shape((3, length * rows, LANES), f32),
            shape((length * rows, LANES), f32),
            shape((3, length * rows, LANES), f32),
            shape((modes, rows, LANES), f32),
        ],
        [up_three, up_blocks, up_three, mode_spec],
        [padded, states],
        work * (6 * lags + 2 * modes),
    )

    def entering(end, later):
        gathered = lax.all_gather(end, "hi")
        held = jnp.zeros_like(end)
        for hop in reversed(range(hi)) if later else range(hi):
            used = hop > plane if later else hop < plane
            held = jnp.where(used, plane_decay * held + gathered[hop], held)
        return held

    before = entering(ending, False)
    field, gated = call(
        functools.partial(field_kernel, rows, tok),
        "field",
        lo,
        (mixed, smoothed, before, decay, residue, direct),
        [up_blocks, up_one, mode_spec, mode_spec, mode_spec, skip_spec],
        [shape((length * rows, LANES), f32), shape((length, wide), jnp.bfloat16)],
        [up_blocks, pl.BlockSpec((tok, wide), lambda n: (n, 0))],
        [pltpu.VMEM((flat, LANES), f32), states],
        work * 4 * modes,
    )

    partial_grad = lax.dot_general(
        cotangent, gated, (((0,), (0,)), ((), ())), preferred_element_type=f32
    ).astype(jnp.bfloat16)
    reduced = lax.psum_scatter(partial_grad, "hi", scatter_dimension=0, tiled=True)
    grad_weight = lax.all_to_all(reduced.reshape(lo, -1, wide), "lo", 0, 1)
    grad_weight = grad_weight.reshape(-1, channels).astype(f32)

    upstream = jnp.dot(cotangent, weights, preferred_element_type=f32)
    partial_out = lax.dot_general(
        gated, weights, (((1,), (1,)), ((), ())), preferred_element_type=f32
    ).astype(jnp.bfloat16)
    output = lax.psum_scatter(partial_out, "lo", scatter_dimension=0, tiled=True)
    output = lax.psum_scatter(output, "tp", scatter_dimension=1, tiled=True)

    upt, back_end, grad_skip = call(
        functools.partial(cotangent_kernel, rows, tok),
        "cotangent",
        lo,
        (upstream, smoothed, mixed, decay),
        [
            pl.BlockSpec((tok, wide), lambda n: (lo - 1 - n, 0)),
            down_one,
            down_blocks,
            mode_spec,
        ],
        [
            shape((length * rows, LANES), f32),
            shape((modes, rows, LANES), f32),
            shape((rows, LANES), f32),
        ],
        [down_blocks, mode_spec, skip_spec],
        [states, pltpu.VMEM((rows, LANES), f32)],
        work * (2 * modes + 3),
    )
    after = entering(back_end, True)
    grads, grad_taps, head, tail = call(
        functools.partial(back_kernel, rows, tok),
        "back",
        lo,
        (upt, smoothed, field, xt, after, decay, residue, direct, taps),
        [
            down_blocks,
            down_three,
            down_blocks,
            down_three,
            mode_spec,
            mode_spec,
            mode_spec,
            skip_spec,
            taps_spec,
        ],
        [
            shape((lo, 3, tok, wide), jnp.bfloat16),
            shape((3, lags, rows, LANES), f32),
            shape((3, EDGE * rows, LANES), f32),
            shape((3, EDGE * rows, LANES), f32),
        ],
        [
            pl.BlockSpec((1, 3, tok, wide), lambda n: (lo - 1 - n, 0, 0, 0)),
            taps_spec,
            edge_spec,
            edge_spec,
        ],
        [
            padded,
            pltpu.VMEM((flat, LANES), f32),
            states,
            pltpu.VMEM((3, lags, rows, LANES), f32),
        ],
        work * (4 * modes + 12 * lags),
    )

    beyond = lax.ppermute(head, "hi", backward).reshape(3, EDGE, rows, LANES)
    tail = tail.reshape(3, EDGE, rows, LANES)
    joined = jnp.concatenate([tail, beyond], axis=1)
    extra = jnp.concatenate([jnp.zeros_like(tail), beyond], axis=1)
    last = xt[:, -EDGE * rows :, :].reshape(3, EDGE, rows, LANES)
    ends = sum(taps[:, j, None] * joined[:, j : j + EDGE] for j in range(lags))
    grads = lax.dynamic_update_slice(
        grads,
        ends.reshape(1, 3, EDGE, wide).astype(jnp.bfloat16),
        (lo - 1, 0, tok - EDGE, 0),
    )
    grad_taps = grad_taps + jnp.stack(
        [jnp.sum(last * extra[:, j : j + EDGE], axis=1) for j in range(lags)], axis=1
    )
    grad_streams = lax.all_to_all(grads, "lo", 0, 2).reshape(3, tok, channels)

    grad_taps = jnp.sum(grad_taps.reshape(3 * lags * near, members), axis=1)
    small = jnp.concatenate([grad_skip.reshape(-1), grad_taps])
    small = jnp.sum(lax.all_gather(small, ("hi", "lo")).reshape(hi, lo, -1), axis=0)
    grad_skip = small[:, :wide].reshape(channels)
    grad_short = jnp.moveaxis(small[:, wide:].reshape(lo, 3, lags, near), 0, 2)
    return output, grad_streams, grad_short.reshape(3, lags, groups), grad_skip, grad_weight


def solution(mesh):
    count, parts = mesh.shape["ctx"], mesh.shape["tp"]
    lo = math.gcd(count, 8)
    cut = Mesh(mesh.devices.reshape(count // lo, lo, parts), ("hi", "lo", "tp"))
    ctx = ("hi", "lo")
    return jax.shard_map(
        shards,
        mesh=cut,
        in_specs=(
            P(None, ctx, "tp"),
            P(None, None, "tp"),
            P(None, "tp"),
            P(None, "tp"),
            P("tp"),
            P(ctx, "tp"),
            P(ctx, "tp"),
        ),
        out_specs=(
            P(ctx, "tp"),
            P(None, ctx, "tp"),
            P(None, None, "tp"),
            P("tp"),
            P(ctx, "tp"),
        ),
        check_vma=False,
    )
```

time: 2050 us -> 686 us (0.33)
  waiting for transfers between devices: 1350 us -> 402 us
  local copies, waits for them, and re-layouts: 268 us -> 64.8 us
  matrix products: 218 us -> 40.4 us
  other arithmetic: 168 us -> 4.53 us
  Pallas kernels: 0 us -> 71 us
  blocking collectives: 0 us -> 69.5 us
    unnamed x7 -> x6, waiting for transfers between devices: 932 us -> 128 us
    all_gather x4 -> x2, waiting for transfers between devices: 374 us -> 64.3 us  [the longest x1 55.5 us: shards(): cotangent = lax.all_gather(cotangent, 'lo', axis=0, tiled=True)]
    dot_general x8 -> x1, matrix products: 163 us -> 14.9 us  [shards(): upstream = jnp.dot(cotangent, weights, preferred_element_type=f32)]
    reduce_scatter x0 -> x2, waiting for transfers between devices: none -> 128 us  [the longest x1 79.8 us: shards(): lax.psum_scatter(partial_grad, 'hi', scatter_dimension=0, tiled=True)]
    gather x2 -> x0, local copies, waits for them, and re-layouts: 100 us -> none  [modal_tables(): jnp.take(profile, jnp.maximum(offset, 0), axis=0)]
    pallas_call x0 -> x4, Pallas kernels: none -> 71 us  [call(): pl.pallas_call(kernel, grid=(blocks,), in_specs=in_specs, out_specs=out_s...]
    rev x3 -> x0, local copies, waits for them, and re-layouts: 70.8 us -> none  [the longest x2 38.3 us: shards(): flipped = grad_field[::-1].reshape(row_count, groups, members)]
    all_to_all x0 -> x3, waiting for transfers between devices: none -> 70.7 us  [the longest x1 70.7 us: shards(): x = lax.all_to_all(streams.reshape(3, tok, lo, wide), 'lo', 2, 0)]
  transfers between devices with their start and end apart: 8 -> 10, of which waited for: 4 -> 8; matrix products, arithmetic and copies ran while one was open for 19% -> 10% of each run, Pallas kernels for 0% -> 7%
where the time goes in v1:
time: 686 us; the launch traced here: 684 us
  waiting for transfers between devices  402 us (59%)
  Pallas kernels  71 us (10%)
  blocking collectives  69.5 us (10%)
  local copies, waits for them, and re-layouts  64.8 us (9%)
  matrix products  40.4 us (6%)
  starting transfers between devices  18.4 us (3%)
  between operations  14.1 us (2%)
    unnamed x6, waiting for transfers between devices  128 us
    reduce_scatter x1, waiting for transfers between devices, shards(): lax.psum_scatter(partial_grad, 'hi', scatter_dimension=0, tiled=True)  79.8 us
    pallas_call x4, Pallas kernels, call(): pl.pallas_call(kernel, grid=(blocks,), in_specs=in_specs, out_specs=out_s...  71 us
    all_to_all x1, waiting for transfers between devices, shards(): x = lax.all_to_all(streams.reshape(3, tok, lo, wide), 'lo', 2, 0)  70.7 us
    all_gather x1, waiting for transfers between devices, shards(): cotangent = lax.all_gather(cotangent, 'lo', axis=0, tiled=True)  55.5 us
    reduce_scatter x1, waiting for transfers between devices, shards(): lax.psum_scatter(partial_out, 'lo', scatter_dimension=0, tiled=True)  48.5 us
    all_gather x2, blocking collectives, entering(): gathered = lax.all_gather(end, 'hi')  37.7 us
    unnamed x30, local copies, waits for them, and re-layouts  37.3 us
  transfers between devices with their start and end apart: 10, of which 8 were waited for; matrix products, arithmetic and copies ran while one was open for 10% of the time, Pallas kernels for 7%

profile of v1, /device:TPU:0, one launch (start us, length us, event | category | flops | bytes accessed | tf_op | source)
XLA Modules:
  0.0 684.5 jit_solution(9607823677711408732)
XLA Ops:
  7.2 4.1 copy.39
  11.3 31.8 %all_to_all.54 = bf16[1,128,8,1024]{1,3,0,2:T(8,128)(2,1)S(1)} all-to-all(bf16[1,128,8,1024]{1,3,0,2:T(8,128)(2,1)} %bitcast.106), channel_id=1, replica_groups=mesh['hi'=4,'lo'=8,'tp'=1] {'lo'}, dimensions={2} | all-to-all | bytes 4194304 | tf_op jit(solution)/shard_map/all_to_all | solution.py:306
  43.1 2.6 copy.41
  45.7 0.0 all-gather.8.cloned.1.call-start
  45.7 0.7 all-gather.8.cloned.1.call-update
  46.4 8.7 %copy.37 = bf16[3,128,8192]{1,2,0:T(8,128)(2,1)} copy(bf16[3,128,8192]{2,1,0:T(8,128)(2,1)} %param.7) | data formatting | bytes 12582912 | tf_op args[0]
  55.1 8.7 %copy.38 = bf16[1,3,128,8,1024]{4,2,1,0,3:T(8,128)(2,1)} copy(bf16[1,3,128,8,1024]{2,4,3,1,0:T(8,128)(2,1)} %bitcast.102) | data formatting | bytes 12582912 | tf_op jit(solution)/shard_map/broadcast_in_dim;reshape | solution.py:310
  63.8 4.8 all-to-all-start
  68.6 0.0 reduce-scatter.5.cloned.1.call-start
  68.7 0.1 constant_dynamic-slice_fusion.1
  68.8 0.8 multiply_exponential_fusion
  69.5 70.7 %all-to-all-done = bf16[1,3,128,8,1024]{4,2,1,0,3:T(8,128)(2,1)} async-done(((bf16[1,3,128,8,1024]{4,2,1,0,3:T(8,128)(2,1)}), bf16[1,3,128,8,1024]{4,2,1,0,3:T(8,128)(2,1)}, u32[]{:S(2)}, u32[]{:S(2)}) %all-to-all-start) | async-done | bytes 6291488 | tf_op jit(solution)/shard_map/all_to_all | solution.py:310
  140.2 0.8 slice_bitcast_fusion
  141.0 3.5 collective-permute-start
  144.5 0.7 dynamic-slice_bitcast_fusion.skip_ref
  145.2 0.2 broadcast_in_dim.18
  145.4 0.2 exp.13.decay_ref
  145.6 0.2 broadcast_in_dim.17
  145.9 0.2 reshape_reshape.7.taps_ref
  146.1 0.2 broadcast_in_dim.19
  146.3 0.2 exp.15
  146.5 0.2 broadcast_in_dim.20
  146.7 0.2 reshape_reshape.8.residue_ref
  146.9 0.3 collective-permute-done
  147.1 17.4 %smooth.1 = (f32[3,8192,128]{2,1,0:T(8,128)}, f32[8192,128]{1,0:T(8,128)S(1)}, f32[3,8192,128]{2,1,0:T(8,128)}, f32[16,8,128]{2,1,0:T(8,128)S(1)}) custom-call(bf16[8,3,128,1024]{3,2,1,0:T(8,128)(2,1)} %bitcast.3.x_ref, f32[3,8,1024]{2,1,0:T(8,128)S(1)} %convert_element_type.39.rim_ref, f32[3,7,8,128]{3,2,1,0:T(8,128)S(1)} %reshape_reshape.7.taps_ref, ...), custom_call_target="tpu_custom_call" | custom-call | flops 77594624 | bytes 35966976 | tf_op jit(solution)/shard_map/smooth/pallas_call | solution.py:271
  164.6 2.0 copy-done.2
  166.6 23.6 %all-gather = f32[64,8,128]{2,1,0:T(8,128)S(1)} all-gather(f32[16,8,128]{2,1,0:T(8,128)S(1)} %get-tuple-element.20), channel_id=2, replica_groups=mesh['hi'=4,'lo'=8,'tp'=1] {'hi'}, dimensions={0}, use_global_device_ids=true | all-gather | bytes 327680 | tf_op jit(solution)/shard_map/all_gather | solution.py:354
  190.2 8.8 %all-gather.6.cloned.1.call-done = bf16[4096,1024]{1,0:T(8,128)(2,1)} async-done(((bf16[1024,1024]{1,0:T(8,128)(2,1)}), bf16[4096,1024]{1,0:T(8,128)(2,1)}) %all-gather.6.cloned.1.call-update) | async-done | bytes 8388624 | tf_op jit(solution)/shard_map/all_gather | solution.py:307
  199.0 55.5 %all-gather.8.cloned.1.call-done = bf16[1024,4096]{1,0:T(8,128)(2,1)} async-done(((bf16[128,4096]{1,0:T(8,128)(2,1)}), bf16[1024,4096]{1,0:T(8,128)(2,1)}) %all-gather.8.cloned.1.call-update) | async-done | bytes 8388624 | tf_op jit(solution)/shard_map/all_gather | solution.py:309
  254.5 14.9 %fusion.40.up_ref = f32[1024,1024]{1,0:T(8,128)} fusion(bf16[1024,4096]{1,0:T(8,128)(2,1)} %all-gather.8.cloned.1.call-done, bf16[4096,1024]{1,0:T(8,128)(2,1)} %all-gather.6.cloned.1.call-done), kind=kOutput, calls=%fused_computation.93 | convolution fusion | flops 8589934592 | bytes 20971520 | tf_op jit(solution)/shard_map/dot_general | solution.py:381
  269.4 9.9 %cotangent.1 = (f32[8192,128]{1,0:T(8,128)S(1)}, f32[16,8,128]{2,1,0:T(8,128)S(1)}, f32[8,128]{1,0:T(8,128)S(1)}) custom-call(f32[1024,1024]{1,0:T(8,128)} %fusion.40.up_ref, f32[3,8192,128]{2,1,0:T(8,128)} %get-tuple-element.19.sm_ref, f32[8192,128]{1,0:T(8,128)} %copy-done.2, f32[16,8,128]{2,1,0:T(8,128)S(1)} %exp.13.decay_ref), custom_call_target="tpu_custom_call" | custom-call | flops 36700160 | bytes 25300992 | tf_op jit(solution)/shard_map/cotangent/pallas_call | solution.py:271
  279.3 2.0 copy-done.3
  281.3 14.1 %all-gather.1 = f32[64,8,128]{2,1,0:T(8,128)S(1)} all-gather(f32[16,8,128]{2,1,0:T(8,128)S(1)} %get-tuple-element.25), channel_id=3, replica_groups=mesh['hi'=4,'lo'=8,'tp'=1] {'hi'}, dimensions={0}, use_global_device_ids=true | all-gather | bytes 327680 | tf_op jit(solution)/shard_map/all_gather | solution.py:354
  295.4 0.1 fusion.31
  295.5 13.0 %field.1 = (f32[8192,128]{1,0:T(8,128)}, bf16[1024,1024]{1,0:T(8,128)(2,1)S(1)}) custom-call(f32[8192,128]{1,0:T(8,128)} %copy-done.2, f32[3,8192,128]{2,1,0:T(8,128)} %get-tuple-element.19.sm_ref, f32[16,8,128]{2,1,0:T(8,128)S(1)} %get-tuple-element.67.before_ref, f32[16,8,128]{2,1,0:T(8,128)S(1)} %exp.13.decay_ref, ...), custom_call_target="tpu_custom_call" | custom-call | flops 67108864 | bytes 23269376 | tf_op jit(solution)/shard_map/field/pallas_call | solution.py:271
  308.5 11.1 %convert_bitcast_fusion = bf16[4096,1024]{0,1:T(8,128)(2,1)} fusion(bf16[1024,1024]{1,0:T(8,128)(2,1)S(1)} %get-tuple-element.21, bf16[1024,4096]{1,0:T(8,128)(2,1)S(1)} %bitcast.114), kind=kOutput, calls=%fused_computation | convolution fusion | flops 8594128896 | bytes 18874368 | tf_op jit(solution)/shard_map/dot_general | solution.py:374
  319.6 0.2 all-reduce.4.cloned.1.call-start
  319.9 2.2 copy-done.4
  322.1 30.7 %back.1 = (bf16[8,3,128,1024]{3,2,1,0:T(8,128)(2,1)}, f32[3,7,8,128]{3,2,1,0:T(8,128)S(1)}, f32[3,64,128]{2,1,0:T(8,128)S(1)}, f32[3,64,128]{2,1,0:T(8,128)S(1)}) custom-call(f32[8192,128]{1,0:T(8,128)S(1)} %copy-done.4, f32[3,8192,128]{2,1,0:T(8,128)} %get-tuple-element.19.sm_ref, f32[8192,128]{1,0:T(8,128)} %get-tuple-element.23.field_ref, ...), custom_call_target="tpu_custom_call" | custom-call | flops 155189248 | bytes 40415232 | tf_op jit(solution)/shard_map/back/pallas_call | solution.py:271
  352.8 1.3 collective-permute-start.1
  354.1 10.5 %collective-permute-done.1 = f32[3,64,128]{2,1,0:T(8,128)S(1)} collective-permute-done((f32[3,64,128]{2,1,0:T(8,128)S(1)}, f32[3,64,128]{2,1,0:T(8,128)S(1)}, u32[]{:S(2)}, u32[]{:S(2)}) %collective-permute-start.1) | collective-permute-done | bytes 98336 | tf_op jit(solution)/shard_map/ppermute | solution.py:446
  364.6 1.0 fusion.28
  365.7 0.2 reshape.75
  365.9 0.3 reduce_sum.88
  366.2 0.1 maximum_dynamic-update-slice_fusion
  366.4 0.7 copy-done.5
  367.1 0.0 reduce-scatter.3.cloned.1.call-start
  367.2 14.3 %convolution_convert_fusion = bf16[1024,4096]{1,0:T(8,128)(2,1)} fusion(bf16[1024,1024]{1,0:T(8,128)(2,1)S(1)} %get-tuple-element.21, bf16[4096,1024]{1,0:T(8,128)(2,1)} %all-gather.6.cloned.1.call-done), kind=kOutput, calls=%fused_computation.1 | convolution fusion | flops 8594128896 | bytes 18874368 | tf_op jit(solution)/shard_map/dot_general | solution.py:382
  381.6 0.6 constant_dynamic-update-slice_fusion.7
  382.2 4.8 all-to-all-start.2
  387.0 79.8 %reduce-scatter.5.cloned.1.call-done = bf16[1024,1024]{0,1:T(8,128)(2,1)} async-done(((bf16[4096,1024]{0,1:T(8,128)(2,1)}), bf16[1024,1024]{0,1:T(8,128)(2,1)}) %reduce-scatter.5.cloned.1.call-update) | async-done | bytes 2097168 | tf_op jit(solution)/shard_map/reduce_scatter | solution.py:377
  466.9 2.2 copy.49
  469.1 1.7 copy.45
  470.7 3.7 all-to-all-start.3
  474.4 127.0 %all-reduce.4.cloned.1.call-done = f32[75776]{0:T(1024)} async-done(((f32[75776]{0:T(1024)}), f32[75776]{0:T(1024)}) %all-reduce.4.cloned.1.call-update) | async-done | bytes 303120
  601.4 1.1 reshape.76
  602.5 0.1 reshape.77
  602.6 0.7 reshape.78
  603.3 0.6 copy.51
  603.9 8.6 %copy.43 = bf16[8,3,128,1,1024]{2,4,0,1,3:T(8,128)(2,1)} copy(bf16[8,3,128,1,1024]{4,2,1,3,0:T(8,128)(2,1)} %all-to-all-done.2) | data formatting | bytes 12582912 | tf_op jit(solution)/shard_map/all_to_all | solution.py:460
  612.5 9.1 %copy.46 = bf16[3,128,8192]{2,1,0:T(8,128)(2,1)} copy(bf16[3,128,8192]{1,2,0:T(8,128)(2,1)} %bitcast.101) | data formatting | bytes 12582912
  621.6 2.2 bitcast_convert_fusion
  623.9 5.6 copy.47
  629.5 48.5 %reduce-scatter.3.cloned.1.call-done = bf16[128,4096]{1,0:T(8,128)(2,1)} async-done(((bf16[1024,4096]{1,0:T(8,128)(2,1)}), bf16[128,4096]{1,0:T(8,128)(2,1)}) %reduce-scatter.3.cloned.1.call-update) | async-done | bytes 1048592 | tf_op jit(solution)/shard_map/reduce_scatter | solution.py:385
  (36 shorter events, 0.3 us)
Async XLA Ops:
  7.2 61.5 %copy-start = (f32[3,7,512]{2,1,0:T(8,128)S(1)}, f32[3,7,512]{2,1,0:T(8,128)}, u32[]{:S(2)}) copy-start(f32[3,7,512]{2,1,0:T(8,128)} %param.8) | copy-start | bytes 129028
  7.2 191.8 %all-gather.6.cloned.1.call-start = ((), (), s32[]{:S(2)}) async-start(), calls=%async_computation.6 | async-start | bytes 10485760 | tf_op jit(solution)/shard_map/all_gather | solution.py:307
  45.7 208.8 %all-gather.8.cloned.1.call-start = ((), (), s32[]{:S(2)}) async-start(), calls=%async_computation.8 | async-start | bytes 9437184 | tf_op jit(solution)/shard_map/all_gather | solution.py:309
  63.8 76.4 %all-to-all-start = ((bf16[1,3,128,8,1024]{4,2,1,0,3:T(8,128)(2,1)}), bf16[1,3,128,8,1024]{4,2,1,0,3:T(8,128)(2,1)}, u32[]{:S(2)}, u32[]{:S(2)}) async-start(bf16[1,3,128,8,1024]{4,2,1,0,3:T(8,128)(2,1)} %copy.38), calls=%async_computation | async-start | bytes 12582912 | tf_op jit(solution)/shard_map/all_to_all | solution.py:310
  68.6 398.2 %reduce-scatter.5.cloned.1.call-start = ((), (), s32[]{:S(2)}) async-start(), calls=%async_computation.9 | async-start | bytes 10485760 | tf_op jit(solution)/shard_map/reduce_scatter | solution.py:377
  141.0 6.1 collective-permute-start
  164.6 2.0 copy-start.2
  279.3 2.0 copy-start.3
  281.3 27.2 %slice-start = ((s8[8388608]{0:T(1024)(128)(4,1)}), s8[4194304]{0:T(1024)(128)(4,1)S(1)}, s32[]{:S(2)}) async-start(s8[8388608]{0:T(1024)(128)(4,1)} %bitcast.113), calls=%async_computation.11 | async-start | bytes 8388608
  295.5 13.0 %slice-start.1 = ((s8[8388608]{0:T(1024)(128)(4,1)}), s8[4194304]{0:T(1024)(128)(4,1)S(1)}, s32[]{:S(2)}) async-start(s8[8388608]{0:T(1024)(128)(4,1)} %bitcast.113), calls=%async_computation.12 | async-start | bytes 8388608
  319.6 281.7 %all-reduce.4.cloned.1.call-start = ((), (), s32[]{:S(2)}) async-start(), calls=%async_computation.10 | async-start | bytes 606208
  319.9 2.2 copy-start.4
  352.8 11.8 %collective-permute-start.1 = (f32[3,64,128]{2,1,0:T(8,128)S(1)}, f32[3,64,128]{2,1,0:T(8,128)S(1)}, u32[]{:S(2)}, u32[]{:S(2)}) collective-permute-start(f32[3,64,128]{2,1,0:T(8,128)S(1)} %get-tuple-element.28), channel_id=1, source_target_pairs={{8,0},{16,8},{24,16},{9,1},{17,9},{25,17},{10,2},{18,10},{26,18},{... | collective-permute-start | bytes 294920 | tf_op jit(solution)/shard_map/ppermute | solution.py:446
  366.4 0.7 copy-start.5
  367.1 310.8 %reduce-scatter.3.cloned.1.call-start = ((), (), s32[]{:S(2)}) async-start(), calls=%async_computation.7 | async-start | bytes 9437184 | tf_op jit(solution)/shard_map/reduce_scatter | solution.py:385
  382.2 88.5 %all-to-all-start.2 = ((bf16[8,3,128,1,1024]{4,2,1,3,0:T(8,128)(2,1)}), bf16[8,3,128,1,1024]{4,2,1,3,0:T(8,128)(2,1)}, u32[]{:S(2)}, u32[]{:S(2)}) async-start(bf16[8,3,128,1,1024]{4,2,1,3,0:T(8,128)(2,1)} %bitcast.108), calls=%async_computation.3 | async-start | bytes 12582912 | tf_op jit(solution)/shard_map/all_to_all | solution.py:460
  470.7 150.9 %all-to-all-start.3 = ((bf16[8,128,1,1024]{1,3,2,0:T(8,128)(2,1)}), bf16[8,128,1,1024]{1,3,2,0:T(8,128)(2,1)S(1)}, u32[]{:S(2)}, u32[]{:S(2)}) async-start(bf16[8,128,1,1024]{1,3,2,0:T(8,128)(2,1)} %copy.45), calls=%async_computation.5 | async-start | bytes 4194304 | tf_op jit(solution)/shard_map/all_to_all | solution.py:378
  612.5 65.4 %copy-start.1 = (f32[3,7,512]{2,1,0:T(8,128)S(1)}, f32[3,7,512]{2,1,0:T(8,128)}, u32[]{:S(2)}) copy-start(f32[3,7,512]{2,1,0:T(8,128)} %param.8) | copy-start | bytes 129028
Sparse Core Ops, SparseCore 0:
  45.8 153.1 all-gather.5
  200.9 53.5 all-gather.7
  319.8 147.0 reduce-scatter.4
  472.1 129.2 all-reduce.3
  605.6 72.2 reduce-scatter.2

commit v2 on v1

v2 whole, which is shorter than its diff:
```python
import functools
import math

import jax
import jax.numpy as jnp
from jax import lax
from jax.experimental import pallas as pl
from jax.experimental.pallas import tpu as pltpu
from jax.sharding import Mesh, PartitionSpec as P

LANES = 128
EDGE = 8
STEP = 8
VMEM = 48 * 1024 * 1024


def at(token, rows):
    start = token * rows
    return pl.ds(start if isinstance(start, int) else pl.multiple_of(start, rows), rows)


def total_of(terms):
    while len(terms) > 1:
        terms = [
            terms[k] + terms[k + 1] if k + 1 < len(terms) else terms[k]
            for k in range(0, len(terms), 2)
        ]
    return terms[0]


def to_token_rows(ref, first, value, rows):
    count = value.shape[0]
    for j in range(rows):
        ref[pl.ds(first * rows + j, count, stride=rows), :] = value[
            :, j * LANES : (j + 1) * LANES
        ].astype(jnp.float32)


def fill(pad, parts, rims, rows, tok):
    first = pl.program_id(0) == 0

    @pl.when(first)
    def _():
        for i in range(pad.shape[0]):
            to_token_rows(pad.at[i], 0, rims[i], rows)

    @pl.when(jnp.logical_not(first))
    def _():
        for i in range(pad.shape[0]):
            pad[i, pl.ds(0, EDGE * rows), :] = pad[i, pl.ds(tok * rows, EDGE * rows), :]

    for i in range(pad.shape[0]):
        to_token_rows(pad.at[i], EDGE, parts[i], rows)


def rim_rows(rim_ref):
    rims = rim_ref[0].astype(jnp.float32)
    return [rims[i * EDGE : (i + 1) * EDGE] for i in range(3)]


def convolved(pad, i, taps, base, rows):
    lags = len(taps)
    window = [pad[i, at(base + EDGE - (lags - 1) + k, rows), :] for k in range(STEP + lags - 1)]
    return [
        total_of([taps[j] * window[u + lags - 1 - j] for j in range(lags)]) for u in range(STEP)
    ]


def smooth_kernel(
    rows,
    tok,
    x_ref,
    rim_ref,
    taps_ref,
    decay_ref,
    hold_ref,
    sm_ref,
    mixed_ref,
    xt_ref,
    end_ref,
    room_ref,
    pad,
    state,
):
    modes, lags = decay_ref.shape[0], taps_ref.shape[1]

    @pl.when(pl.program_id(0) == 0)
    def _():
        state[...] = jnp.zeros_like(state)

    parts = [x_ref[0, pl.ds(i * tok, tok), :] for i in range(2)]
    fill(pad, parts, rim_rows(rim_ref)[1:], rows, tok)
    for i in range(2):
        xt_ref[i] = pad[i, pl.ds(EDGE * rows, tok * rows), :]

    def smooth(n, carry):
        base = n * STEP
        results = []
        for i in range(2):
            taps = [taps_ref[i + 1, j] for j in range(lags)]
            results.append(convolved(pad, i, taps, base, rows))
            for u in range(STEP):
                sm_ref[i, at(base + u, rows), :] = results[i][u]
        for u in range(STEP):
            mixed_ref[at(base + u, rows), :] = (
                (results[0][u] * results[1][u]).astype(jnp.bfloat16).astype(jnp.float32)
            )
        return carry

    lax.fori_loop(0, tok // STEP, smooth, 0)
    decay = [decay_ref[m] for m in range(modes)]

    def advance(n, held):
        held = list(held)
        for u in range(STEP):
            x = mixed_ref[at(n * STEP + u, rows), :]
            held = [decay[m] * held[m] + x for m in range(modes)]
        return tuple(held)

    held = lax.fori_loop(0, tok // STEP, advance, tuple(state[m] for m in range(modes)))
    for m in range(modes):
        state[m] = held[m]
        end_ref[m] = held[m]


def field_kernel(
    rows,
    tok,
    x_ref,
    rim_ref,
    taps_ref,
    mixed_ref,
    before_ref,
    decay_ref,
    residue_ref,
    skip_ref,
    sm_ref,
    xt_ref,
    field_ref,
    gated_ref,
    pad,
    staged,
    state,
):
    modes, lags = decay_ref.shape[0], taps_ref.shape[1]

    @pl.when(pl.program_id(0) == 0)
    def _():
        state[...] = before_ref[...]

    fill(pad, [x_ref[0, 0]], rim_rows(rim_ref), rows, tok)
    xt_ref[...] = pad[0, pl.ds(EDGE * rows, tok * rows), :]
    taps = [taps_ref[0, j] for j in range(lags)]

    def smooth(n, carry):
        results = convolved(pad, 0, taps, n * STEP, rows)
        for u in range(STEP):
            sm_ref[at(n * STEP + u, rows), :] = results[u]
        return carry

    lax.fori_loop(0, tok // STEP, smooth, 0)
    decay = [decay_ref[m] for m in range(modes)]
    residue = [residue_ref[m] for m in range(modes)]
    skip = skip_ref[...]

    def advance(n, held):
        held = list(held)
        for u in range(STEP):
            place = at(n * STEP + u, rows)
            x = mixed_ref[place, :]
            held = [decay[m] * held[m] + x for m in range(modes)]
            field = total_of([residue[m] * held[m] for m in range(modes)] + [skip * x])
            field_ref[place, :] = field
            staged[place, :] = sm_ref[place, :] * field
        return tuple(held)

    held = lax.fori_loop(0, tok // STEP, advance, tuple(state[m] for m in range(modes)))
    for m in range(modes):
        state[m] = held[m]
    for j in range(rows):
        gated_ref[:, j * LANES : (j + 1) * LANES] = staged[
            pl.ds(j, tok, stride=rows), :
        ].astype(jnp.bfloat16)


def clear_or_shift(pad, rows, tok):
    first = pl.program_id(0) == 0

    @pl.when(first)
    def _():
        for i in range(pad.shape[0]):
            pad[i, pl.ds(tok * rows, EDGE * rows), :] = jnp.zeros((EDGE * rows, LANES), jnp.float32)

    @pl.when(jnp.logical_not(first))
    def _():
        for i in range(pad.shape[0]):
            pad[i, pl.ds(tok * rows, EDGE * rows), :] = pad[i, pl.ds(0, EDGE * rows), :]


def spread_back(
    rows, tok, i, pad, xt_at, taps, total, out_ref, gtaps_ref, staged
):
    lags = len(taps)

    def spread(n, sums):
        base = n * STEP
        sums = list(sums)
        window = [pad[i, at(base + k, rows), :] for k in range(STEP + lags - 1)]
        for u in range(STEP):
            x = xt_at(at(base + u, rows))
            for j in range(lags):
                sums[j] = sums[j] + x * window[u + j]
            staged[at(base + u, rows), :] = total_of(
                [taps[j] * window[u + j] for j in range(lags)]
            )
        return tuple(sums)

    sums = lax.fori_loop(0, tok // STEP, spread, tuple(total[i, j] for j in range(lags)))
    for j in range(lags):
        total[i, j] = sums[j]
        gtaps_ref[i, j] = sums[j]
    for j in range(rows):
        out_ref[0, i, :, j * LANES : (j + 1) * LANES] = staged[
            pl.ds(j, tok, stride=rows), :
        ].astype(jnp.bfloat16)


def cotangent_kernel(
    rows,
    tok,
    up_ref,
    gated_ref,
    sm_ref,
    mixed_ref,
    field_ref,
    xt_ref,
    taps_ref,
    decay_ref,
    grad_ref,
    mid_ref,
    end_ref,
    gskip_ref,
    out_ref,
    gtaps_ref,
    head_ref,
    tail_ref,
    kept_ref,
    pad,
    staged,
    state,
    summed,
    total,
):
    modes, lags = decay_ref.shape[0], taps_ref.shape[1]

    @pl.when(pl.program_id(0) == 0)
    def _():
        state[...] = jnp.zeros_like(state)
        summed[...] = jnp.zeros_like(summed)
        total[...] = jnp.zeros_like(total)

    kept_ref[...] = gated_ref[...]
    clear_or_shift(pad, rows, tok)
    to_token_rows(staged, 0, up_ref[...], rows)
    decay = [decay_ref[m] for m in range(modes)]

    def retreat(n, carry):
        held, added = list(carry[:-1]), carry[-1]
        for u in range(STEP):
            place = at(tok - 1 - (n * STEP + u), rows)
            up = staged[place, :]
            grad = up * sm_ref[place, :]
            grad_ref[place, :] = grad
            pad[0, place, :] = up * field_ref[place, :]
            added = added + grad * mixed_ref[place, :]
            held = [decay[m] * held[m] + grad for m in range(modes)]
        return tuple(held) + (added,)

    last = tok // STEP - 1
    carry = lax.fori_loop(
        0, last, retreat, tuple(state[m] for m in range(modes)) + (summed[...],)
    )
    for m in range(modes):
        mid_ref[m] = carry[m]
    carry = retreat(last, carry)
    for m in range(modes):
        state[m] = carry[m]
        end_ref[m] = carry[m]
    summed[...] = carry[-1]
    gskip_ref[...] = carry[-1]
    spread_back(
        rows,
        tok,
        0,
        pad,
        lambda place: xt_ref[place, :],
        [taps_ref[0, j] for j in range(lags)],
        total,
        out_ref,
        gtaps_ref,
        staged,
    )

    @pl.when(pl.program_id(0) == 0)
    def _():
        tail_ref[...] = pad[0, pl.ds((tok - EDGE) * rows, EDGE * rows), :]

    head_ref[...] = pad[0, pl.ds(0, EDGE * rows), :]


def back_kernel(
    rows,
    tok,
    grad_ref,
    sm_ref,
    xt_ref,
    after_ref,
    ahead_ref,
    decay_ref,
    residue_ref,
    skip_ref,
    taps_ref,
    out_ref,
    gtaps_ref,
    pad,
    staged,
    state,
    total,
):
    modes, lags = decay_ref.shape[0], taps_ref.shape[1]
    decay = [decay_ref[m] for m in range(modes)]
    residue = [residue_ref[m] for m in range(modes)]
    skip = skip_ref[...]

    @pl.when(pl.program_id(0) == 0)
    def _():
        total[...] = jnp.zeros_like(total)
        held = [after_ref[m] for m in range(modes)]
        for u in reversed(range(EDGE)):
            grad, one, two = [ahead_ref[at(k * EDGE + u, rows), :] for k in range(3)]
            held = [decay[m] * held[m] + grad for m in range(modes)]
            mixed = total_of([residue[m] * held[m] for m in range(modes)] + [skip * grad])
            pad[0, at(tok + u, rows), :] = mixed * two
            pad[1, at(tok + u, rows), :] = mixed * one
        for m in range(modes):
            state[m] = held[m]

    @pl.when(pl.program_id(0) != 0)
    def _():
        for i in range(2):
            pad[i, pl.ds(tok * rows, EDGE * rows), :] = pad[i, pl.ds(0, EDGE * rows), :]


    def retreat(n, held):
        held = list(held)
        for u in range(STEP):
            place = at(tok - 1 - (n * STEP + u), rows)
            grad = grad_ref[place, :]
            held = [decay[m] * held[m] + grad for m in range(modes)]
            mixed = total_of([residue[m] * held[m] for m in range(modes)] + [skip * grad])
            pad[0, place, :] = mixed * sm_ref[1, place, :]
            pad[1, place, :] = mixed * sm_ref[0, place, :]
        return tuple(held)

    held = lax.fori_loop(0, tok // STEP, retreat, tuple(state[m] for m in range(modes)))
    for m in range(modes):
        state[m] = held[m]
    for i in range(2):
        spread_back(
            rows,
            tok,
            i,
            pad,
            lambda place, i=i: xt_ref[i, place, :],
            [taps_ref[i + 1, j] for j in range(lags)],
            total,
            out_ref,
            gtaps_ref,
            staged,
        )


def whole(shape):
    return pl.BlockSpec(shape, lambda n: (0,) * len(shape))


def call(kernel, name, blocks, ins, in_specs, outs, out_specs, scratch, ops, aliases={}):
    return pl.pallas_call(
        kernel,
        grid=(blocks,),
        in_specs=in_specs,
        out_specs=out_specs,
        out_shape=outs,
        scratch_shapes=scratch,
        input_output_aliases=aliases,
        compiler_params=pltpu.CompilerParams(vmem_limit_bytes=VMEM),
        cost_estimate=pl.CostEstimate(flops=ops, bytes_accessed=0, transcendentals=0),
        name=name,
    )(*ins)


def tie_kernel(*refs):
    pass


def tie(values, after):
    values, after = tuple(values), tuple(after)
    held = pl.BlockSpec(memory_space=pl.ANY)
    return pl.pallas_call(
        tie_kernel,
        in_specs=[held] * (len(values) + len(after)),
        out_specs=[held] * len(values),
        out_shape=[jax.ShapeDtypeStruct(a.shape, a.dtype) for a in values],
        input_output_aliases={i: i for i in range(len(values))},
        compiler_params=pltpu.CompilerParams(vmem_limit_bytes=VMEM),
        name="tie",
    )(*values, *after)


def split_kernel(in_ref, out_ref):
    out_ref[0] = in_ref[...].astype(out_ref.dtype)


def split_channels(a, lo, first, count):
    tok, wide = a.shape[1], a.shape[2] // lo
    return call(
        split_kernel,
        "split",
        lo * count,
        (a,),
        [pl.BlockSpec((1, tok, wide), lambda n: (first + n // lo, 0, n % lo))],
        jax.ShapeDtypeStruct((lo, count, tok, wide), a.dtype),
        pl.BlockSpec((1, 1, tok, wide), lambda n: (n % lo, n // lo, 0, 0)),
        [],
        0,
    )


def pack_kernel(tok, x_ref, rim_ref, out_ref, first_ref):
    first_ref[0, 0] = x_ref[0]
    out_ref[0, pl.ds(0, tok), :] = x_ref[1]
    out_ref[0, pl.ds(tok, tok), :] = x_ref[2]
    rims = [rim_ref[i].astype(jnp.float32) for i in range(3)]
    rims.append(jnp.zeros_like(rims[0]))
    out_ref[0, pl.ds(2 * tok, 4 * EDGE), :] = jnp.concatenate(rims).astype(out_ref.dtype)


def pack(streams, rim, lo):
    tok, wide = streams.shape[1], streams.shape[2] // lo
    held = 2 * tok + 4 * EDGE
    return call(
        functools.partial(pack_kernel, tok),
        "pack",
        lo,
        (streams, rim),
        [
            pl.BlockSpec((3, tok, wide), lambda n: (0, 0, n)),
            pl.BlockSpec((3, EDGE, wide), lambda n: (0, 0, n)),
        ],
        [
            jax.ShapeDtypeStruct((lo, held, wide), streams.dtype),
            jax.ShapeDtypeStruct((lo, 1, tok, wide), streams.dtype),
        ],
        [
            pl.BlockSpec((1, held, wide), lambda n: (n, 0, 0)),
            pl.BlockSpec((1, 1, tok, wide), lambda n: (n, 0, 0, 0)),
        ],
        [],
        0,
    )


def join_kernel(*refs):
    out_ref, first = refs[-1], 0
    for ref in refs[:-1]:
        out_ref[pl.ds(first, ref.shape[1])] = ref[0].astype(out_ref.dtype)
        first += ref.shape[1]


def join_channels(pieces, dtype, tok):
    lo, _, _, wide = pieces[0].shape
    total = sum(piece.shape[1] for piece in pieces)
    return call(
        join_kernel,
        "join",
        lo,
        pieces,
        [
            pl.BlockSpec((1, piece.shape[1], tok, wide), lambda n: (n, 0, 0, 0))
            for piece in pieces
        ],
        jax.ShapeDtypeStruct((total, tok, lo * wide), dtype),
        pl.BlockSpec((total, tok, wide), lambda n: (0, 0, n)),
        [],
        0,
    )


class Planes:
    def __init__(self, block, hi, plane):
        self.block, self.hi, self.plane = block, hi, plane
        self.rows, self.done, self.placed = block.shape[0], 0, 0
        self.right, self.left = block, block
        self.arrived = []
        self.result = None

    def step(self):
        self.done += 1
        k, hi = self.done, self.hi
        self.right = lax.ppermute(self.right, "hi", [(z, z + 1) for z in range(k - 1, hi - 1)])
        self.left = lax.ppermute(self.left, "hi", [(z + 1, z) for z in range(hi - k)])
        self.arrived.append((self.right, self.left))

    def put(self, piece, there):
        valid = jnp.logical_and(there >= 0, there < self.hi)
        self.result = lax.dynamic_update_slice_in_dim(
            self.result,
            jnp.where(valid, piece, self.block),
            jnp.where(valid, there, self.plane) * self.rows,
            0,
        )

    def place(self):
        if not self.placed:
            self.put(self.block, self.plane)
        if self.done:
            self.arrived[-1] = (self.right, self.left)
        while self.placed < self.done:
            self.placed += 1
            k, (right, left) = self.placed, self.arrived[self.placed - 1]
            if 2 * k < self.hi:
                self.put(right, self.plane - k)
                self.put(left, self.plane + k)
            else:
                below = self.plane >= k
                self.put(
                    jnp.where(below, right, left),
                    jnp.where(below, self.plane - k, self.plane + k),
                )


class Sums:
    def __init__(self, partial, hi, plane):
        self.partial, self.hi, self.plane = partial, hi, plane
        self.rows, self.done = partial.shape[0] // hi, 0
        self.right, self.left = None, None

    def part(self, d):
        first = jnp.clip(d, 0, self.hi - 1) * self.rows
        return lax.dynamic_slice_in_dim(self.partial, first, self.rows, 0).astype(jnp.float32)

    def step(self):
        self.done += 1
        s, hi, dtype = self.done, self.hi, self.partial.dtype
        self.to_right = add(self.part(hi - s + self.plane), self.right).astype(dtype)
        self.to_left = add(self.part(s - hi + self.plane), self.left).astype(dtype)
        self.right = lax.ppermute(self.to_right, "hi", [(z, z + 1) for z in range(s)])
        self.left = lax.ppermute(
            self.to_left, "hi", [(hi - 1 - z, hi - 2 - z) for z in range(s)]
        )

    def finish(self):
        return add(add(self.part(self.plane), self.right), self.left)


def add(mine, arrived):
    return mine if arrived is None else mine + arrived.astype(jnp.float32)


def shards(streams, short_filter, residues, rates, skip, out_weight, out_cotangent):
    hi, lo = lax.axis_size("hi"), lax.axis_size("lo")
    plane, place = lax.axis_index("hi"), lax.axis_index("lo")
    tok, channels = streams.shape[1:]
    modes, groups = residues.shape
    members = channels // groups
    lags = short_filter.shape[1]
    wide, near = channels // lo, groups // lo
    rows = wide // LANES
    length = tok * lo
    f32 = jnp.float32
    shape = jax.ShapeDtypeStruct

    def mine(a):
        a = lax.dynamic_slice_in_dim(a, place * near, near, a.ndim - 1)
        return jnp.repeat(a, members, axis=-1).reshape(a.shape[:-1] + (rows, LANES))

    taps, residue, rate = mine(short_filter), mine(residues), mine(rates)
    decay = jnp.exp(-rate)
    plane_decay = jnp.exp(-rate * length)
    direct = lax.dynamic_slice_in_dim(skip, place * wide, wide, 0).reshape(rows, LANES)

    ends = [(z * lo - 1, z * lo) for z in range(1, hi)]
    rim = lax.ppermute(streams[:, tok - EDGE :, :], ("hi", "lo"), ends)
    own = lax.all_to_all(split_channels(out_weight[None], lo, 0, 1), "lo", 0, 0, tiled=True)
    own = own.reshape(-1, wide)
    packed12, packed0 = tie(pack(streams, rim, lo), (own,))
    x12 = lax.all_to_all(packed12, "lo", 0, 0, tiled=True)
    (packed0,) = tie((packed0,), (x12,))
    x0 = lax.all_to_all(packed0, "lo", 0, 0, tiled=True)
    (cotangent,) = tie((out_cotangent,), (x12,))
    cotangent = lax.all_gather(cotangent, "tp", axis=1, tiled=True)
    cotangent = lax.all_gather(cotangent, "lo", axis=0, tiled=True)

    flat = tok * rows
    tokens = length * rows
    up_one = pl.BlockSpec((flat, LANES), lambda n: (n, 0))
    up_two = pl.BlockSpec((2, flat, LANES), lambda n: (0, n, 0))
    up_wide = pl.BlockSpec((tok, wide), lambda n: (n, 0))
    down_one = pl.BlockSpec((flat, LANES), lambda n: (lo - 1 - n, 0))
    down_two = pl.BlockSpec((2, flat, LANES), lambda n: (0, lo - 1 - n, 0))
    down_wide = pl.BlockSpec((tok, wide), lambda n: (lo - 1 - n, 0))
    taps_spec = whole((3, lags, rows, LANES))
    mode_spec = whole((modes, rows, LANES))
    skip_spec = whole((rows, LANES))
    held_spec = pl.BlockSpec(memory_space=pl.ANY)
    states = pltpu.VMEM((modes, rows, LANES), f32)
    staged = pltpu.VMEM((flat, LANES), f32)
    work = length * wide

    def padded(count):
        return pltpu.VMEM((count, (tok + EDGE) * rows, LANES), f32)

    rim_spec = pl.BlockSpec((1, 4 * EDGE, wide), lambda n: (0, 2 * tok // (4 * EDGE), 0))

    def grads_spec(count):
        return pl.BlockSpec((1, count, tok, wide), lambda n: (lo - 1 - n, 0, 0, 0))

    mover = Planes(own, hi, plane)
    mover.step()

    sm12, mixed, xt12, ending, mover.result = call(
        functools.partial(smooth_kernel, rows, tok),
        "smooth",
        lo,
        (x12, x12, taps, decay, mover.right),
        [
            pl.BlockSpec((1, 2 * tok, wide), lambda n: (n, 0, 0)),
            rim_spec,
            taps_spec,
            mode_spec,
            held_spec,
        ],
        [
            shape((2, tokens, LANES), f32),
            shape((tokens, LANES), f32),
            shape((2, tokens, LANES), f32),
            shape((modes, rows, LANES), f32),
            shape((hi * own.shape[0], wide), own.dtype),
        ],
        [up_two, up_one, up_two, mode_spec, held_spec],
        [padded(2), states],
        0,
    )
    mover.step()

    def from_plane(a, distance):
        pairs = [(z + distance, z) for z in range(max(0, -distance), hi - max(0, distance))]
        return lax.ppermute(a, "hi", pairs)

    before = jnp.zeros_like(ending)
    for k in reversed(range(1, hi)):
        before = from_plane(ending, -k) + plane_decay * before
    mover.right, mover.left = tie((mover.right, mover.left), (before,))
    sm0, xt0, field, gated = call(
        functools.partial(field_kernel, rows, tok),
        "field",
        lo,
        (x0, x12, taps, mixed, before, decay, residue, direct),
        [
            pl.BlockSpec((1, 1, tok, wide), lambda n: (n, 0, 0, 0)),
            rim_spec,
            taps_spec,
            up_one,
            mode_spec,
            mode_spec,
            mode_spec,
            skip_spec,
        ],
        [
            shape((tokens, LANES), f32),
            shape((tokens, LANES), f32),
            shape((tokens, LANES), f32),
            shape((length, wide), jnp.bfloat16),
        ],
        [up_one, up_one, up_one, up_wide],
        [padded(1), staged, states],
        0,
    )
    mover.place()
    while mover.done < hi - 1:
        mover.step()

    partial_grad = lax.dot_general(
        cotangent, gated, (((0,), (0,)), ((), ())), preferred_element_type=f32
    ).astype(jnp.bfloat16)
    sums = Sums(partial_grad, hi, plane)
    sums.step()
    mover.right, mover.left = tie((mover.right, mover.left), (sums.to_right, sums.to_left))
    mover.place()
    weights = mover.result

    upstream = jnp.dot(cotangent, weights, preferred_element_type=f32)
    grad_field, back_mid, back_end, grad_skip, grads0, grad_taps0, head, tail, kept = call(
        functools.partial(cotangent_kernel, rows, tok),
        "cotangent",
        lo,
        (upstream, gated, sm0, mixed, field, xt0, taps, decay),
        [
            down_wide,
            down_wide,
            down_one,
            down_one,
            down_one,
            down_one,
            taps_spec,
            mode_spec,
        ],
        [
            shape((tokens, LANES), f32),
            shape((modes, rows, LANES), f32),
            shape((modes, rows, LANES), f32),
            shape((rows, LANES), f32),
            shape((lo, 1, tok, wide), jnp.bfloat16),
            shape((1, lags, rows, LANES), f32),
            shape((EDGE * rows, LANES), f32),
            shape((EDGE * rows, LANES), f32),
            shape(gated.shape, gated.dtype),
        ],
        [
            down_one,
            mode_spec,
            mode_spec,
            skip_spec,
            grads_spec(1),
            whole((1, lags, rows, LANES)),
            whole((EDGE * rows, LANES)),
            whole((EDGE * rows, LANES)),
            down_wide,
        ],
        [
            padded(1),
            staged,
            states,
            pltpu.VMEM((rows, LANES), f32),
            pltpu.VMEM((1, lags, rows, LANES), f32),
        ],
        0,
    )

    back_mid, back_end = tie((back_mid, back_end), (sums.right, sums.left))
    edge = EDGE * rows
    heads = [
        back_mid.reshape(-1, LANES),
        grad_field[:edge],
        sm12[0, :edge],
        sm12[1, :edge],
        head,
    ]
    ahead = from_plane(jnp.concatenate(heads), 1)
    beyond = jnp.zeros_like(back_end)
    for k in reversed(range(2, hi)):
        beyond = from_plane(back_end, k) + plane_decay * beyond
    after = ahead[: modes * rows].reshape(back_end.shape) + beyond * jnp.exp(
        -rate * (length - EDGE)
    )
    ahead = ahead[modes * rows :]

    edges = (EDGE, rows, LANES)
    beyond, tail = ahead[3 * edge :].reshape(edges), tail.reshape(edges)
    last = xt0[-edge:].reshape(edges)
    joined = jnp.concatenate([tail, beyond])
    extra = jnp.concatenate([jnp.zeros_like(tail), beyond])
    fixed = sum(taps[0, j] * joined[j : j + EDGE] for j in range(lags))
    grads0 = lax.dynamic_update_slice(
        grads0,
        fixed.reshape(1, 1, EDGE, wide).astype(grads0.dtype),
        (lo - 1, 0, tok - EDGE, 0),
    )
    grad_taps0 = grad_taps0[0] + jnp.stack(
        [jnp.sum(last * extra[j : j + EDGE], axis=0) for j in range(lags)]
    )
    grads0 = lax.all_to_all(grads0, "lo", 0, 0, tiled=True)

    sums.right, sums.left = tie((sums.right, sums.left), (after, ahead))
    sums.step()
    (kept,) = tie((kept,), (sums.to_right, sums.to_left))
    partial_out = lax.dot_general(
        kept, weights, (((1,), (1,)), ((), ())), preferred_element_type=f32
    ).astype(jnp.bfloat16)
    output = lax.psum_scatter(partial_out, "lo", scatter_dimension=0, tiled=True)
    output = lax.psum_scatter(output, "tp", scatter_dimension=1, tiled=True)

    grads12, grad_taps12 = call(
        functools.partial(back_kernel, rows, tok),
        "back",
        lo,
        (grad_field, sm12, xt12, after, ahead, decay, residue, direct, taps),
        [
            down_one,
            down_two,
            down_two,
            mode_spec,
            whole((4 * edge, LANES)),
            mode_spec,
            mode_spec,
            skip_spec,
            taps_spec,
        ],
        [
            shape((lo, 2, tok, wide), jnp.bfloat16),
            shape((2, lags, rows, LANES), f32),
        ],
        [grads_spec(2), whole((2, lags, rows, LANES))],
        [padded(2), staged, states, pltpu.VMEM((2, lags, rows, LANES), f32)],
        0,
    )
    grads12 = lax.all_to_all(grads12, "lo", 0, 0, tiled=True)
    grad_taps = jnp.concatenate([grad_taps0[None], grad_taps12])
    grad_taps = jnp.sum(grad_taps.reshape(3 * lags * near, members), axis=1)
    part = jnp.concatenate([grad_skip.reshape(-1), grad_taps])
    part = jnp.pad(part, (0, -part.size % wide)).reshape(-1, wide)
    part = jnp.pad(part, ((0, -part.shape[0] % EDGE), (0, 0)))
    small = part
    for k in range(1, hi):
        small = small + lax.ppermute(part, "hi", [(z, (z + k) % hi) for z in range(hi)])
    sums.right, sums.left = tie((sums.right, sums.left), (small,))
    while sums.done < hi - 1:
        sums.step()

    reduced = sums.finish().astype(jnp.bfloat16).reshape(lo, -1, wide)
    count = reduced.shape[1]
    coarse = small.astype(jnp.bfloat16)
    fine = (small - coarse.astype(f32)).astype(jnp.bfloat16)
    extra = jnp.concatenate([coarse, fine])
    extra = jnp.broadcast_to(extra, (lo,) + extra.shape)
    reduced = jnp.concatenate([reduced, extra], axis=1)[:, None]
    reduced = lax.all_to_all(reduced, "lo", 0, 0, tiled=True)
    grad_weight = join_channels((reduced,), f32, count)[0]
    grad_streams = join_channels((grads0, grads12), grads0.dtype, tok)
    small = reduced[:, 0, count:].astype(f32)
    small = (small[:, : part.shape[0]] + small[:, part.shape[0] :]).reshape(lo, -1)
    grad_skip = small[:, :wide].reshape(channels)
    grad_short = small[:, wide : wide + 3 * lags * near].reshape(lo, 3, lags, near)
    grad_short = jnp.moveaxis(grad_short, 0, 2)
    return output, grad_streams, grad_short.reshape(3, lags, groups), grad_skip, grad_weight


def solution(mesh):
    count, parts = mesh.shape["ctx"], mesh.shape["tp"]
    lo = math.gcd(count, 8)
    cut = Mesh(mesh.devices.reshape(count // lo, lo, parts), ("hi", "lo", "tp"))
    ctx = ("hi", "lo")
    return jax.shard_map(
        shards,
        mesh=cut,
        in_specs=(
            P(None, ctx, "tp"),
            P(None, None, "tp"),
            P(None, "tp"),
            P(None, "tp"),
            P("tp"),
            P(ctx, "tp"),
            P(ctx, "tp"),
        ),
        out_specs=(
            P(ctx, "tp"),
            P(None, ctx, "tp"),
            P(None, None, "tp"),
            P("tp"),
            P(ctx, "tp"),
        ),
        check_vma=False,
    )
```

time: 686 us -> 517 us (0.75)
  waiting for transfers between devices: 402 us -> 160 us
  starting transfers between devices: 18.4 us -> 74.3 us
  other arithmetic: 4.53 us -> 36.7 us
  local copies, waits for them, and re-layouts: 64.8 us -> 37 us
  Pallas kernels: 71 us -> 91.6 us
  blocking collectives: 69.5 us -> 58.3 us
    unnamed x6 -> x2, waiting for transfers between devices: 128 us -> 0.03 us
    ppermute x2 -> x22, waiting for transfers between devices: 10.8 us -> 121 us  [the longest x3 41.7 us: step(): lax.ppermute(self.to_left, 'hi', [(hi - 1 - z, hi - 2 - z) for z in range...]
    reduce_scatter x1 -> x0, waiting for transfers between devices: 79.8 us -> none  [shards(): lax.psum_scatter(partial_grad, 'hi', scatter_dimension=0, tiled=True)]
    all_gather x1, waiting for transfers between devices: 55.5 us -> 0.01 us  [shards(): cotangent = lax.all_gather(cotangent, 'lo', axis=0, tiled=True)]
    reduce_scatter x1, waiting for transfers between devices: 48.5 us -> 0.01 us  [shards(): lax.psum_scatter(partial_out, 'lo', scatter_dimension=0, tiled=True)]
    ppermute x2 -> x22, starting transfers between devices: 4.79 us -> 51.9 us  [the longest x6 14.2 us: from_plane(): return lax.ppermute(a, 'hi', pairs)]
    all_gather x2 -> x0, blocking collectives: 37.7 us -> none  [entering(): gathered = lax.all_gather(end, 'hi')]
    all_to_all x3 -> x5, waiting for transfers between devices: 70.7 us -> 39.5 us  [the longest x1 21.7 us: shards(): reduced = lax.all_to_all(reduced, 'lo', 0, 0, tiled=True)]
  transfers between devices with their start and end apart: 10 -> 29, of which waited for: 8 -> 14; matrix products, arithmetic and copies ran while one was open for 10% -> 13% of each run, Pallas kernels for 7% -> 18%
where the time goes in v2:
time: 517 us; the launch traced here: 515 us
  waiting for transfers between devices  160 us (31%)
  Pallas kernels  91.6 us (18%)
  starting transfers between devices  74.3 us (14%)
  blocking collectives  58.3 us (11%)
  matrix products  42.2 us (8%)
  local copies, waits for them, and re-layouts  37 us (7%)
  other arithmetic  36.7 us (7%)
  between operations  14.8 us (3%)
    pallas_call x8, Pallas kernels, call(): pl.pallas_call(kernel, grid=(blocks,), in_specs=in_specs, out_specs=out_s...  91.6 us
    all_to_all x1, blocking collectives, shards(): x12 = lax.all_to_all(packed12, 'lo', 0, 0, tiled=True)  58.3 us
    ppermute x3, waiting for transfers between devices, step(): lax.ppermute(self.to_left, 'hi', [(hi - 1 - z, hi - 2 - z) for z in range...  41.7 us
    ppermute x3, waiting for transfers between devices, step(): lax.ppermute(self.right, 'hi', [(z, z + 1) for z in range(k - 1, hi - 1)])  41.6 us
    unnamed x55, local copies, waits for them, and re-layouts  29.5 us
    all_to_all x1, waiting for transfers between devices, shards(): reduced = lax.all_to_all(reduced, 'lo', 0, 0, tiled=True)  21.7 us
    all_to_all x1, waiting for transfers between devices, shards(): lax.all_to_all(split_channels(out_weight[None], lo, 0, 1), 'lo', 0, 0, ti...  16.2 us
    dynamic_update_slice x4, other arithmetic, put(): lax.dynamic_update_slice_in_dim(self.result, jnp.where(valid, piece, self...  15.1 us
  transfers between devices with their start and end apart: 29, of which 14 were waited for; matrix products, arithmetic and copies ran while one was open for 13% of the time, Pallas kernels for 18%

profile of v2, /device:TPU:0, one launch (start us, length us, event | category | flops | bytes accessed | tf_op | source)
XLA Modules:
  0.0 515.2 jit_solution(15993582875073782608)
XLA Ops:
  7.2 2.4 copy.80.refs_0_
  10.3 1.3 copy-done.13
  11.6 5.2 %all-to-all-start = ((bf16[8,1,128,1024]{3,2,1,0:T(8,128)(2,1)}), bf16[8,1,128,1024]{3,2,1,0:T(8,128)(2,1)S(1)}, u32[]{:S(2)}, u32[]{:S(2)}) async-start(bf16[8,1,128,1024]{3,2,1,0:T(8,128)(2,1)} %copy-done.13), calls=%async_computation | async-start | bytes 4194304 | tf_op jit(solution)/shard_map/all_to_all | solution.py:594
  18.5 7.4 %pack.1 = (bf16[8,288,1024]{2,1,0:T(8,128)(2,1)}, bf16[8,1,128,1024]{3,2,1,0:T(8,128)(2,1)S(1)}) custom-call(bf16[3,128,8192]{2,1,0:T(8,128)(2,1)} %x_ref.1, bf16[3,8,8192]{2,1,0:T(8,128)(2,1)S(1)} %collective-permute-done.rim_ref), custom_call_target="tpu_custom_call" | custom-call | tf_op jit(solution)/shard_map/pack/pallas_call | solution.py:388
  27.2 16.2 %all-to-all-done = bf16[8,1,128,1024]{3,2,1,0:T(8,128)(2,1)S(1)} async-done(((bf16[8,1,128,1024]{3,2,1,0:T(8,128)(2,1)}), bf16[8,1,128,1024]{3,2,1,0:T(8,128)(2,1)S(1)}, u32[]{:S(2)}, u32[]{:S(2)}) %all-to-all-start) | async-done | bytes 2097184 | tf_op jit(solution)/shard_map/all_to_all | solution.py:594
  43.4 1.6 copy-done.4
  46.3 58.3 %all_to_all.30.refs_1_.x_ref.rim_ref = bf16[8,288,1024]{2,1,0:T(8,128)(2,1)S(1)} all-to-all(bf16[8,288,1024]{2,1,0:T(8,128)(2,1)} %get-tuple-element.41), channel_id=1, replica_groups=mesh['hi'=4,'lo'=8,'tp'=1] {'lo'}, dimensions={0} | all-to-all | bytes 9437184 | tf_op jit(solution)/shard_map/all_to_all | solution.py:597
  104.6 2.2 copy-done.2
  106.8 9.0 %collective-permute-start.1 = (bf16[1024,1024]{1,0:T(8,128)(2,1)S(1)}, bf16[1024,1024]{1,0:T(8,128)(2,1)}, u32[]{:S(2)}, u32[]{:S(2)}) collective-permute-start(bf16[1024,1024]{1,0:T(8,128)(2,1)S(1)} %bitcast.89), channel_id=1, source_target_pairs={{0,8},{8,16},{16,24},{1,9},{9,17},{17,25},{2,10},{10,18},{18,26},{... | collective-permute-start | bytes 6291464 | tf_op jit(solution)/shard_map/ppermute | solution.py:510
  117.1 41.6 %collective-permute-done.1.hold_ref = bf16[1024,1024]{1,0:T(8,128)(2,1)} collective-permute-done((bf16[1024,1024]{1,0:T(8,128)(2,1)S(1)}, bf16[1024,1024]{1,0:T(8,128)(2,1)}, u32[]{:S(2)}, u32[]{:S(2)}) %collective-permute-start.1) | collective-permute-done | bytes 2097184 | tf_op jit(solution)/shard_map/ppermute | solution.py:510
  158.8 2.0 collective-permute-start.3
  160.7 3.5 collective-permute-done.2
  166.2 1.6 copy-done.6
  167.8 1.4 copy-done.7
  169.2 4.4 all-to-all-start.2
  176.3 15.0 %smooth.1 = (f32[2,8192,128]{2,1,0:T(8,128)}, f32[8192,128]{1,0:T(8,128)}, f32[2,8192,128]{2,1,0:T(8,128)}, f32[16,8,128]{2,1,0:T(8,128)S(1)}, bf16[4096,1024]{1,0:T(8,128)(2,1)}) custom-call(bf16[8,288,1024]{2,1,0:T(8,128)(2,1)} %copy-done.2, bf16[8,288,1024]{2,1,0:T(8,128)(2,1)} %copy-done.2, f32[3,7,8,128]{3,2,1,0:T(8,128)S(1)} %reshape_reshape.7.taps_ref, ...), custom_call_target="tpu_custom_call" | custom-call | tf_op jit(solution)/shard_map/smooth/pallas_call | solution.py:388
  191.3 4.5 collective-permute-start.5
  195.9 4.5 collective-permute-start.6
  201.7 1.5 constant_dynamic-update-slice_fusion.8
  203.2 2.3 select_dynamic-update-slice_fusion.3
  205.5 3.9 select_dynamic-update-slice_fusion.2
  209.5 2.7 collective-permute-done.4.refs_1_
  212.1 2.0 collective-permute-start.8
  214.2 1.5 collective-permute-start.9
  215.6 4.4 select_dynamic-update-slice_fusion.1
  220.0 16.9 %field.1 = (f32[8192,128]{1,0:T(8,128)}, f32[8192,128]{1,0:T(8,128)}, f32[8192,128]{1,0:T(8,128)}, bf16[1024,1024]{1,0:T(8,128)(2,1)S(1)}) custom-call(bf16[8,1,128,1024]{3,2,1,0:T(8,128)(2,1)} %all-to-all-done.2.x_ref, bf16[8,288,1024]{2,1,0:T(8,128)(2,1)} %copy-done.2, f32[3,7,8,128]{3,2,1,0:T(8,128)S(1)} %reshape_reshape.7.taps_ref, ...), custom_call_target="tpu_custom_call" | custom-call | tf_op jit(solution)/shard_map/field/pallas_call | solution.py:388
  236.9 1.4 copy-done.16
  238.3 12.9 %convolution_convert_fusion.1 = bf16[4096,1024]{1,0:T(8,128)(2,1)S(1)} fusion(bf16[1024,4096]{1,0:T(8,128)(2,1)} %all-gather.2.cloned.1.call-done, bf16[1024,1024]{1,0:T(8,128)(2,1)} %copy-done.16), kind=kOutput, calls=%fused_computation.1 | convolution fusion | flops 8594128896 | bytes 18874368 | tf_op jit(solution)/shard_map/dot_general | solution.py:693
  251.7 2.8 copy-done.17
  254.5 5.9 %collective-permute-start.10 = (bf16[1024,1024]{1,0:T(8,128)(2,1)S(1)}, bf16[1024,1024]{1,0:T(8,128)(2,1)S(1)}, u32[]{:S(2)}, u32[]{:S(2)}) collective-permute-start(bf16[1024,1024]{1,0:T(8,128)(2,1)S(1)} %get-tuple-element.88.refs_2_), channel_id=1, source_target_pairs={{0,8},{1,9},{2,10},{3,11},{4,12},{5,13},{6,14},{7,15}} | collective-permute-start | bytes 6291464 | tf_op jit(solution)/shard_map/ppermute | solution.py:557
  261.4 4.5 select_dynamic-update-slice_fusion
  265.9 15.0 %fusion.24.up_ref = f32[1024,1024]{1,0:T(8,128)} fusion(bf16[1024,4096]{1,0:T(8,128)(2,1)} %all-gather.2.cloned.1.call-done, bf16[4096,1024]{1,0:T(8,128)(2,1)} %select_dynamic-update-slice_fusion), kind=kOutput, calls=%fused_computation.93 | convolution fusion | flops 8589934592 | bytes 20971520 | tf_op jit(solution)/shard_map/dot_general | solution.py:702
  280.9 16.9 %cotangent.1 = (f32[8192,128]{1,0:T(8,128)}, f32[16,8,128]{2,1,0:T(8,128)S(1)}, f32[16,8,128]{2,1,0:T(8,128)S(1)}, f32[8,128]{1,0:T(8,128)S(1)}, bf16[8,1,128,10...) custom-call(f32[1024,1024]{1,0:T(8,128)} %fusion.24.up_ref, ...), custom_call_target="tpu_custom_call" | custom-call | tf_op jit(solution)/shard_map/cotangent/pallas_call | solution.py:388
  297.7 4.7 collective-permute-done.10.refs_2_.refs_0_
  303.1 1.4 slice_dynamic-update-slice_fusion
  304.5 1.4 bitcast_dynamic-update-slice_fusion.2
  305.8 1.4 bitcast_dynamic-update-slice_fusion.1
  312.1 4.7 collective-permute-done.12
  316.8 3.7 collective-permute-done.13
  320.5 2.3 collective-permute-done.14
  323.8 1.6 copy-done.9
  325.4 1.6 copy-done.11
  326.9 5.7 %add_convert_fusion.3 = (bf16[1024,1024]{1,0:T(8,128)(2,1)}, bf16[1024,1024]{1,0:T(8,128)(2,1)S(1)}) fusion(bf16[1024,1024]{1,0:T(8,128)(2,1)S(1)} %get-tuple-element.63, bf16[4096,1024]{1,0:T(8,128)(2,1)} %copy-done.17, s32[]{:T(128)S(6)} %select_n.132, bf16[1024,1024]{1,0:T(8,128)(2,1)S(1)} %get-tuple-element.62, s32[]{:T(128)S(6)} %select_n.131), kind=kLoop, calls=%fused_computation.5 | loop fusion | flops 8388608 | bytes 12582920 | tf_op jit(solution)/shard_map/convert_element_type | solution.py:556
  332.7 1.4 copy-done.12
  334.0 14.3 %convolution_convert_fusion = bf16[1024,4096]{1,0:T(8,128)(2,1)} fusion(bf16[1024,1024]{1,0:T(8,128)(2,1)S(1)} %tie.16, bf16[4096,1024]{1,0:T(8,128)(2,1)} %select_dynamic-update-slice_fusion), kind=kOutput, calls=%fused_computation | convolution fusion | flops 8594128896 | bytes 18874368 | tf_op jit(solution)/shard_map/dot_general | solution.py:787
  349.1 4.4 all-to-all-start.3
  353.5 1.7 collective-permute-start.15
  355.2 2.0 collective-permute-start.16
  358.0 23.5 %back.1 = (bf16[8,2,128,1024]{3,2,1,0:T(8,128)(2,1)S(1)}, f32[2,7,8,128]{3,2,1,0:T(8,128)S(1)}) custom-call(f32[8192,128]{1,0:T(8,128)} %get-tuple-element.58.grad_ref, f32[2,8192,128]{2,1,0:T(8,128)} %get-tuple-element.59.sm_ref, f32[2,8192,128]{2,1,0:T(8,128)} %get-tuple-element.66.xt_ref, f32[16,8,128]{2,1,0:T(8,128)S(1)} %fusion.2.refs_2_.after_ref, ...), custom_call_target="tpu_custom_call" | custom-call | tf_op jit(solution)/shard_map/back/pallas_call | solution.py:388
  381.6 2.0 copy-done.14
  383.6 1.6 all-to-all-done.3.refs_0_
  385.2 4.8 all-to-all-start.4
  390.8 1.9 collective-permute-start.17
  392.7 9.2 %collective-permute-done.19 = f32[8,1024]{1,0:T(8,128)S(1)} collective-permute-done((f32[8,1024]{1,0:T(8,128)S(1)}, f32[8,1024]{1,0:T(8,128)S(1)}, u32[]{:S(2)}, u32[]{:S(2)}) %collective-permute-start.19) | collective-permute-done | bytes 32800 | tf_op jit(solution)/shard_map/ppermute | solution.py:825
  401.9 5.4 %collective-permute-done.18 = f32[8,1024]{1,0:T(8,128)S(1)} collective-permute-done((f32[8,1024]{1,0:T(8,128)S(1)}, f32[8,1024]{1,0:T(8,128)S(1)}, u32[]{:S(2)}, u32[]{:S(2)}) %collective-permute-start.18) | collective-permute-done | bytes 32800 | tf_op jit(solution)/shard_map/ppermute | solution.py:825
  407.4 7.0 %add_convert_fusion.2 = (bf16[1024,1024]{1,0:T(8,128)(2,1)}, bf16[1024,1024]{1,0:T(8,128)(2,1)}) fusion(bf16[1024,1024]{1,0:T(8,128)(2,1)S(1)} %get-tuple-element.71, bf16[4096,1024]{1,0:T(8,128)(2,1)} %copy-done.17, s32[]{:T(128)S(6)} %select_n.134, bf16[1024,1024]{1,0:T(8,128)(2,1)} %get-tuple-element.72, s32[]{:T(128)S(6)} %select_n.135), kind=kLoop, calls=%fused_computation.4 | loop fusion | flops 8388608 | bytes 12582920 | tf_op jit(solution)/shard_map/convert_element_type | solution.py:555
  415.7 5.9 %collective-permute-start.20 = (bf16[1024,1024]{1,0:T(8,128)(2,1)}, bf16[1024,1024]{1,0:T(8,128)(2,1)}, u32[]{:S(2)}, u32[]{:S(2)}) collective-permute-start(bf16[1024,1024]{1,0:T(8,128)(2,1)} %get-tuple-element.83), channel_id=1, source_target_pairs={{0,8},{8,16},{16,24},{1,9},{9,17},{17,25},{2,10},{10,18},{18,26},{... | collective-permute-start | bytes 6291464 | tf_op jit(solution)/shard_map/ppermute | solution.py:557
  421.7 41.7 %collective-permute-done.21 = bf16[1024,1024]{1,0:T(8,128)(2,1)S(1)} collective-permute-done((bf16[1024,1024]{1,0:T(8,128)(2,1)}, bf16[1024,1024]{1,0:T(8,128)(2,1)S(1)}, u32[]{:S(2)}, u32[]{:S(2)}) %collective-permute-start.21) | collective-permute-done | bytes 2097184 | tf_op jit(solution)/shard_map/ppermute | solution.py:558
  464.7 3.7 add_convert_fusion
  468.4 1.7 maximum_bitcast_fusion
  470.1 3.6 all-to-all-start.5
  473.7 7.8 %join.2 = bf16[3,128,8192]{2,1,0:T(8,128)(2,1)} custom-call(bf16[8,1,128,1024]{3,2,1,0:T(8,128)(2,1)} %all-to-all-done.3.refs_0_, bf16[8,2,128,1024]{3,2,1,0:T(8,128)(2,1)} %all-to-all-done.4.refs_1_), custom_call_target="tpu_custom_call" | custom-call | tf_op jit(solution)/shard_map/join/pallas_call | solution.py:388
  481.4 21.7 %all-to-all-done.5.refs_0_ = bf16[8,1,144,1024]{3,2,1,0:T(8,128)(2,1)S(1)} async-done(((bf16[8,1,144,1024]{3,2,1,0:T(8,128)(2,1)}), bf16[8,1,144,1024]{3,2,1,0:T(8,128)(2,1)S(1)}, u32[]{:S(2)}, u32[]{:S(2)}) %all-to-all-start.5) | async-done | bytes 2359328 | tf_op jit(solution)/shard_map/all_to_all | solution.py:837
  504.8 3.5 join.3
  (122 shorter events, 26.5 us)
Async XLA Ops:
  7.2 158.5 %copy-start = (f32[3,7,512]{2,1,0:T(8,128)S(1)}, f32[3,7,512]{2,1,0:T(8,128)}, u32[]{:S(2)}) copy-start(f32[3,7,512]{2,1,0:T(8,128)} %param.8) | copy-start | bytes 129028
  7.2 2.5 copy-start.15
  10.3 1.3 copy-start.13
  11.6 31.8 %all-to-all-start = ((bf16[8,1,128,1024]{3,2,1,0:T(8,128)(2,1)}), bf16[8,1,128,1024]{3,2,1,0:T(8,128)(2,1)S(1)}, u32[]{:S(2)}, u32[]{:S(2)}) async-start(bf16[8,1,128,1024]{3,2,1,0:T(8,128)(2,1)} %copy-done.13), calls=%async_computation | async-start | bytes 4194304 | tf_op jit(solution)/shard_map/all_to_all | solution.py:594
  16.8 221.5 %all-gather.2.cloned.1.call-start = ((), (), s32[]{:S(2)}) async-start(), calls=%async_computation.7 | async-start | bytes 9437184 | tf_op jit(solution)/shard_map/all_gather | solution.py:602
  17.8 0.7 collective-permute-start
  25.9 1.3 copy-start.3
  43.4 1.6 copy-start.4
  45.0 1.3 copy-start.5
  104.6 2.2 copy-start.2
  106.8 51.9 %collective-permute-start.1 = (bf16[1024,1024]{1,0:T(8,128)(2,1)S(1)}, bf16[1024,1024]{1,0:T(8,128)(2,1)}, u32[]{:S(2)}, u32[]{:S(2)}) collective-permute-start(bf16[1024,1024]{1,0:T(8,128)(2,1)S(1)} %bitcast.89), channel_id=1, source_target_pairs={{0,8},{8,16},{16,24},{1,9},{9,17},{17,25},{2,10},{10,18},{18,26},{... | collective-permute-start | bytes 6291464 | tf_op jit(solution)/shard_map/ppermute | solution.py:510
  115.8 48.4 %collective-permute-start.2 = (bf16[1024,1024]{1,0:T(8,128)(2,1)S(1)}, bf16[1024,1024]{1,0:T(8,128)(2,1)}, u32[]{:S(2)}, u32[]{:S(2)}) collective-permute-start(bf16[1024,1024]{1,0:T(8,128)(2,1)S(1)} %bitcast.90), channel_id=1, source_target_pairs={{8,0},{16,8},{24,16},{9,1},{17,9},{25,17},{10,2},{18,10},{26,18},{... | collective-permute-start | bytes 6291464 | tf_op jit(solution)/shard_map/ppermute | solution.py:511
  158.8 50.7 %collective-permute-start.3 = (bf16[1024,1024]{1,0:T(8,128)(2,1)}, bf16[1024,1024]{1,0:T(8,128)(2,1)}, u32[]{:S(2)}, u32[]{:S(2)}) collective-permute-start(bf16[1024,1024]{1,0:T(8,128)(2,1)} %collective-permute-done.1.hold_ref), channel_id=1, source_target_pairs={{8,16},{16,24},{9,17},{17,25},{10,18},{18,26},{11,19},{19,27},{12,... | collective-permute-start | bytes 6291464 | tf_op jit(solution)/shard_map/ppermute | solution.py:510
  164.3 47.9 %collective-permute-start.4 = (bf16[1024,1024]{1,0:T(8,128)(2,1)}, bf16[1024,1024]{1,0:T(8,128)(2,1)}, u32[]{:S(2)}, u32[]{:S(2)}) collective-permute-start(bf16[1024,1024]{1,0:T(8,128)(2,1)} %collective-permute-done.2), channel_id=1, source_target_pairs={{8,0},{16,8},{9,1},{17,9},{10,2},{18,10},{11,3},{19,11},{12,4},{20... | collective-permute-start | bytes 6291464 | tf_op jit(solution)/shard_map/ppermute | solution.py:511
  166.2 1.6 copy-start.6
  167.8 1.4 copy-start.7
  169.2 50.8 %all-to-all-start.2 = ((bf16[8,1,128,1024]{3,2,1,0:T(8,128)(2,1)}), bf16[8,1,128,1024]{3,2,1,0:T(8,128)(2,1)}, u32[]{:S(2)}, u32[]{:S(2)}) async-start(bf16[8,1,128,1024]{3,2,1,0:T(8,128)(2,1)} %copy-done.7), calls=%async_computation.2 | async-start | bytes 4194304 | tf_op jit(solution)/shard_map/all_to_all | solution.py:599
  173.6 334.8 %reduce-scatter.2.cloned.1.call-start = ((), (), s32[]{:S(2)}) async-start(), calls=%async_computation.8 | async-start | bytes 9437184 | tf_op jit(solution)/shard_map/reduce_scatter | solution.py:790
  191.3 18.1 %collective-permute-start.5 = (f32[16,8,128]{2,1,0:T(8,128)S(1)}, f32[16,8,128]{2,1,0:T(8,128)S(1)}, u32[]{:S(2)}, u32[]{:S(2)}) collective-permute-start(f32[16,8,128]{2,1,0:T(8,128)S(1)} %get-tuple-element.43), channel_id=1, source_target_pairs={{0,8},{8,16},{16,24},{1,9},{9,17},{17,25},{2,10},{10,18},{18,26},{... | collective-permute-start | bytes 196616 | tf_op jit(solution)/shard_map/ppermute | solution.py:658
  195.9 13.5 %collective-permute-start.6 = (f32[16,8,128]{2,1,0:T(8,128)S(1)}, f32[16,8,128]{2,1,0:T(8,128)S(1)}, u32[]{:S(2)}, u32[]{:S(2)}) collective-permute-start(f32[16,8,128]{2,1,0:T(8,128)S(1)} %get-tuple-element.43), channel_id=1, source_target_pairs={{0,16},{8,24},{1,17},{9,25},{2,18},{10,26},{3,19},{11,27},{4,20},{... | collective-permute-start | bytes 196616 | tf_op jit(solution)/shard_map/ppermute | solution.py:658
  200.4 9.0 %collective-permute-start.7 = (f32[16,8,128]{2,1,0:T(8,128)S(1)}, f32[16,8,128]{2,1,0:T(8,128)S(1)}, u32[]{:S(2)}, u32[]{:S(2)}) collective-permute-start(f32[16,8,128]{2,1,0:T(8,128)S(1)} %get-tuple-element.43), channel_id=1, source_target_pairs={{0,24},{1,25},{2,26},{3,27},{4,28},{5,29},{6,30},{7,31}} | collective-permute-start | bytes 196616 | tf_op jit(solution)/shard_map/ppermute | solution.py:658
  212.1 49.2 %collective-permute-start.8 = (bf16[1024,1024]{1,0:T(8,128)(2,1)}, bf16[1024,1024]{1,0:T(8,128)(2,1)}, u32[]{:S(2)}, u32[]{:S(2)}) collective-permute-start(bf16[1024,1024]{1,0:T(8,128)(2,1)} %get-tuple-element.44), channel_id=1, source_target_pairs={{16,24},{17,25},{18,26},{19,27},{20,28},{21,29},{22,30},{23,31}} | collective-permute-start | bytes 6291464 | tf_op jit(solution)/shard_map/ppermute | solution.py:510
  214.2 47.2 %collective-permute-start.9 = (bf16[1024,1024]{1,0:T(8,128)(2,1)}, bf16[1024,1024]{1,0:T(8,128)(2,1)}, u32[]{:S(2)}, u32[]{:S(2)}) collective-permute-start(bf16[1024,1024]{1,0:T(8,128)(2,1)} %get-tuple-element.45), channel_id=1, source_target_pairs={{8,0},{9,1},{10,2},{11,3},{12,4},{13,5},{14,6},{15,7}} | collective-permute-start | bytes 6291464 | tf_op jit(solution)/shard_map/ppermute | solution.py:511
  236.9 1.4 copy-start.16
  251.2 3.3 copy-start.17
  254.5 6.9 %copy-start.18 = (bf16[1024,1024]{1,0:T(8,128)(2,1)}, bf16[1024,1024]{1,0:T(8,128)(2,1)S(1)}, u32[]{:S(2)}) copy-start(bf16[1024,1024]{1,0:T(8,128)(2,1)S(1)} %get-tuple-element.87.refs_3_) | copy-start | bytes 6291460
  254.5 7.0 %copy-start.19 = (bf16[1024,1024]{1,0:T(8,128)(2,1)}, bf16[1024,1024]{1,0:T(8,128)(2,1)S(1)}, u32[]{:S(2)}) copy-start(bf16[1024,1024]{1,0:T(8,128)(2,1)S(1)} %get-tuple-element.88.refs_2_) | copy-start | bytes 6291460
  254.5 47.9 %collective-permute-start.10 = (bf16[1024,1024]{1,0:T(8,128)(2,1)S(1)}, bf16[1024,1024]{1,0:T(8,128)(2,1)S(1)}, u32[]{:S(2)}, u32[]{:S(2)}) collective-permute-start(bf16[1024,1024]{1,0:T(8,128)(2,1)S(1)} %get-tuple-element.88.refs_2_), channel_id=1, source_target_pairs={{0,8},{1,9},{2,10},{3,11},{4,12},{5,13},{6,14},{7,15}} | collective-permute-start | bytes 6291464 | tf_op jit(solution)/shard_map/ppermute | solution.py:557
  260.4 42.0 %collective-permute-start.11 = (bf16[1024,1024]{1,0:T(8,128)(2,1)S(1)}, bf16[1024,1024]{1,0:T(8,128)(2,1)S(1)}, u32[]{:S(2)}, u32[]{:S(2)}) collective-permute-start(bf16[1024,1024]{1,0:T(8,128)(2,1)S(1)} %get-tuple-element.87.refs_3_), channel_id=1, source_target_pairs={{24,16},{25,17},{26,18},{27,19},{28,20},{29,21},{30,22},{31,23}} | collective-permute-start | bytes 6291464 | tf_op jit(solution)/shard_map/ppermute | solution.py:558
  302.4 5.5 %copy-start.8 = (bf16[1024,1024]{1,0:T(8,128)(2,1)}, bf16[1024,1024]{1,0:T(8,128)(2,1)S(1)}, u32[]{:S(2)}) copy-start(bf16[1024,1024]{1,0:T(8,128)(2,1)S(1)} %collective-permute-done.10.refs_2_.refs_0_) | copy-start | bytes 6291460
  302.4 5.5 %copy-start.10 = (bf16[1024,1024]{1,0:T(8,128)(2,1)}, bf16[1024,1024]{1,0:T(8,128)(2,1)S(1)}, u32[]{:S(2)}) copy-start(bf16[1024,1024]{1,0:T(8,128)(2,1)S(1)} %collective-permute-done.11.refs_3_.refs_1_) | copy-start | bytes 6291460
  307.8 9.0 %collective-permute-start.12 = (f32[384,128]{1,0:T(8,128)}, f32[384,128]{1,0:T(8,128)S(1)}, u32[]{:S(2)}, u32[]{:S(2)}) collective-permute-start(f32[384,128]{1,0:T(8,128)} %constant_dynamic-update-slice_fusion), channel_id=1, source_target_pairs={{8,0},{16,8},{24,16},{9,1},{17,9},{25,17},{10,2},{18,10},{26,18},{... | collective-permute-start | bytes 589832 | tf_op jit(solution)/shard_map/ppermute | solution.py:658
  309.1 11.4 %collective-permute-start.13 = (f32[16,8,128]{2,1,0:T(8,128)S(1)}, f32[16,8,128]{2,1,0:T(8,128)}, u32[]{:S(2)}, u32[]{:S(2)}) collective-permute-start(f32[16,8,128]{2,1,0:T(8,128)S(1)} %get-tuple-element.61), channel_id=1, source_target_pairs={{16,0},{24,8},{17,1},{25,9},{18,2},{26,10},{19,3},{27,11},{20,4},{... | collective-permute-start | bytes 196616 | tf_op jit(solution)/shard_map/ppermute | solution.py:658
  310.4 12.4 %collective-permute-start.14 = (f32[16,8,128]{2,1,0:T(8,128)S(1)}, f32[16,8,128]{2,1,0:T(8,128)}, u32[]{:S(2)}, u32[]{:S(2)}) collective-permute-start(f32[16,8,128]{2,1,0:T(8,128)S(1)} %get-tuple-element.61), channel_id=1, source_target_pairs={{24,0},{25,1},{26,2},{27,3},{28,4},{29,5},{30,6},{31,7}} | collective-permute-start | bytes 196616 | tf_op jit(solution)/shard_map/ppermute | solution.py:658
  323.8 1.6 copy-start.9
  325.4 1.6 copy-start.11
  332.7 1.4 copy-start.12
  349.1 36.1 %all-to-all-start.3 = ((bf16[8,1,128,1024]{3,2,1,0:T(8,128)(2,1)}), bf16[8,1,128,1024]{3,2,1,0:T(8,128)(2,1)}, u32[]{:S(2)}, u32[]{:S(2)}) async-start(bf16[8,1,128,1024]{3,2,1,0:T(8,128)(2,1)} %bitcast_dynamic-update-slice_fusion.3), calls=%async_computation.4 | async-start | bytes 4194304 | tf_op jit(solution)/shard_map/all_to_all | solution.py:782
  353.5 53.9 %collective-permute-start.15 = (bf16[1024,1024]{1,0:T(8,128)(2,1)}, bf16[1024,1024]{1,0:T(8,128)(2,1)S(1)}, u32[]{:S(2)}, u32[]{:S(2)}) collective-permute-start(bf16[1024,1024]{1,0:T(8,128)(2,1)} %copy-done.12), channel_id=1, source_target_pairs={{0,8},{8,16},{1,9},{9,17},{2,10},{10,18},{3,11},{11,19},{4,12},{12... | collective-permute-start | bytes 6291464 | tf_op jit(solution)/shard_map/ppermute | solution.py:557
  355.2 52.2 %collective-permute-start.16 = (bf16[1024,1024]{1,0:T(8,128)(2,1)}, bf16[1024,1024]{1,0:T(8,128)(2,1)}, u32[]{:S(2)}, u32[]{:S(2)}) collective-permute-start(bf16[1024,1024]{1,0:T(8,128)(2,1)} %get-tuple-element.85.refs_2_), channel_id=1, source_target_pairs={{24,16},{16,8},{25,17},{17,9},{26,18},{18,10},{27,19},{19,11},{28,... | collective-permute-start | bytes 6291464 | tf_op jit(solution)/shard_map/ppermute | solution.py:558
  381.6 2.0 copy-start.14
  385.2 84.8 %all-to-all-start.4 = ((bf16[8,2,128,1024]{3,2,1,0:T(8,128)(2,1)}), bf16[8,2,128,1024]{3,2,1,0:T(8,128)(2,1)}, u32[]{:S(2)}, u32[]{:S(2)}) async-start(bf16[8,2,128,1024]{3,2,1,0:T(8,128)(2,1)} %copy-done.14), calls=%async_computation.5 | async-start | bytes 8388608 | tf_op jit(solution)/shard_map/all_to_all | solution.py:817
  390.7 11.3 %collective-permute-start.19 = (f32[8,1024]{1,0:T(8,128)S(1)}, f32[8,1024]{1,0:T(8,128)S(1)}, u32[]{:S(2)}, u32[]{:S(2)}) collective-permute-start(f32[8,1024]{1,0:T(8,128)S(1)} %pad.10), channel_id=1, source_target_pairs={{0,24},{8,0},{16,8},{24,16},{1,25},{9,1},{17,9},{25,17},{2,26},{10... | collective-permute-start | bytes 98312 | tf_op jit(solution)/shard_map/ppermute | solution.py:825
  390.7 16.6 %collective-permute-start.18 = (f32[8,1024]{1,0:T(8,128)S(1)}, f32[8,1024]{1,0:T(8,128)S(1)}, u32[]{:S(2)}, u32[]{:S(2)}) collective-permute-start(f32[8,1024]{1,0:T(8,128)S(1)} %pad.10), channel_id=1, source_target_pairs={{0,16},{8,24},{16,0},{24,8},{1,17},{9,25},{17,1},{25,9},{2,18},{10... | collective-permute-start | bytes 98312 | tf_op jit(solution)/shard_map/ppermute | solution.py:825
  390.8 16.5 %collective-permute-start.17 = (f32[8,1024]{1,0:T(8,128)S(1)}, f32[8,1024]{1,0:T(8,128)S(1)}, u32[]{:S(2)}, u32[]{:S(2)}) collective-permute-start(f32[8,1024]{1,0:T(8,128)S(1)} %pad.10), channel_id=1, source_target_pairs={{0,8},{8,16},{16,24},{24,0},{1,9},{9,17},{17,25},{25,1},{2,10},{10... | collective-permute-start | bytes 98312 | tf_op jit(solution)/shard_map/ppermute | solution.py:825
  414.4 49.0 %collective-permute-start.21 = (bf16[1024,1024]{1,0:T(8,128)(2,1)}, bf16[1024,1024]{1,0:T(8,128)(2,1)S(1)}, u32[]{:S(2)}, u32[]{:S(2)}) collective-permute-start(bf16[1024,1024]{1,0:T(8,128)(2,1)} %get-tuple-element.84), channel_id=1, source_target_pairs={{24,16},{16,8},{8,0},{25,17},{17,9},{9,1},{26,18},{18,10},{10,2},{... | collective-permute-start | bytes 6291464 | tf_op jit(solution)/shard_map/ppermute | solution.py:558
  415.7 49.0 %collective-permute-start.20 = (bf16[1024,1024]{1,0:T(8,128)(2,1)}, bf16[1024,1024]{1,0:T(8,128)(2,1)}, u32[]{:S(2)}, u32[]{:S(2)}) collective-permute-start(bf16[1024,1024]{1,0:T(8,128)(2,1)} %get-tuple-element.83), channel_id=1, source_target_pairs={{0,8},{8,16},{16,24},{1,9},{9,17},{17,25},{2,10},{10,18},{18,26},{... | collective-permute-start | bytes 6291464 | tf_op jit(solution)/shard_map/ppermute | solution.py:557
  470.1 33.1 %all-to-all-start.5 = ((bf16[8,1,144,1024]{3,2,1,0:T(8,128)(2,1)}), bf16[8,1,144,1024]{3,2,1,0:T(8,128)(2,1)S(1)}, u32[]{:S(2)}, u32[]{:S(2)}) async-start(bf16[8,1,144,1024]{3,2,1,0:T(8,128)(2,1)} %maximum_bitcast_fusion), calls=%async_computation.6 | async-start | bytes 4718592 | tf_op jit(solution)/shard_map/all_to_all | solution.py:837
  504.2 4.1 copy-start.1
Sparse Core Ops, SparseCore 0:
  107.0 57.9 all-gather.1
  348.5 104.8 reduce-scatter.1

commit v3 on v2

--- a/solution.py
+++ b/solution.py
@@ -11,7 +11,7 @@
 LANES = 128
 EDGE = 8
 STEP = 8
-VMEM = 48 * 1024 * 1024
+VMEM = 60 * 1024 * 1024
 
 
 def at(token, rows):
@@ -73,7 +73,6 @@
     rim_ref,
     taps_ref,
     decay_ref,
-    hold_ref,
     sm_ref,
     mixed_ref,
     xt_ref,
@@ -183,20 +182,6 @@
         ].astype(jnp.bfloat16)
 
 
-def clear_or_shift(pad, rows, tok):
-    first = pl.program_id(0) == 0
-
-    @pl.when(first)
-    def _():
-        for i in range(pad.shape[0]):
-            pad[i, pl.ds(tok * rows, EDGE * rows), :] = jnp.zeros((EDGE * rows, LANES), jnp.float32)
-
-    @pl.when(jnp.logical_not(first))
-    def _():
-        for i in range(pad.shape[0]):
-            pad[i, pl.ds(tok * rows, EDGE * rows), :] = pad[i, pl.ds(0, EDGE * rows), :]
-
-
 def spread_back(
     rows, tok, i, pad, xt_at, taps, total, out_ref, gtaps_ref, staged
 ):
@@ -229,38 +214,28 @@
     rows,
     tok,
     up_ref,
-    gated_ref,
     sm_ref,
     mixed_ref,
     field_ref,
-    xt_ref,
-    taps_ref,
     decay_ref,
+    heads_ref,
+    hold_ref,
     grad_ref,
-    mid_ref,
+    zero_ref,
+    ahead_ref,
     end_ref,
     gskip_ref,
-    out_ref,
-    gtaps_ref,
-    head_ref,
-    tail_ref,
-    kept_ref,
-    pad,
     staged,
     state,
     summed,
-    total,
 ):
-    modes, lags = decay_ref.shape[0], taps_ref.shape[1]
+    modes = decay_ref.shape[0]
 
     @pl.when(pl.program_id(0) == 0)
     def _():
         state[...] = jnp.zeros_like(state)
         summed[...] = jnp.zeros_like(summed)
-        total[...] = jnp.zeros_like(total)
-
-    kept_ref[...] = gated_ref[...]
-    clear_or_shift(pad, rows, tok)
+
     to_token_rows(staged, 0, up_ref[...], rows)
     decay = [decay_ref[m] for m in range(modes)]
 
@@ -271,7 +246,7 @@
             up = staged[place, :]
             grad = up * sm_ref[place, :]
             grad_ref[place, :] = grad
-            pad[0, place, :] = up * field_ref[place, :]
+            zero_ref[place, :] = up * field_ref[place, :]
             added = added + grad * mixed_ref[place, :]
             held = [decay[m] * held[m] + grad for m in range(modes)]
         return tuple(held) + (added,)
@@ -281,38 +256,26 @@
         0, last, retreat, tuple(state[m] for m in range(modes)) + (summed[...],)
     )
     for m in range(modes):
-        mid_ref[m] = carry[m]
+        ahead_ref[pl.ds(m * rows, rows), :] = carry[m]
     carry = retreat(last, carry)
+    edge = EDGE * rows
+    heads = [grad_ref[pl.ds(0, edge), :], heads_ref[0], heads_ref[1], zero_ref[pl.ds(0, edge), :]]
+    for k, head in enumerate(heads):
+        ahead_ref[pl.ds(modes * rows + k * edge, edge), :] = head
     for m in range(modes):
         state[m] = carry[m]
         end_ref[m] = carry[m]
     summed[...] = carry[-1]
     gskip_ref[...] = carry[-1]
-    spread_back(
-        rows,
-        tok,
-        0,
-        pad,
-        lambda place: xt_ref[place, :],
-        [taps_ref[0, j] for j in range(lags)],
-        total,
-        out_ref,
-        gtaps_ref,
-        staged,
-    )
-
-    @pl.when(pl.program_id(0) == 0)
-    def _():
-        tail_ref[...] = pad[0, pl.ds((tok - EDGE) * rows, EDGE * rows), :]
-
-    head_ref[...] = pad[0, pl.ds(0, EDGE * rows), :]
 
 
 def back_kernel(
     rows,
     tok,
     grad_ref,
+    zero_ref,
     sm_ref,
+    first_ref,
     xt_ref,
     after_ref,
     ahead_ref,
@@ -340,15 +303,18 @@
             grad, one, two = [ahead_ref[at(k * EDGE + u, rows), :] for k in range(3)]
             held = [decay[m] * held[m] + grad for m in range(modes)]
             mixed = total_of([residue[m] * held[m] for m in range(modes)] + [skip * grad])
-            pad[0, at(tok + u, rows), :] = mixed * two
-            pad[1, at(tok + u, rows), :] = mixed * one
+            pad[0, at(tok + u, rows), :] = ahead_ref[at(3 * EDGE + u, rows), :]
+            pad[1, at(tok + u, rows), :] = mixed * two
+            pad[2, at(tok + u, rows), :] = mixed * one
         for m in range(modes):
             state[m] = held[m]
 
     @pl.when(pl.program_id(0) != 0)
     def _():
-        for i in range(2):
+        for i in range(3):
             pad[i, pl.ds(tok * rows, EDGE * rows), :] = pad[i, pl.ds(0, EDGE * rows), :]
+
+    pad[0, pl.ds(0, tok * rows), :] = zero_ref[...]
 
 
     def retreat(n, held):
@@ -358,21 +324,21 @@
             grad = grad_ref[place, :]
             held = [decay[m] * held[m] + grad for m in range(modes)]
             mixed = total_of([residue[m] * held[m] for m in range(modes)] + [skip * grad])
-            pad[0, place, :] = mixed * sm_ref[1, place, :]
-            pad[1, place, :] = mixed * sm_ref[0, place, :]
+            pad[1, place, :] = mixed * sm_ref[1, place, :]
+            pad[2, place, :] = mixed * sm_ref[0, place, :]
         return tuple(held)
 
     held = lax.fori_loop(0, tok // STEP, retreat, tuple(state[m] for m in range(modes)))
     for m in range(modes):
         state[m] = held[m]
-    for i in range(2):
+    for i in range(3):
         spread_back(
             rows,
             tok,
             i,
             pad,
-            lambda place, i=i: xt_ref[i, place, :],
-            [taps_ref[i + 1, j] for j in range(lags)],
+            lambda place, i=i: xt_ref[i - 1, place, :] if i else first_ref[place, :],
+            [taps_ref[i, j] for j in range(lags)],
             total,
             out_ref,
             gtaps_ref,
@@ -403,7 +369,7 @@
     pass
 
 
-def tie(values, after):
+def tie(values, after, flops=0):
     values, after = tuple(values), tuple(after)
     held = pl.BlockSpec(memory_space=pl.ANY)
     return pl.pallas_call(
@@ -413,6 +379,7 @@
         out_shape=[jax.ShapeDtypeStruct(a.shape, a.dtype) for a in values],
         input_output_aliases={i: i for i in range(len(values))},
         compiler_params=pltpu.CompilerParams(vmem_limit_bytes=VMEM),
+        cost_estimate=pl.CostEstimate(flops=flops, bytes_accessed=0, transcendentals=0),
         name="tie",
     )(*values, *after)
 
@@ -491,6 +458,28 @@
         ],
         jax.ShapeDtypeStruct((total, tok, lo * wide), dtype),
         pl.BlockSpec((total, tok, wide), lambda n: (0, 0, n)),
+        [],
+        0,
+    )
+
+
+def project_kernel(x_ref, w_ref, out_ref):
+    out_ref[...] = lax.dot_general(
+        x_ref[...], w_ref[...], (((1,), (1,)), ((), ())), preferred_element_type=jnp.float32
+    ).astype(out_ref.dtype)
+
+
+def project(x, w):
+    (tokens, wide), outs = x.shape, w.shape[0]
+    size = math.gcd(outs, 512)
+    return call(
+        project_kernel,
+        "project",
+        outs // size,
+        (x, w),
+        [whole((tokens, wide)), pl.BlockSpec((size, wide), lambda n: (n, 0))],
+        jax.ShapeDtypeStruct((tokens, outs), x.dtype),
+        pl.BlockSpec((tokens, size), lambda n: (0, n)),
         [],
         0,
     )
@@ -597,10 +586,6 @@
     x12 = lax.all_to_all(packed12, "lo", 0, 0, tiled=True)
     (packed0,) = tie((packed0,), (x12,))
     x0 = lax.all_to_all(packed0, "lo", 0, 0, tiled=True)
-    (cotangent,) = tie((out_cotangent,), (x12,))
-    cotangent = lax.all_gather(cotangent, "tp", axis=1, tiled=True)
-    cotangent = lax.all_gather(cotangent, "lo", axis=0, tiled=True)
-
     flat = tok * rows
     tokens = length * rows
     up_one = pl.BlockSpec((flat, LANES), lambda n: (n, 0))
@@ -627,18 +612,20 @@
 
     mover = Planes(own, hi, plane)
     mover.step()
+    (cotangent,) = tie((out_cotangent,), (x12, mover.right, mover.left))
+    cotangent = lax.all_gather(cotangent, "tp", axis=1, tiled=True)
+    cotangent = lax.all_gather(cotangent, "lo", axis=0, tiled=True)
 
     sm12, mixed, xt12, ending, mover.result = call(
         functools.partial(smooth_kernel, rows, tok),
         "smooth",
         lo,
-        (x12, x12, taps, decay, mover.right),
+        (x12, x12, taps, decay),
         [
             pl.BlockSpec((1, 2 * tok, wide), lambda n: (n, 0, 0)),
             rim_spec,
             taps_spec,
             mode_spec,
-            held_spec,
         ],
         [
             shape((2, tokens, LANES), f32),
@@ -700,63 +687,39 @@
     weights = mover.result
 
     upstream = jnp.dot(cotangent, weights, preferred_element_type=f32)
-    grad_field, back_mid, back_end, grad_skip, grads0, grad_taps0, head, tail, kept = call(
+    partial_out = project(gated, weights)
+    output = lax.psum_scatter(partial_out, "lo", scatter_dimension=0, tiled=True)
+    output = lax.psum_scatter(output, "tp", scatter_dimension=1, tiled=True)
+    edge = EDGE * rows
+    held = modes * rows + 4 * edge
+    grad_field, grad_zero, ahead, back_end, grad_skip = call(
         functools.partial(cotangent_kernel, rows, tok),
         "cotangent",
         lo,
-        (upstream, gated, sm0, mixed, field, xt0, taps, decay),
-        [
-            down_wide,
+        (upstream, sm0, mixed, field, decay, sm12, partial_out),
+        [
             down_wide,
             down_one,
             down_one,
             down_one,
-            down_one,
-            taps_spec,
             mode_spec,
+            whole((2, edge, LANES)),
+            held_spec,
         ],
         [
             shape((tokens, LANES), f32),
-            shape((modes, rows, LANES), f32),
+            shape((tokens, LANES), f32),
+            shape((held, LANES), f32),
             shape((modes, rows, LANES), f32),
             shape((rows, LANES), f32),
-            shape((lo, 1, tok, wide), jnp.bfloat16),
-            shape((1, lags, rows, LANES), f32),
-            shape((EDGE * rows, LANES), f32),
-            shape((EDGE * rows, LANES), f32),
-            shape(gated.shape, gated.dtype),
-        ],
-        [
-            down_one,
-            mode_spec,
-            mode_spec,
-            skip_spec,
-            grads_spec(1),
-            whole((1, lags, rows, LANES)),
-            whole((EDGE * rows, LANES)),
-            whole((EDGE * rows, LANES)),
-            down_wide,
-        ],
-        [
-            padded(1),
-            staged,
-            states,
-            pltpu.VMEM((rows, LANES), f32),
-            pltpu.VMEM((1, lags, rows, LANES), f32),
-        ],
+        ],
+        [down_one, down_one, whole((held, LANES)), mode_spec, skip_spec],
+        [staged, states, pltpu.VMEM((rows, LANES), f32)],
         0,
     )
 
-    back_mid, back_end = tie((back_mid, back_end), (sums.right, sums.left))
-    edge = EDGE * rows
-    heads = [
-        back_mid.reshape(-1, LANES),
-        grad_field[:edge],
-        sm12[0, :edge],
-        sm12[1, :edge],
-        head,
-    ]
-    ahead = from_plane(jnp.concatenate(heads), 1)
+    ahead, back_end = tie((ahead, back_end), (sums.right, sums.left))
+    ahead = from_plane(ahead, 1)
     beyond = jnp.zeros_like(back_end)
     for k in reversed(range(2, hi)):
         beyond = from_plane(back_end, k) + plane_decay * beyond
@@ -765,39 +728,18 @@
     )
     ahead = ahead[modes * rows :]
 
-    edges = (EDGE, rows, LANES)
-    beyond, tail = ahead[3 * edge :].reshape(edges), tail.reshape(edges)
-    last = xt0[-edge:].reshape(edges)
-    joined = jnp.concatenate([tail, beyond])
-    extra = jnp.concatenate([jnp.zeros_like(tail), beyond])
-    fixed = sum(taps[0, j] * joined[j : j + EDGE] for j in range(lags))
-    grads0 = lax.dynamic_update_slice(
-        grads0,
-        fixed.reshape(1, 1, EDGE, wide).astype(grads0.dtype),
-        (lo - 1, 0, tok - EDGE, 0),
-    )
-    grad_taps0 = grad_taps0[0] + jnp.stack(
-        [jnp.sum(last * extra[j : j + EDGE], axis=0) for j in range(lags)]
-    )
-    grads0 = lax.all_to_all(grads0, "lo", 0, 0, tiled=True)
-
     sums.right, sums.left = tie((sums.right, sums.left), (after, ahead))
     sums.step()
-    (kept,) = tie((kept,), (sums.to_right, sums.to_left))
-    partial_out = lax.dot_general(
-        kept, weights, (((1,), (1,)), ((), ())), preferred_element_type=f32
-    ).astype(jnp.bfloat16)
-    output = lax.psum_scatter(partial_out, "lo", scatter_dimension=0, tiled=True)
-    output = lax.psum_scatter(output, "tp", scatter_dimension=1, tiled=True)
-
-    grads12, grad_taps12 = call(
+    grads, grad_taps = call(
         functools.partial(back_kernel, rows, tok),
         "back",
         lo,
-        (grad_field, sm12, xt12, after, ahead, decay, residue, direct, taps),
-        [
+        (grad_field, grad_zero, sm12, xt0, xt12, after, ahead, decay, residue, direct, taps),
+        [
+            down_one,
             down_one,
             down_two,
+            down_one,
             down_two,
             mode_spec,
             whole((4 * edge, LANES)),
@@ -807,15 +749,15 @@
             taps_spec,
         ],
         [
-            shape((lo, 2, tok, wide), jnp.bfloat16),
-            shape((2, lags, rows, LANES), f32),
-        ],
-        [grads_spec(2), whole((2, lags, rows, LANES))],
-        [padded(2), staged, states, pltpu.VMEM((2, lags, rows, LANES), f32)],
+            shape((lo, 3, tok, wide), jnp.bfloat16),
+            shape((3, lags, rows, LANES), f32),
+        ],
+        [grads_spec(3), taps_spec],
+        [padded(3), staged, states, pltpu.VMEM((3, lags, rows, LANES), f32)],
         0,
     )
-    grads12 = lax.all_to_all(grads12, "lo", 0, 0, tiled=True)
-    grad_taps = jnp.concatenate([grad_taps0[None], grad_taps12])
+    grads = lax.all_to_all(grads, "lo", 0, 0, tiled=True)
+    sums.right, sums.left = tie((sums.right, sums.left), (grad_taps,), 30 * 10**9)
     grad_taps = jnp.sum(grad_taps.reshape(3 * lags * near, members), axis=1)
     part = jnp.concatenate([grad_skip.reshape(-1), grad_taps])
     part = jnp.pad(part, (0, -part.size % wide)).reshape(-1, wide)
@@ -823,7 +765,6 @@
     small = part
     for k in range(1, hi):
         small = small + lax.ppermute(part, "hi", [(z, (z + k) % hi) for z in range(hi)])
-    sums.right, sums.left = tie((sums.right, sums.left), (small,))
     while sums.done < hi - 1:
         sums.step()
 
@@ -834,9 +775,10 @@
     extra = jnp.concatenate([coarse, fine])
     extra = jnp.broadcast_to(extra, (lo,) + extra.shape)
     reduced = jnp.concatenate([reduced, extra], axis=1)[:, None]
+    (reduced,) = tie((reduced,), (output,), 30 * 10**9)
     reduced = lax.all_to_all(reduced, "lo", 0, 0, tiled=True)
     grad_weight = join_channels((reduced,), f32, count)[0]
-    grad_streams = join_channels((grads0, grads12), grads0.dtype, tok)
+    grad_streams = join_channels((grads,), grads.dtype, tok)
     small = reduced[:, 0, count:].astype(f32)
     small = (small[:, : part.shape[0]] + small[:, part.shape[0] :]).reshape(lo, -1)
     grad_skip = small[:, :wide].reshape(channels)

time: 517 us -> 462 us (0.89)
  blocking collectives: 58.3 us -> 0 us
  Pallas kernels: 91.6 us -> 120 us
  local copies, waits for them, and re-layouts: 37 us -> 22.3 us
  matrix products: 42.2 us -> 28.7 us
  starting transfers between devices: 74.3 us -> 79.8 us
    all_to_all x1 -> x0, blocking collectives: 58.3 us -> none  [shards(): x12 = lax.all_to_all(packed12, 'lo', 0, 0, tiled=True)]
    ppermute x3, waiting for transfers between devices: 41.7 us -> 0.01 us  [step(): lax.ppermute(self.to_left, 'hi', [(hi - 1 - z, hi - 2 - z) for z in range...]
    pallas_call x8 -> x9, Pallas kernels: 91.6 us -> 120 us  [call(): pl.pallas_call(kernel, grid=(blocks,), in_specs=in_specs, out_specs=out_s...]
    ppermute x3, waiting for transfers between devices: 14.6 us -> 39.2 us  [shards(): lax.ppermute(part, 'hi', [(z, (z + k) % hi) for z in range(hi)])]
    unnamed x55 -> x28, local copies, waits for them, and re-layouts: 29.5 us -> 9.69 us
    dot_general x1 -> x0, matrix products: 14.3 us -> none  [shards(): lax.dot_general(kept, weights, (((1,), (1,)), ((), ())), preferred_elemen...]
    ppermute x3, waiting for transfers between devices: 5.94 us -> 12.8 us  [step(): lax.ppermute(self.to_right, 'hi', [(z, z + 1) for z in range(s)])]
  transfers between devices with their start and end apart: 29 -> 29, of which waited for: 14 -> 15; matrix products, arithmetic and copies ran while one was open for 13% -> 16% of each run, Pallas kernels for 18% -> 20%
where the time goes in v3:
time: 462 us; the launch traced here: 460 us
  waiting for transfers between devices  158 us (34%)
  Pallas kernels  120 us (26%)
  starting transfers between devices  79.8 us (17%)
  other arithmetic  37.3 us (8%)
  matrix products  28.7 us (6%)
  local copies, waits for them, and re-layouts  22.3 us (5%)
  between operations  14.5 us (3%)
    pallas_call x9, Pallas kernels, call(): pl.pallas_call(kernel, grid=(blocks,), in_specs=in_specs, out_specs=out_s...  120 us
    ppermute x3, waiting for transfers between devices, step(): lax.ppermute(self.right, 'hi', [(z, z + 1) for z in range(k - 1, hi - 1)])  43.9 us
    ppermute x3, waiting for transfers between devices, shards(): lax.ppermute(part, 'hi', [(z, (z + k) % hi) for z in range(hi)])  39.2 us
    all_to_all x1, waiting for transfers between devices, shards(): reduced = lax.all_to_all(reduced, 'lo', 0, 0, tiled=True)  21.6 us
    ppermute x6, starting transfers between devices, from_plane(): return lax.ppermute(a, 'hi', pairs)  18.3 us
    all_to_all x1, waiting for transfers between devices, shards(): lax.all_to_all(split_channels(out_weight[None], lo, 0, 1), 'lo', 0, 0, ti...  16.2 us
    dot_general x1, matrix products, shards(): upstream = jnp.dot(cotangent, weights, preferred_element_type=f32)  15.7 us
    dynamic_update_slice x4, other arithmetic, put(): lax.dynamic_update_slice_in_dim(self.result, jnp.where(valid, piece, self...  15 us
  transfers between devices with their start and end apart: 29, of which 15 were waited for; matrix products, arithmetic and copies ran while one was open for 16% of the time, Pallas kernels for 20%

profile of v3, /device:TPU:0, one launch (start us, length us, event | category | flops | bytes accessed | tf_op | source)
XLA Modules:
  0.0 459.8 jit_solution(5067333502484429490)
XLA Ops:
  7.2 2.3 copy.54.refs_0_
  9.5 5.6 %split.1 = bf16[8,1,128,1024]{3,2,1,0:T(8,128)(2,1)} custom-call(bf16[1,128,8192]{2,1,0:T(8,128)(2,1)} %bitcast.47), custom_call_target="tpu_custom_call" | custom-call | tf_op jit(solution)/shard_map/split/pallas_call | solution.py:354
  15.1 5.2 %all-to-all-start = ((bf16[8,1,128,1024]{3,2,1,0:T(8,128)(2,1)}), bf16[8,1,128,1024]{3,2,1,0:T(8,128)(2,1)S(1)}, u32[]{:S(2)}, u32[]{:S(2)}) async-start(bf16[8,1,128,1024]{3,2,1,0:T(8,128)(2,1)} %split.1), calls=%async_computation | async-start | bytes 4194304 | tf_op jit(solution)/shard_map/all_to_all | solution.py:583
  22.8 7.9 %pack.1 = (bf16[8,288,1024]{2,1,0:T(8,128)(2,1)}, bf16[8,1,128,1024]{3,2,1,0:T(8,128)(2,1)}) custom-call(bf16[3,128,8192]{2,1,0:T(8,128)(2,1)} %x_ref.1, bf16[3,8,8192]{2,1,0:T(8,128)(2,1)} %copy-done.9), custom_call_target="tpu_custom_call" | custom-call | tf_op jit(solution)/shard_map/pack/pallas_call | solution.py:354
  30.7 16.2 %all-to-all-done = bf16[8,1,128,1024]{3,2,1,0:T(8,128)(2,1)S(1)} async-done(((bf16[8,1,128,1024]{3,2,1,0:T(8,128)(2,1)}), bf16[8,1,128,1024]{3,2,1,0:T(8,128)(2,1)S(1)}, u32[]{:S(2)}, u32[]{:S(2)}) %all-to-all-start) | async-done | bytes 2097184 | tf_op jit(solution)/shard_map/all_to_all | solution.py:583
  47.0 1.3 copy-done.2
  48.3 4.7 %all-to-all-start.1 = ((bf16[8,288,1024]{2,1,0:T(8,128)(2,1)}), bf16[8,288,1024]{2,1,0:T(8,128)(2,1)}, u32[]{:S(2)}, u32[]{:S(2)}) async-start(bf16[8,288,1024]{2,1,0:T(8,128)(2,1)} %get-tuple-element.38), calls=%async_computation.1 | async-start | bytes 9437184 | tf_op jit(solution)/shard_map/all_to_all | solution.py:586
  53.1 7.8 %collective-permute-start.4 = (bf16[1024,1024]{1,0:T(8,128)(2,1)S(1)}, bf16[1024,1024]{1,0:T(8,128)(2,1)S(1)}, u32[]{:S(2)}, u32[]{:S(2)}) collective-permute-start(bf16[1024,1024]{1,0:T(8,128)(2,1)S(1)} %bitcast.38), channel_id=1, source_target_pairs={{0,8},{8,16},{16,24},{1,9},{9,17},{17,25},{2,10},{10,18},{18,26},{... | collective-permute-start | bytes 6291464 | tf_op jit(solution)/shard_map/ppermute | solution.py:499
  60.9 1.3 collective-permute-start.5
  62.2 43.9 %collective-permute-done.4.refs_2_ = bf16[1024,1024]{1,0:T(8,128)(2,1)S(1)} collective-permute-done((bf16[1024,1024]{1,0:T(8,128)(2,1)S(1)}, bf16[1024,1024]{1,0:T(8,128)(2,1)S(1)}, u32[]{:S(2)}, u32[]{:S(2)}) %collective-permute-start.4) | collective-permute-done | bytes 2097184 | tf_op jit(solution)/shard_map/ppermute | solution.py:499
  106.2 1.4 copy-done.7
  107.5 3.0 collective-permute-done.5.refs_3_
  110.5 2.0 collective-permute-start.6
  112.5 1.3 collective-permute-start.7
  115.1 4.4 all-to-all-start.2
  122.8 1.3 dynamic-slice_bitcast_fusion.skip_ref
  124.1 15.2 %smooth.1 = (f32[2,8192,128]{2,1,0:T(8,128)}, f32[8192,128]{1,0:T(8,128)}, f32[2,8192,128]{2,1,0:T(8,128)}, f32[16,8,128]{2,1,0:T(8,128)}, bf16[4096,1024]{1,0:T(8,128)(2,1)}) custom-call(bf16[8,288,1024]{2,1,0:T(8,128)(2,1)} %all-to-all-done.1.refs_1_.x_ref.rim_ref, bf16[8,288,1024]{2,1,0:T(8,128)(2,1)} %all-to-all-done.1.refs_1_.x_ref.rim_ref, ...), custom_call_target="tpu_custom_call" | custom-call | tf_op jit(solution)/shard_map/smooth/pallas_call | solution.py:354
  139.3 8.5 %collective-permute-start.1 = (f32[16,8,128]{2,1,0:T(8,128)}, f32[16,8,128]{2,1,0:T(8,128)S(1)}, u32[]{:S(2)}, u32[]{:S(2)}) collective-permute-start(f32[16,8,128]{2,1,0:T(8,128)} %get-tuple-element.40), channel_id=1, source_target_pairs={{0,8},{8,16},{16,24},{1,9},{9,17},{17,25},{2,10},{10,18},{18,26},{... | collective-permute-start | bytes 196616 | tf_op jit(solution)/shard_map/ppermute | solution.py:645
  147.8 4.7 %collective-permute-start.2 = (f32[16,8,128]{2,1,0:T(8,128)}, f32[16,8,128]{2,1,0:T(8,128)S(1)}, u32[]{:S(2)}, u32[]{:S(2)}) collective-permute-start(f32[16,8,128]{2,1,0:T(8,128)} %get-tuple-element.40), channel_id=1, source_target_pairs={{0,16},{8,24},{1,17},{9,25},{2,18},{10,26},{3,19},{11,27},{4,20},{... | collective-permute-start | bytes 196616 | tf_op jit(solution)/shard_map/ppermute | solution.py:645
  152.5 1.3 collective-permute-start.3
  153.8 1.5 constant_dynamic-update-slice_fusion
  155.3 2.3 select_dynamic-update-slice_fusion.3
  157.6 3.9 select_dynamic-update-slice_fusion.2
  162.2 1.6 collective-permute-done.7.refs_1_
  163.7 2.0 collective-permute-start.8
  165.7 1.5 collective-permute-start.9
  167.2 4.4 select_dynamic-update-slice_fusion.1
  171.6 18.3 %field.1 = (f32[8192,128]{1,0:T(8,128)}, f32[8192,128]{1,0:T(8,128)}, f32[8192,128]{1,0:T(8,128)}, bf16[1024,1024]{1,0:T(8,128)(2,1)}) custom-call(bf16[8,1,128,1024]{3,2,1,0:T(8,128)(2,1)} %all-to-all-done.2.x_ref, bf16[8,288,1024]{2,1,0:T(8,128)(2,1)} %all-to-all-done.1.refs_1_.x_ref.rim_ref, f32[3,7,8,128]{3,2,1,0:T(8,128)} %reshape_reshape.7.taps_ref, ...), custom_call_target="tpu_custom_call" | custom-call | tf_op jit(solution)/shard_map/field/pallas_call | solution.py:354
  189.9 12.9 %convolution_convert_fusion = bf16[4096,1024]{1,0:T(8,128)(2,1)S(1)} fusion(bf16[1024,4096]{1,0:T(8,128)(2,1)} %all-gather.2.cloned.1.call-done, bf16[1024,1024]{1,0:T(8,128)(2,1)} %get-tuple-element.41.x_ref), kind=kOutput, calls=%fused_computation | convolution fusion | flops 8594128896 | bytes 18874368 | tf_op jit(solution)/shard_map/dot_general | solution.py:680
  202.9 2.8 constant_dynamic-slice_fusion
  205.7 1.8 copy-done.4
  207.5 6.4 %collective-permute-done.9.refs_1_ = bf16[1024,1024]{1,0:T(8,128)(2,1)} collective-permute-done((bf16[1024,1024]{1,0:T(8,128)(2,1)}, bf16[1024,1024]{1,0:T(8,128)(2,1)}, u32[]{:S(2)}, u32[]{:S(2)}) %collective-permute-start.9) | collective-permute-done | bytes 2097184 | tf_op jit(solution)/shard_map/ppermute | solution.py:500
  213.9 4.4 select_dynamic-update-slice_fusion.w_ref
  218.3 14.5 %project.1.hold_ref = bf16[1024,4096]{1,0:T(8,128)(2,1)} custom-call(bf16[1024,1024]{1,0:T(8,128)(2,1)} %get-tuple-element.41.x_ref, bf16[4096,1024]{1,0:T(8,128)(2,1)} %select_dynamic-update-slice_fusion.w_ref), custom_call_target="tpu_custom_call" | custom-call | tf_op jit(solution)/shard_map/project/pallas_call | solution.py:354
  232.8 1.6 collective-permute-start.10
  234.5 2.0 collective-permute-start.11
  236.5 15.7 %fusion.4.up_ref = f32[1024,1024]{1,0:T(8,128)} fusion(bf16[1024,4096]{1,0:T(8,128)(2,1)} %all-gather.2.cloned.1.call-done, bf16[4096,1024]{1,0:T(8,128)(2,1)} %select_dynamic-update-slice_fusion.w_ref), kind=kOutput, calls=%fused_computation.35 | convolution fusion | flops 8589934592 | bytes 20971520 | tf_op jit(solution)/shard_map/dot_general | solution.py:689
  252.2 13.7 %cotangent.1 = (f32[8192,128]{1,0:T(8,128)}, f32[8192,128]{1,0:T(8,128)}, f32[384,128]{1,0:T(8,128)}, f32[16,8,128]{2,1,0:T(8,128)}, f32[8,128]{1,0:T(8,128)}) custom-call(f32[1024,1024]{1,0:T(8,128)} %fusion.4.up_ref, f32[8192,128]{1,0:T(8,128)} %get-tuple-element.47.sm_ref, f32[8192,128]{1,0:T(8,128)} %get-tuple-element.39.mixed_ref, ...), custom_call_target="tpu_custom_call" | custom-call | tf_op jit(solution)/shard_map/cotangent/pallas_call | solution.py:354
  266.0 11.3 %collective-permute-done.10.refs_2_.refs_0_ = bf16[1024,1024]{1,0:T(8,128)(2,1)S(1)} collective-permute-done((bf16[1024,1024]{1,0:T(8,128)(2,1)}, bf16[1024,1024]{1,0:T(8,128)(2,1)S(1)}, u32[]{:S(2)}, u32[]{:S(2)}) %collective-permute-start.10) | collective-permute-done | bytes 2097184 | tf_op jit(solution)/shard_map/ppermute | solution.py:546
  277.3 1.3 copy-done.5
  278.6 1.3 collective-permute-start.12
  279.9 1.3 collective-permute-start.13
  281.2 1.3 collective-permute-start.14
  282.9 4.6 %collective-permute-done.12 = f32[384,128]{1,0:T(8,128)S(1)} collective-permute-done((f32[384,128]{1,0:T(8,128)}, f32[384,128]{1,0:T(8,128)S(1)}, u32[]{:S(2)}, u32[]{:S(2)}) %collective-permute-start.12) | collective-permute-done | bytes 196640 | tf_op jit(solution)/shard_map/ppermute | solution.py:645
  288.2 2.1 collective-permute-done.13
  291.6 6.9 %add_convert_fusion.3 = (bf16[1024,1024]{1,0:T(8,128)(2,1)S(1)}, bf16[1024,1024]{1,0:T(8,128)(2,1)}) fusion(bf16[1024,1024]{1,0:T(8,128)(2,1)} %get-tuple-element.60, bf16[4096,1024]{1,0:T(8,128)(2,1)} %copy-done.4, s32[]{:T(128)S(6)} %select_n.134, bf16[1024,1024]{1,0:T(8,128)(2,1)} %get-tuple-element.59, s32[]{:T(128)S(6)} %select_n.133), kind=kLoop, calls=%fused_computation.4 | loop fusion | flops 8388608 | bytes 12582920 | tf_op jit(solution)/shard_map/convert_element_type | solution.py:545
  298.6 3.2 collective-permute-start.15
  301.8 2.0 collective-permute-start.16
  303.8 30.5 %back.1 = (bf16[8,3,128,1024]{3,2,1,0:T(8,128)(2,1)}, f32[3,7,8,128]{3,2,1,0:T(8,128)}) custom-call(f32[8192,128]{1,0:T(8,128)} %get-tuple-element.50.grad_ref, f32[8192,128]{1,0:T(8,128)} %get-tuple-element.51.zero_ref, f32[2,8192,128]{2,1,0:T(8,128)} %get-tuple-element.49.heads_ref.sm_ref, f32[8192,128]{1,0:T(8,128)} %get-tuple-element.52.first_ref, ...), custom_call_target="tpu_custom_call" | custom-call | tf_op jit(solution)/shard_map/back/pallas_call | solution.py:354
  334.3 6.0 %all-to-all-start.3 = ((bf16[8,3,128,1024]{3,2,1,0:T(8,128)(2,1)}), bf16[8,3,128,1024]{3,2,1,0:T(8,128)(2,1)}, u32[]{:S(2)}, u32[]{:S(2)}) async-start(bf16[8,3,128,1024]{3,2,1,0:T(8,128)(2,1)} %get-tuple-element.58), calls=%async_computation.4 | async-start | bytes 12582912 | tf_op jit(solution)/shard_map/all_to_all | solution.py:759
  340.3 1.5 collective-permute-done.15.refs_0_
  341.8 6.9 %add_convert_fusion.2 = (bf16[1024,1024]{1,0:T(8,128)(2,1)S(1)}, bf16[1024,1024]{1,0:T(8,128)(2,1)}) fusion(bf16[1024,1024]{1,0:T(8,128)(2,1)} %get-tuple-element.62, bf16[4096,1024]{1,0:T(8,128)(2,1)} %copy-done.4, s32[]{:T(128)S(6)} %select_n.132, bf16[1024,1024]{1,0:T(8,128)(2,1)} %get-tuple-element.63, s32[]{:T(128)S(6)} %select_n.135), kind=kLoop, calls=%fused_computation.3 | loop fusion | flops 8388608 | bytes 12582920 | tf_op jit(solution)/shard_map/convert_element_type | solution.py:544
  348.7 1.3 collective-permute-start.18
  350.0 7.1 %collective-permute-start.17 = (bf16[1024,1024]{1,0:T(8,128)(2,1)S(1)}, bf16[1024,1024]{1,0:T(8,128)(2,1)}, u32[]{:S(2)}, u32[]{:S(2)}) collective-permute-start(bf16[1024,1024]{1,0:T(8,128)(2,1)S(1)} %get-tuple-element.67), channel_id=1, source_target_pairs={{0,8},{8,16},{16,24},{1,9},{9,17},{17,25},{2,10},{10,18},{18,26},{... | collective-permute-start | bytes 6291464 | tf_op jit(solution)/shard_map/ppermute | solution.py:546
  358.1 1.7 collective-permute-start.20
  359.8 1.5 collective-permute-start.19
  361.3 38.5 %collective-permute-done.21 = f32[8,1024]{1,0:T(8,128)S(1)} collective-permute-done((f32[8,1024]{1,0:T(8,128)S(1)}, f32[8,1024]{1,0:T(8,128)S(1)}, u32[]{:S(2)}, u32[]{:S(2)}) %collective-permute-start.21) | collective-permute-done | bytes 32800 | tf_op jit(solution)/shard_map/ppermute | solution.py:767
  400.5 4.3 add_convert_fusion
  404.9 1.6 maximum_bitcast_fusion.refs_0_
  406.5 5.4 %all-to-all-done.3.refs_0_ = bf16[8,3,128,1024]{3,2,1,0:T(8,128)(2,1)} async-done(((bf16[8,3,128,1024]{3,2,1,0:T(8,128)(2,1)}), bf16[8,3,128,1024]{3,2,1,0:T(8,128)(2,1)}, u32[]{:S(2)}, u32[]{:S(2)}) %all-to-all-start.3) | async-done | bytes 6291488 | tf_op jit(solution)/shard_map/all_to_all | solution.py:759
  412.0 3.6 all-to-all-start.4
  415.6 7.8 %join.2 = bf16[3,128,8192]{2,1,0:T(8,128)(2,1)} custom-call(bf16[8,3,128,1024]{3,2,1,0:T(8,128)(2,1)} %all-to-all-done.3.refs_0_), custom_call_target="tpu_custom_call" | custom-call | tf_op jit(solution)/shard_map/join/pallas_call | solution.py:354
  423.4 21.6 %all-to-all-done.4.refs_0_ = bf16[8,1,144,1024]{3,2,1,0:T(8,128)(2,1)S(1)} async-done(((bf16[8,1,144,1024]{3,2,1,0:T(8,128)(2,1)}), bf16[8,1,144,1024]{3,2,1,0:T(8,128)(2,1)S(1)}, u32[]{:S(2)}, u32[]{:S(2)}) %all-to-all-start.4) | async-done | bytes 2359328 | tf_op jit(solution)/shard_map/all_to_all | solution.py:779
  447.0 6.0 %join.3 = f32[1,128,8192]{2,1,0:T(8,128)} custom-call(bf16[8,1,144,1024]{3,2,1,0:T(8,128)(2,1)} %copy-done.6), custom_call_target="tpu_custom_call" | custom-call | tf_op jit(solution)/shard_map/join/pallas_call | solution.py:354
  (85 shorter events, 13.7 us)
Async XLA Ops:
  7.2 106.7 %copy-start = (f32[3,7,512]{2,1,0:T(8,128)S(1)}, f32[3,7,512]{2,1,0:T(8,128)}, u32[]{:S(2)}) copy-start(f32[3,7,512]{2,1,0:T(8,128)} %param.8) | copy-start | bytes 129028
  15.1 31.8 %all-to-all-start = ((bf16[8,1,128,1024]{3,2,1,0:T(8,128)(2,1)}), bf16[8,1,128,1024]{3,2,1,0:T(8,128)(2,1)S(1)}, u32[]{:S(2)}, u32[]{:S(2)}) async-start(bf16[8,1,128,1024]{3,2,1,0:T(8,128)(2,1)} %split.1), calls=%async_computation | async-start | bytes 4194304 | tf_op jit(solution)/shard_map/all_to_all | solution.py:583
  21.3 0.7 collective-permute-start
  22.0 0.8 copy-start.9
  46.9 1.3 copy-start.2
  48.3 4.8 %copy-start.3 = (bf16[8,1,128,1024]{3,2,1,0:T(8,128)(2,1)S(1)}, bf16[8,1,128,1024]{3,2,1,0:T(8,128)(2,1)}, u32[]{:S(2)}) copy-start(bf16[8,1,128,1024]{3,2,1,0:T(8,128)(2,1)} %copy-done.2) | copy-start | bytes 6291460
  48.3 62.2 %all-to-all-start.1 = ((bf16[8,288,1024]{2,1,0:T(8,128)(2,1)}), bf16[8,288,1024]{2,1,0:T(8,128)(2,1)}, u32[]{:S(2)}, u32[]{:S(2)}) async-start(bf16[8,288,1024]{2,1,0:T(8,128)(2,1)} %get-tuple-element.38), calls=%async_computation.1 | async-start | bytes 9437184 | tf_op jit(solution)/shard_map/all_to_all | solution.py:586
  53.0 136.9 %all-gather.2.cloned.1.call-start = ((), (), s32[]{:S(2)}) async-start(), calls=%async_computation.6 | async-start | bytes 9437184 | tf_op jit(solution)/shard_map/all_gather | solution.py:617
  53.1 53.1 %collective-permute-start.4 = (bf16[1024,1024]{1,0:T(8,128)(2,1)S(1)}, bf16[1024,1024]{1,0:T(8,128)(2,1)S(1)}, u32[]{:S(2)}, u32[]{:S(2)}) collective-permute-start(bf16[1024,1024]{1,0:T(8,128)(2,1)S(1)} %bitcast.38), channel_id=1, source_target_pairs={{0,8},{8,16},{16,24},{1,9},{9,17},{17,25},{2,10},{10,18},{18,26},{... | collective-permute-start | bytes 6291464 | tf_op jit(solution)/shard_map/ppermute | solution.py:499
  60.9 49.6 %collective-permute-start.5 = (bf16[1024,1024]{1,0:T(8,128)(2,1)S(1)}, bf16[1024,1024]{1,0:T(8,128)(2,1)}, u32[]{:S(2)}, u32[]{:S(2)}) collective-permute-start(bf16[1024,1024]{1,0:T(8,128)(2,1)S(1)} %bitcast.39), channel_id=1, source_target_pairs={{8,0},{16,8},{24,16},{9,1},{17,9},{25,17},{10,2},{18,10},{26,18},{... | collective-permute-start | bytes 6291464 | tf_op jit(solution)/shard_map/ppermute | solution.py:500
  106.2 1.4 copy-start.7
  110.5 51.6 %collective-permute-start.6 = (bf16[1024,1024]{1,0:T(8,128)(2,1)}, bf16[1024,1024]{1,0:T(8,128)(2,1)}, u32[]{:S(2)}, u32[]{:S(2)}) collective-permute-start(bf16[1024,1024]{1,0:T(8,128)(2,1)} %copy-done.7), channel_id=1, source_target_pairs={{8,16},{16,24},{9,17},{17,25},{10,18},{18,26},{11,19},{19,27},{12,... | collective-permute-start | bytes 6291464 | tf_op jit(solution)/shard_map/ppermute | solution.py:499
  112.5 51.2 %collective-permute-start.7 = (bf16[1024,1024]{1,0:T(8,128)(2,1)}, bf16[1024,1024]{1,0:T(8,128)(2,1)}, u32[]{:S(2)}, u32[]{:S(2)}) collective-permute-start(bf16[1024,1024]{1,0:T(8,128)(2,1)} %collective-permute-done.5.refs_3_), channel_id=1, source_target_pairs={{8,0},{16,8},{9,1},{17,9},{10,2},{18,10},{11,3},{19,11},{12,4},{20... | collective-permute-start | bytes 6291464 | tf_op jit(solution)/shard_map/ppermute | solution.py:500
  115.1 56.5 %all-to-all-start.2 = ((bf16[8,1,128,1024]{3,2,1,0:T(8,128)(2,1)}), bf16[8,1,128,1024]{3,2,1,0:T(8,128)(2,1)}, u32[]{:S(2)}, u32[]{:S(2)}) async-start(bf16[8,1,128,1024]{3,2,1,0:T(8,128)(2,1)} %tie.10), calls=%async_computation.2 | async-start | bytes 4194304 | tf_op jit(solution)/shard_map/all_to_all | solution.py:588
  119.5 287.0 %reduce-scatter.2.cloned.1.call-start = ((), (), s32[]{:S(2)}) async-start(), calls=%async_computation.7 | async-start | bytes 9437184 | tf_op jit(solution)/shard_map/reduce_scatter | solution.py:691
  139.3 16.0 %copy-start.8 = (bf16[1024,1024]{1,0:T(8,128)(2,1)S(1)}, bf16[1024,1024]{1,0:T(8,128)(2,1)}, u32[]{:S(2)}) copy-start(bf16[1024,1024]{1,0:T(8,128)(2,1)} %copy-done.7) | copy-start | bytes 6291460
  139.3 22.2 %collective-permute-start.1 = (f32[16,8,128]{2,1,0:T(8,128)}, f32[16,8,128]{2,1,0:T(8,128)S(1)}, u32[]{:S(2)}, u32[]{:S(2)}) collective-permute-start(f32[16,8,128]{2,1,0:T(8,128)} %get-tuple-element.40), channel_id=1, source_target_pairs={{0,8},{8,16},{16,24},{1,9},{9,17},{17,25},{2,10},{10,18},{18,26},{... | collective-permute-start | bytes 196616 | tf_op jit(solution)/shard_map/ppermute | solution.py:645
  147.8 13.7 %collective-permute-start.2 = (f32[16,8,128]{2,1,0:T(8,128)}, f32[16,8,128]{2,1,0:T(8,128)S(1)}, u32[]{:S(2)}, u32[]{:S(2)}) collective-permute-start(f32[16,8,128]{2,1,0:T(8,128)} %get-tuple-element.40), channel_id=1, source_target_pairs={{0,16},{8,24},{1,17},{9,25},{2,18},{10,26},{3,19},{11,27},{4,20},{... | collective-permute-start | bytes 196616 | tf_op jit(solution)/shard_map/ppermute | solution.py:645
  152.5 9.1 %collective-permute-start.3 = (f32[16,8,128]{2,1,0:T(8,128)}, f32[16,8,128]{2,1,0:T(8,128)S(1)}, u32[]{:S(2)}, u32[]{:S(2)}) collective-permute-start(f32[16,8,128]{2,1,0:T(8,128)} %get-tuple-element.40), channel_id=1, source_target_pairs={{0,24},{1,25},{2,26},{3,27},{4,28},{5,29},{6,30},{7,31}} | collective-permute-start | bytes 196616 | tf_op jit(solution)/shard_map/ppermute | solution.py:645
  163.7 43.8 %collective-permute-start.8 = (bf16[1024,1024]{1,0:T(8,128)(2,1)}, bf16[1024,1024]{1,0:T(8,128)(2,1)}, u32[]{:S(2)}, u32[]{:S(2)}) collective-permute-start(bf16[1024,1024]{1,0:T(8,128)(2,1)} %get-tuple-element.43), channel_id=1, source_target_pairs={{16,24},{17,25},{18,26},{19,27},{20,28},{21,29},{22,30},{23,31}} | collective-permute-start | bytes 6291464 | tf_op jit(solution)/shard_map/ppermute | solution.py:499
  165.7 48.2 %collective-permute-start.9 = (bf16[1024,1024]{1,0:T(8,128)(2,1)}, bf16[1024,1024]{1,0:T(8,128)(2,1)}, u32[]{:S(2)}, u32[]{:S(2)}) collective-permute-start(bf16[1024,1024]{1,0:T(8,128)(2,1)} %get-tuple-element.44), channel_id=1, source_target_pairs={{8,0},{9,1},{10,2},{11,3},{12,4},{13,5},{14,6},{15,7}} | collective-permute-start | bytes 6291464 | tf_op jit(solution)/shard_map/ppermute | solution.py:500
  202.9 4.6 %copy-start.4 = (bf16[4096,1024]{1,0:T(8,128)(2,1)}, bf16[4096,1024]{1,0:T(8,128)(2,1)S(1)}, u32[]{:S(2)}) copy-start(bf16[4096,1024]{1,0:T(8,128)(2,1)S(1)} %convolution_convert_fusion) | copy-start | bytes 25165828
  232.8 44.5 %collective-permute-start.10 = (bf16[1024,1024]{1,0:T(8,128)(2,1)}, bf16[1024,1024]{1,0:T(8,128)(2,1)S(1)}, u32[]{:S(2)}, u32[]{:S(2)}) collective-permute-start(bf16[1024,1024]{1,0:T(8,128)(2,1)} %get-tuple-element.72.refs_2_), channel_id=1, source_target_pairs={{0,8},{1,9},{2,10},{3,11},{4,12},{5,13},{6,14},{7,15}} | collective-permute-start | bytes 6291464 | tf_op jit(solution)/shard_map/ppermute | solution.py:546
  234.5 42.8 %collective-permute-start.11 = (bf16[1024,1024]{1,0:T(8,128)(2,1)}, bf16[1024,1024]{1,0:T(8,128)(2,1)}, u32[]{:S(2)}, u32[]{:S(2)}) collective-permute-start(bf16[1024,1024]{1,0:T(8,128)(2,1)} %get-tuple-element.71.refs_3_), channel_id=1, source_target_pairs={{24,16},{25,17},{26,18},{27,19},{28,20},{29,21},{30,22},{31,23}} | collective-permute-start | bytes 6291464 | tf_op jit(solution)/shard_map/ppermute | solution.py:547
  277.3 1.3 copy-start.5
  278.6 8.9 %collective-permute-start.12 = (f32[384,128]{1,0:T(8,128)}, f32[384,128]{1,0:T(8,128)S(1)}, u32[]{:S(2)}, u32[]{:S(2)}) collective-permute-start(f32[384,128]{1,0:T(8,128)} %get-tuple-element.56), channel_id=1, source_target_pairs={{8,0},{16,8},{24,16},{9,1},{17,9},{25,17},{10,2},{18,10},{26,18},{... | collective-permute-start | bytes 589832 | tf_op jit(solution)/shard_map/ppermute | solution.py:645
  279.9 10.4 %collective-permute-start.13 = (f32[16,8,128]{2,1,0:T(8,128)}, f32[16,8,128]{2,1,0:T(8,128)S(1)}, u32[]{:S(2)}, u32[]{:S(2)}) collective-permute-start(f32[16,8,128]{2,1,0:T(8,128)} %get-tuple-element.57), channel_id=1, source_target_pairs={{16,0},{24,8},{17,1},{25,9},{18,2},{26,10},{19,3},{27,11},{20,4},{... | collective-permute-start | bytes 196616 | tf_op jit(solution)/shard_map/ppermute | solution.py:645
  281.2 9.8 %collective-permute-start.14 = (f32[16,8,128]{2,1,0:T(8,128)}, f32[16,8,128]{2,1,0:T(8,128)S(1)}, u32[]{:S(2)}, u32[]{:S(2)}) collective-permute-start(f32[16,8,128]{2,1,0:T(8,128)} %get-tuple-element.57), channel_id=1, source_target_pairs={{24,0},{25,1},{26,2},{27,3},{28,4},{29,5},{30,6},{31,7}} | collective-permute-start | bytes 196616 | tf_op jit(solution)/shard_map/ppermute | solution.py:645
  298.6 43.2 %collective-permute-start.15 = (bf16[1024,1024]{1,0:T(8,128)(2,1)}, bf16[1024,1024]{1,0:T(8,128)(2,1)}, u32[]{:S(2)}, u32[]{:S(2)}) collective-permute-start(bf16[1024,1024]{1,0:T(8,128)(2,1)} %get-tuple-element.70), channel_id=1, source_target_pairs={{0,8},{8,16},{1,9},{9,17},{2,10},{10,18},{3,11},{11,19},{4,12},{12... | collective-permute-start | bytes 6291464 | tf_op jit(solution)/shard_map/ppermute | solution.py:546
  301.8 40.0 %collective-permute-start.16 = (bf16[1024,1024]{1,0:T(8,128)(2,1)S(1)}, bf16[1024,1024]{1,0:T(8,128)(2,1)}, u32[]{:S(2)}, u32[]{:S(2)}) collective-permute-start(bf16[1024,1024]{1,0:T(8,128)(2,1)S(1)} %get-tuple-element.69), channel_id=1, source_target_pairs={{24,16},{16,8},{25,17},{17,9},{26,18},{18,10},{27,19},{19,11},{28,... | collective-permute-start | bytes 6291464 | tf_op jit(solution)/shard_map/ppermute | solution.py:547
  334.3 77.6 %all-to-all-start.3 = ((bf16[8,3,128,1024]{3,2,1,0:T(8,128)(2,1)}), bf16[8,3,128,1024]{3,2,1,0:T(8,128)(2,1)}, u32[]{:S(2)}, u32[]{:S(2)}) async-start(bf16[8,3,128,1024]{3,2,1,0:T(8,128)(2,1)} %get-tuple-element.58), calls=%async_computation.4 | async-start | bytes 12582912 | tf_op jit(solution)/shard_map/all_to_all | solution.py:759
  341.8 15.3 %copy-start.10 = (f32[3,7,8,128]{3,2,1,0:T(8,128)S(1)}, f32[3,7,8,128]{3,2,1,0:T(8,128)}, u32[]{:S(2)}) copy-start(f32[3,7,8,128]{3,2,1,0:T(8,128)} %get-tuple-element.61.refs_2_) | copy-start | bytes 258052
  341.8 15.8 %copy-start.11 = (f32[8,128]{1,0:T(8,128)S(1)}, f32[8,128]{1,0:T(8,128)}, u32[]{:S(2)}) copy-start(f32[8,128]{1,0:T(8,128)} %get-tuple-element.64) | copy-start | bytes 12292
  348.7 51.8 %collective-permute-start.18 = (bf16[1024,1024]{1,0:T(8,128)(2,1)}, bf16[1024,1024]{1,0:T(8,128)(2,1)}, u32[]{:S(2)}, u32[]{:S(2)}) collective-permute-start(bf16[1024,1024]{1,0:T(8,128)(2,1)} %get-tuple-element.68), channel_id=1, source_target_pairs={{24,16},{16,8},{8,0},{25,17},{17,9},{9,1},{26,18},{18,10},{10,2},{... | collective-permute-start | bytes 6291464 | tf_op jit(solution)/shard_map/ppermute | solution.py:547
  350.0 50.5 %collective-permute-start.17 = (bf16[1024,1024]{1,0:T(8,128)(2,1)S(1)}, bf16[1024,1024]{1,0:T(8,128)(2,1)}, u32[]{:S(2)}, u32[]{:S(2)}) collective-permute-start(bf16[1024,1024]{1,0:T(8,128)(2,1)S(1)} %get-tuple-element.67), channel_id=1, source_target_pairs={{0,8},{8,16},{16,24},{1,9},{9,17},{17,25},{2,10},{10,18},{18,26},{... | collective-permute-start | bytes 6291464 | tf_op jit(solution)/shard_map/ppermute | solution.py:546
  357.6 42.1 %collective-permute-start.21 = (f32[8,1024]{1,0:T(8,128)S(1)}, f32[8,1024]{1,0:T(8,128)S(1)}, u32[]{:S(2)}, u32[]{:S(2)}) collective-permute-start(f32[8,1024]{1,0:T(8,128)S(1)} %pad.9), channel_id=1, source_target_pairs={{0,24},{8,0},{16,8},{24,16},{1,25},{9,1},{17,9},{25,17},{2,26},{10... | collective-permute-start | bytes 98312 | tf_op jit(solution)/shard_map/ppermute | solution.py:767
  358.1 42.0 %collective-permute-start.20 = (f32[8,1024]{1,0:T(8,128)S(1)}, f32[8,1024]{1,0:T(8,128)S(1)}, u32[]{:S(2)}, u32[]{:S(2)}) collective-permute-start(f32[8,1024]{1,0:T(8,128)S(1)} %pad.9), channel_id=1, source_target_pairs={{0,16},{8,24},{16,0},{24,8},{1,17},{9,25},{17,1},{25,9},{2,18},{10... | collective-permute-start | bytes 98312 | tf_op jit(solution)/shard_map/ppermute | solution.py:767
  359.8 40.6 %collective-permute-start.19 = (f32[8,1024]{1,0:T(8,128)S(1)}, f32[8,1024]{1,0:T(8,128)S(1)}, u32[]{:S(2)}, u32[]{:S(2)}) collective-permute-start(f32[8,1024]{1,0:T(8,128)S(1)} %pad.9), channel_id=1, source_target_pairs={{0,8},{8,16},{16,24},{24,0},{1,9},{9,17},{17,25},{25,1},{2,10},{10... | collective-permute-start | bytes 98312 | tf_op jit(solution)/shard_map/ppermute | solution.py:767
  412.0 33.0 %all-to-all-start.4 = ((bf16[8,1,144,1024]{3,2,1,0:T(8,128)(2,1)}), bf16[8,1,144,1024]{3,2,1,0:T(8,128)(2,1)S(1)}, u32[]{:S(2)}, u32[]{:S(2)}) async-start(bf16[8,1,144,1024]{3,2,1,0:T(8,128)(2,1)} %tie.17), calls=%async_computation.5 | async-start | bytes 4718592 | tf_op jit(solution)/shard_map/all_to_all | solution.py:779
  445.0 2.0 copy-start.6
  446.4 6.6 %copy-start.1 = (f32[3,7,512]{2,1,0:T(8,128)S(1)}, f32[3,7,512]{2,1,0:T(8,128)}, u32[]{:S(2)}) copy-start(f32[3,7,512]{2,1,0:T(8,128)} %param.8) | copy-start | bytes 129028
Sparse Core Ops, SparseCore 0:
  110.7 76.2 all-gather.1
  232.9 73.2 reduce-scatter.1

commit v4 on v3

--- a/solution.py
+++ b/solution.py
@@ -688,8 +688,6 @@
 
     upstream = jnp.dot(cotangent, weights, preferred_element_type=f32)
     partial_out = project(gated, weights)
-    output = lax.psum_scatter(partial_out, "lo", scatter_dimension=0, tiled=True)
-    output = lax.psum_scatter(output, "tp", scatter_dimension=1, tiled=True)
     edge = EDGE * rows
     held = modes * rows + 4 * edge
     grad_field, grad_zero, ahead, back_end, grad_skip = call(
@@ -718,6 +716,9 @@
         0,
     )
 
+    (partial_out,) = tie((partial_out,), (back_end,))
+    output = lax.psum_scatter(partial_out, "lo", scatter_dimension=0, tiled=True)
+    output = lax.psum_scatter(output, "tp", scatter_dimension=1, tiled=True)
     ahead, back_end = tie((ahead, back_end), (sums.right, sums.left))
     ahead = from_plane(ahead, 1)
     beyond = jnp.zeros_like(back_end)

time: 462 us -> 490 us (1.061)
  waiting for transfers between devices: 158 us -> 187 us
    ppermute x3, waiting for transfers between devices: 12.8 us -> 42.3 us  [step(): lax.ppermute(self.to_right, 'hi', [(z, z + 1) for z in range(s)])]
  transfers between devices with their start and end apart: 29 -> 29, of which waited for: 15 -> 15; matrix products, arithmetic and copies ran while one was open for 16% -> 12% of each run, Pallas kernels for 20% -> 16%
where the time goes in v4:
time: 490 us; the launch traced here: 488 us
  waiting for transfers between devices  187 us (38%)
  Pallas kernels  119 us (24%)
  starting transfers between devices  79.9 us (16%)
  other arithmetic  37.3 us (8%)
  matrix products  27.9 us (6%)
  local copies, waits for them, and re-layouts  22.3 us (5%)
  between operations  14.5 us (3%)
    pallas_call x9, Pallas kernels, call(): pl.pallas_call(kernel, grid=(blocks,), in_specs=in_specs, out_specs=out_s...  119 us
    ppermute x3, waiting for transfers between devices, step(): lax.ppermute(self.right, 'hi', [(z, z + 1) for z in range(k - 1, hi - 1)])  43.9 us
    ppermute x3, waiting for transfers between devices, step(): lax.ppermute(self.to_right, 'hi', [(z, z + 1) for z in range(s)])  42.3 us
    ppermute x3, waiting for transfers between devices, shards(): lax.ppermute(part, 'hi', [(z, (z + k) % hi) for z in range(hi)])  39.3 us
    all_to_all x1, waiting for transfers between devices, shards(): reduced = lax.all_to_all(reduced, 'lo', 0, 0, tiled=True)  21.6 us
    ppermute x6, starting transfers between devices, from_plane(): return lax.ppermute(a, 'hi', pairs)  18.6 us
    all_to_all x1, waiting for transfers between devices, shards(): lax.all_to_all(split_channels(out_weight[None], lo, 0, 1), 'lo', 0, 0, ti...  16.2 us
    dynamic_update_slice x4, other arithmetic, put(): lax.dynamic_update_slice_in_dim(self.result, jnp.where(valid, piece, self...  15 us
  transfers between devices with their start and end apart: 29, of which 15 were waited for; matrix products, arithmetic and copies ran while one was open for 12% of the time, Pallas kernels for 16%

profile of v4, /device:TPU:0, one launch (start us, length us, event | category | flops | bytes accessed | tf_op | source)
XLA Modules:
  0.0 488.3 jit_solution(15841437582259252309)
XLA Ops:
  7.2 2.3 copy.56.refs_0_
  9.5 5.6 %split.1 = bf16[8,1,128,1024]{3,2,1,0:T(8,128)(2,1)} custom-call(bf16[1,128,8192]{2,1,0:T(8,128)(2,1)} %bitcast.47), custom_call_target="tpu_custom_call" | custom-call | tf_op jit(solution)/shard_map/split/pallas_call | solution.py:354
  15.1 5.2 %all-to-all-start = ((bf16[8,1,128,1024]{3,2,1,0:T(8,128)(2,1)}), bf16[8,1,128,1024]{3,2,1,0:T(8,128)(2,1)S(1)}, u32[]{:S(2)}, u32[]{:S(2)}) async-start(bf16[8,1,128,1024]{3,2,1,0:T(8,128)(2,1)} %split.1), calls=%async_computation | async-start | bytes 4194304 | tf_op jit(solution)/shard_map/all_to_all | solution.py:583
  22.8 7.9 %pack.1 = (bf16[8,288,1024]{2,1,0:T(8,128)(2,1)}, bf16[8,1,128,1024]{3,2,1,0:T(8,128)(2,1)}) custom-call(bf16[3,128,8192]{2,1,0:T(8,128)(2,1)} %x_ref.1, bf16[3,8,8192]{2,1,0:T(8,128)(2,1)} %copy-done.9), custom_call_target="tpu_custom_call" | custom-call | tf_op jit(solution)/shard_map/pack/pallas_call | solution.py:354
  30.7 16.2 %all-to-all-done = bf16[8,1,128,1024]{3,2,1,0:T(8,128)(2,1)S(1)} async-done(((bf16[8,1,128,1024]{3,2,1,0:T(8,128)(2,1)}), bf16[8,1,128,1024]{3,2,1,0:T(8,128)(2,1)S(1)}, u32[]{:S(2)}, u32[]{:S(2)}) %all-to-all-start) | async-done | bytes 2097184 | tf_op jit(solution)/shard_map/all_to_all | solution.py:583
  47.0 1.3 copy-done.2
  48.3 4.8 all-to-all-start.1
  53.1 7.8 %collective-permute-start.4 = (bf16[1024,1024]{1,0:T(8,128)(2,1)S(1)}, bf16[1024,1024]{1,0:T(8,128)(2,1)S(1)}, u32[]{:S(2)}, u32[]{:S(2)}) collective-permute-start(bf16[1024,1024]{1,0:T(8,128)(2,1)S(1)} %bitcast.38), channel_id=1, source_target_pairs={{0,8},{8,16},{16,24},{1,9},{9,17},{17,25},{2,10},{10,18},{18,26},{... | collective-permute-start | bytes 6291464 | tf_op jit(solution)/shard_map/ppermute | solution.py:499
  61.0 1.3 collective-permute-start.5
  62.3 43.9 %collective-permute-done.4.refs_2_ = bf16[1024,1024]{1,0:T(8,128)(2,1)S(1)} collective-permute-done((bf16[1024,1024]{1,0:T(8,128)(2,1)S(1)}, bf16[1024,1024]{1,0:T(8,128)(2,1)S(1)}, u32[]{:S(2)}, u32[]{:S(2)}) %collective-permute-start.4) | collective-permute-done | bytes 2097184 | tf_op jit(solution)/shard_map/ppermute | solution.py:499
  106.2 1.3 copy-done.7
  107.5 3.0 collective-permute-done.5.refs_3_
  110.6 2.0 collective-permute-start.6
  112.5 1.3 collective-permute-start.7
  115.1 4.4 all-to-all-start.2
  122.7 1.3 dynamic-slice_bitcast_fusion.skip_ref
  124.0 15.2 %smooth.1 = (f32[2,8192,128]{2,1,0:T(8,128)}, f32[8192,128]{1,0:T(8,128)}, f32[2,8192,128]{2,1,0:T(8,128)}, f32[16,8,128]{2,1,0:T(8,128)}, bf16[4096,1024]{1,0:T(8,128)(2,1)}) custom-call(bf16[8,288,1024]{2,1,0:T(8,128)(2,1)} %all-to-all-done.1.refs_1_.x_ref.rim_ref, bf16[8,288,1024]{2,1,0:T(8,128)(2,1)} %all-to-all-done.1.refs_1_.x_ref.rim_ref, ...), custom_call_target="tpu_custom_call" | custom-call | tf_op jit(solution)/shard_map/smooth/pallas_call | solution.py:354
  139.2 8.5 %collective-permute-start.1 = (f32[16,8,128]{2,1,0:T(8,128)}, f32[16,8,128]{2,1,0:T(8,128)S(1)}, u32[]{:S(2)}, u32[]{:S(2)}) collective-permute-start(f32[16,8,128]{2,1,0:T(8,128)} %get-tuple-element.40), channel_id=1, source_target_pairs={{0,8},{8,16},{16,24},{1,9},{9,17},{17,25},{2,10},{10,18},{18,26},{... | collective-permute-start | bytes 196616 | tf_op jit(solution)/shard_map/ppermute | solution.py:645
  147.7 4.7 collective-permute-start.2
  152.5 1.3 collective-permute-start.3
  153.8 1.5 constant_dynamic-update-slice_fusion
  155.2 2.3 select_dynamic-update-slice_fusion.3
  157.5 3.9 select_dynamic-update-slice_fusion.2
  162.1 1.6 collective-permute-done.7.refs_1_
  163.7 2.0 collective-permute-start.8
  165.7 1.3 collective-permute-start.9
  167.0 4.4 select_dynamic-update-slice_fusion.1
  171.4 18.5 %field.1 = (f32[8192,128]{1,0:T(8,128)}, f32[8192,128]{1,0:T(8,128)}, f32[8192,128]{1,0:T(8,128)}, bf16[1024,1024]{1,0:T(8,128)(2,1)}) custom-call(bf16[8,1,128,1024]{3,2,1,0:T(8,128)(2,1)} %all-to-all-done.2.x_ref, bf16[8,288,1024]{2,1,0:T(8,128)(2,1)} %all-to-all-done.1.refs_1_.x_ref.rim_ref, f32[3,7,8,128]{3,2,1,0:T(8,128)} %reshape_reshape.7.taps_ref, ...), custom_call_target="tpu_custom_call" | custom-call | tf_op jit(solution)/shard_map/field/pallas_call | solution.py:354
  189.9 12.9 %convolution_convert_fusion = bf16[4096,1024]{1,0:T(8,128)(2,1)S(1)} fusion(bf16[1024,4096]{1,0:T(8,128)(2,1)} %all-gather.2.cloned.1.call-done, bf16[1024,1024]{1,0:T(8,128)(2,1)} %get-tuple-element.41.x_ref), kind=kOutput, calls=%fused_computation | convolution fusion | flops 8594128896 | bytes 18874368 | tf_op jit(solution)/shard_map/dot_general | solution.py:680
  202.8 2.8 constant_dynamic-slice_fusion
  205.6 1.9 copy-done.4
  207.5 6.3 %collective-permute-done.9.refs_1_ = bf16[1024,1024]{1,0:T(8,128)(2,1)} collective-permute-done((bf16[1024,1024]{1,0:T(8,128)(2,1)}, bf16[1024,1024]{1,0:T(8,128)(2,1)}, u32[]{:S(2)}, u32[]{:S(2)}) %collective-permute-start.9) | collective-permute-done | bytes 2097184 | tf_op jit(solution)/shard_map/ppermute | solution.py:500
  213.9 4.4 select_dynamic-update-slice_fusion.w_ref
  218.3 14.4 %project.1.hold_ref.refs_0_ = bf16[1024,4096]{1,0:T(8,128)(2,1)} custom-call(bf16[1024,1024]{1,0:T(8,128)(2,1)} %get-tuple-element.41.x_ref, bf16[4096,1024]{1,0:T(8,128)(2,1)} %select_dynamic-update-slice_fusion.w_ref), custom_call_target="tpu_custom_call" | custom-call | tf_op jit(solution)/shard_map/project/pallas_call | solution.py:354
  232.7 15.0 %fusion.4.up_ref = f32[1024,1024]{1,0:T(8,128)} fusion(bf16[1024,4096]{1,0:T(8,128)(2,1)} %all-gather.2.cloned.1.call-done, bf16[4096,1024]{1,0:T(8,128)(2,1)} %select_dynamic-update-slice_fusion.w_ref), kind=kOutput, calls=%fused_computation.35 | convolution fusion | flops 8589934592 | bytes 20971520 | tf_op jit(solution)/shard_map/dot_general | solution.py:689
  247.7 13.3 %cotangent.1 = (f32[8192,128]{1,0:T(8,128)}, f32[8192,128]{1,0:T(8,128)}, f32[384,128]{1,0:T(8,128)}, f32[16,8,128]{2,1,0:T(8,128)}, f32[8,128]{1,0:T(8,128)}) custom-call(f32[1024,1024]{1,0:T(8,128)} %fusion.4.up_ref, f32[8192,128]{1,0:T(8,128)} %get-tuple-element.47.sm_ref, f32[8192,128]{1,0:T(8,128)} %get-tuple-element.39.mixed_ref, ...), custom_call_target="tpu_custom_call" | custom-call | tf_op jit(solution)/shard_map/cotangent/pallas_call | solution.py:354
  261.1 1.5 collective-permute-start.10
  262.6 2.0 collective-permute-start.11
  264.6 40.9 %collective-permute-done.10.refs_2_.refs_0_ = bf16[1024,1024]{1,0:T(8,128)(2,1)S(1)} collective-permute-done((bf16[1024,1024]{1,0:T(8,128)(2,1)}, bf16[1024,1024]{1,0:T(8,128)(2,1)S(1)}, u32[]{:S(2)}, u32[]{:S(2)}) %collective-permute-start.10) | collective-permute-done | bytes 2097184 | tf_op jit(solution)/shard_map/ppermute | solution.py:546
  305.5 1.3 copy-done.5
  306.8 1.3 collective-permute-start.12
  308.1 1.3 collective-permute-start.13
  309.4 1.5 collective-permute-start.14
  311.4 4.5 collective-permute-done.12
  316.5 2.0 collective-permute-done.13
  319.9 6.9 %add_convert_fusion.3 = (bf16[1024,1024]{1,0:T(8,128)(2,1)S(1)}, bf16[1024,1024]{1,0:T(8,128)(2,1)}) fusion(bf16[1024,1024]{1,0:T(8,128)(2,1)} %get-tuple-element.60, bf16[4096,1024]{1,0:T(8,128)(2,1)} %copy-done.4, s32[]{:T(128)S(6)} %select_n.134, bf16[1024,1024]{1,0:T(8,128)(2,1)} %get-tuple-element.59, s32[]{:T(128)S(6)} %select_n.133), kind=kLoop, calls=%fused_computation.4 | loop fusion | flops 8388608 | bytes 12582920 | tf_op jit(solution)/shard_map/convert_element_type | solution.py:545
  326.8 3.2 collective-permute-start.15
  330.0 2.0 collective-permute-start.16
  331.9 30.5 %back.1 = (bf16[8,3,128,1024]{3,2,1,0:T(8,128)(2,1)}, f32[3,7,8,128]{3,2,1,0:T(8,128)}) custom-call(f32[8192,128]{1,0:T(8,128)} %get-tuple-element.51.grad_ref, f32[8192,128]{1,0:T(8,128)} %get-tuple-element.52.zero_ref, f32[2,8192,128]{2,1,0:T(8,128)} %get-tuple-element.49.heads_ref.sm_ref, f32[8192,128]{1,0:T(8,128)} %get-tuple-element.53.first_ref, ...), custom_call_target="tpu_custom_call" | custom-call | tf_op jit(solution)/shard_map/back/pallas_call | solution.py:354
  362.4 6.3 %all-to-all-start.3 = ((bf16[8,3,128,1024]{3,2,1,0:T(8,128)(2,1)}), bf16[8,3,128,1024]{3,2,1,0:T(8,128)(2,1)}, u32[]{:S(2)}, u32[]{:S(2)}) async-start(bf16[8,3,128,1024]{3,2,1,0:T(8,128)(2,1)} %get-tuple-element.58), calls=%async_computation.4 | async-start | bytes 12582912 | tf_op jit(solution)/shard_map/all_to_all | solution.py:760
  368.7 1.3 collective-permute-done.15.refs_0_
  370.1 6.9 %add_convert_fusion.2 = (bf16[1024,1024]{1,0:T(8,128)(2,1)S(1)}, bf16[1024,1024]{1,0:T(8,128)(2,1)}) fusion(bf16[1024,1024]{1,0:T(8,128)(2,1)} %get-tuple-element.62, bf16[4096,1024]{1,0:T(8,128)(2,1)} %copy-done.4, s32[]{:T(128)S(6)} %select_n.132, bf16[1024,1024]{1,0:T(8,128)(2,1)} %get-tuple-element.63, s32[]{:T(128)S(6)} %select_n.135), kind=kLoop, calls=%fused_computation.3 | loop fusion | flops 8388608 | bytes 12582920 | tf_op jit(solution)/shard_map/convert_element_type | solution.py:544
  377.0 1.3 collective-permute-start.18
  378.3 7.1 %collective-permute-start.17 = (bf16[1024,1024]{1,0:T(8,128)(2,1)S(1)}, bf16[1024,1024]{1,0:T(8,128)(2,1)}, u32[]{:S(2)}, u32[]{:S(2)}) collective-permute-start(bf16[1024,1024]{1,0:T(8,128)(2,1)S(1)} %get-tuple-element.67), channel_id=1, source_target_pairs={{0,8},{8,16},{16,24},{1,9},{9,17},{17,25},{2,10},{10,18},{18,26},{... | collective-permute-start | bytes 6291464 | tf_op jit(solution)/shard_map/ppermute | solution.py:546
  386.4 1.7 collective-permute-start.20
  388.1 1.5 collective-permute-start.19
  389.6 38.6 %collective-permute-done.21 = f32[8,1024]{1,0:T(8,128)S(1)} collective-permute-done((f32[8,1024]{1,0:T(8,128)S(1)}, f32[8,1024]{1,0:T(8,128)S(1)}, u32[]{:S(2)}, u32[]{:S(2)}) %collective-permute-start.21) | collective-permute-done | bytes 32800 | tf_op jit(solution)/shard_map/ppermute | solution.py:768
  429.0 4.3 add_convert_fusion
  433.3 1.6 maximum_bitcast_fusion.refs_0_
  435.0 5.4 %all-to-all-done.3.refs_0_ = bf16[8,3,128,1024]{3,2,1,0:T(8,128)(2,1)} async-done(((bf16[8,3,128,1024]{3,2,1,0:T(8,128)(2,1)}), bf16[8,3,128,1024]{3,2,1,0:T(8,128)(2,1)}, u32[]{:S(2)}, u32[]{:S(2)}) %all-to-all-start.3) | async-done | bytes 6291488 | tf_op jit(solution)/shard_map/all_to_all | solution.py:760
  440.4 3.6 all-to-all-start.4
  444.0 7.8 %join.2 = bf16[3,128,8192]{2,1,0:T(8,128)(2,1)} custom-call(bf16[8,3,128,1024]{3,2,1,0:T(8,128)(2,1)} %all-to-all-done.3.refs_0_), custom_call_target="tpu_custom_call" | custom-call | tf_op jit(solution)/shard_map/join/pallas_call | solution.py:354
  451.9 21.6 %all-to-all-done.4.refs_0_ = bf16[8,1,144,1024]{3,2,1,0:T(8,128)(2,1)S(1)} async-done(((bf16[8,1,144,1024]{3,2,1,0:T(8,128)(2,1)}), bf16[8,1,144,1024]{3,2,1,0:T(8,128)(2,1)S(1)}, u32[]{:S(2)}, u32[]{:S(2)}) %all-to-all-start.4) | async-done | bytes 2359328 | tf_op jit(solution)/shard_map/all_to_all | solution.py:780
  475.4 6.0 %join.3 = f32[1,128,8192]{2,1,0:T(8,128)} custom-call(bf16[8,1,144,1024]{3,2,1,0:T(8,128)(2,1)} %copy-done.6), custom_call_target="tpu_custom_call" | custom-call | tf_op jit(solution)/shard_map/join/pallas_call | solution.py:354
  (86 shorter events, 13.8 us)
Async XLA Ops:
  7.2 106.7 %copy-start = (f32[3,7,512]{2,1,0:T(8,128)S(1)}, f32[3,7,512]{2,1,0:T(8,128)}, u32[]{:S(2)}) copy-start(f32[3,7,512]{2,1,0:T(8,128)} %param.8) | copy-start | bytes 129028
  15.1 31.8 %all-to-all-start = ((bf16[8,1,128,1024]{3,2,1,0:T(8,128)(2,1)}), bf16[8,1,128,1024]{3,2,1,0:T(8,128)(2,1)S(1)}, u32[]{:S(2)}, u32[]{:S(2)}) async-start(bf16[8,1,128,1024]{3,2,1,0:T(8,128)(2,1)} %split.1), calls=%async_computation | async-start | bytes 4194304 | tf_op jit(solution)/shard_map/all_to_all | solution.py:583
  21.3 0.7 collective-permute-start
  22.0 0.8 copy-start.9
  46.9 1.3 copy-start.2
  48.3 4.8 copy-start.3
  48.3 62.3 %all-to-all-start.1 = ((bf16[8,288,1024]{2,1,0:T(8,128)(2,1)}), bf16[8,288,1024]{2,1,0:T(8,128)(2,1)}, u32[]{:S(2)}, u32[]{:S(2)}) async-start(bf16[8,288,1024]{2,1,0:T(8,128)(2,1)} %get-tuple-element.38), calls=%async_computation.1 | async-start | bytes 9437184 | tf_op jit(solution)/shard_map/all_to_all | solution.py:586
  53.1 136.8 %all-gather.2.cloned.1.call-start = ((), (), s32[]{:S(2)}) async-start(), calls=%async_computation.6 | async-start | bytes 9437184 | tf_op jit(solution)/shard_map/all_gather | solution.py:617
  53.1 53.1 %collective-permute-start.4 = (bf16[1024,1024]{1,0:T(8,128)(2,1)S(1)}, bf16[1024,1024]{1,0:T(8,128)(2,1)S(1)}, u32[]{:S(2)}, u32[]{:S(2)}) collective-permute-start(bf16[1024,1024]{1,0:T(8,128)(2,1)S(1)} %bitcast.38), channel_id=1, source_target_pairs={{0,8},{8,16},{16,24},{1,9},{9,17},{17,25},{2,10},{10,18},{18,26},{... | collective-permute-start | bytes 6291464 | tf_op jit(solution)/shard_map/ppermute | solution.py:499
  61.0 49.6 %collective-permute-start.5 = (bf16[1024,1024]{1,0:T(8,128)(2,1)S(1)}, bf16[1024,1024]{1,0:T(8,128)(2,1)}, u32[]{:S(2)}, u32[]{:S(2)}) collective-permute-start(bf16[1024,1024]{1,0:T(8,128)(2,1)S(1)} %bitcast.39), channel_id=1, source_target_pairs={{8,0},{16,8},{24,16},{9,1},{17,9},{25,17},{10,2},{18,10},{26,18},{... | collective-permute-start | bytes 6291464 | tf_op jit(solution)/shard_map/ppermute | solution.py:500
  106.2 1.3 copy-start.7
  110.6 51.5 %collective-permute-start.6 = (bf16[1024,1024]{1,0:T(8,128)(2,1)}, bf16[1024,1024]{1,0:T(8,128)(2,1)}, u32[]{:S(2)}, u32[]{:S(2)}) collective-permute-start(bf16[1024,1024]{1,0:T(8,128)(2,1)} %copy-done.7), channel_id=1, source_target_pairs={{8,16},{16,24},{9,17},{17,25},{10,18},{18,26},{11,19},{19,27},{12,... | collective-permute-start | bytes 6291464 | tf_op jit(solution)/shard_map/ppermute | solution.py:499
  112.5 51.2 %collective-permute-start.7 = (bf16[1024,1024]{1,0:T(8,128)(2,1)}, bf16[1024,1024]{1,0:T(8,128)(2,1)}, u32[]{:S(2)}, u32[]{:S(2)}) collective-permute-start(bf16[1024,1024]{1,0:T(8,128)(2,1)} %collective-permute-done.5.refs_3_), channel_id=1, source_target_pairs={{8,0},{16,8},{9,1},{17,9},{10,2},{18,10},{11,3},{19,11},{12,4},{20... | collective-permute-start | bytes 6291464 | tf_op jit(solution)/shard_map/ppermute | solution.py:500
  115.1 56.3 %all-to-all-start.2 = ((bf16[8,1,128,1024]{3,2,1,0:T(8,128)(2,1)}), bf16[8,1,128,1024]{3,2,1,0:T(8,128)(2,1)}, u32[]{:S(2)}, u32[]{:S(2)}) async-start(bf16[8,1,128,1024]{3,2,1,0:T(8,128)(2,1)} %tie.11), calls=%async_computation.2 | async-start | bytes 4194304 | tf_op jit(solution)/shard_map/all_to_all | solution.py:588
  119.5 315.5 %reduce-scatter.2.cloned.1.call-start = ((), (), s32[]{:S(2)}) async-start(), calls=%async_computation.7 | async-start | bytes 9437184 | tf_op jit(solution)/shard_map/reduce_scatter | solution.py:720
  139.2 16.0 %copy-start.8 = (bf16[1024,1024]{1,0:T(8,128)(2,1)S(1)}, bf16[1024,1024]{1,0:T(8,128)(2,1)}, u32[]{:S(2)}) copy-start(bf16[1024,1024]{1,0:T(8,128)(2,1)} %copy-done.7) | copy-start | bytes 6291460
  139.2 22.3 %collective-permute-start.1 = (f32[16,8,128]{2,1,0:T(8,128)}, f32[16,8,128]{2,1,0:T(8,128)S(1)}, u32[]{:S(2)}, u32[]{:S(2)}) collective-permute-start(f32[16,8,128]{2,1,0:T(8,128)} %get-tuple-element.40), channel_id=1, source_target_pairs={{0,8},{8,16},{16,24},{1,9},{9,17},{17,25},{2,10},{10,18},{18,26},{... | collective-permute-start | bytes 196616 | tf_op jit(solution)/shard_map/ppermute | solution.py:645
  147.7 13.7 %collective-permute-start.2 = (f32[16,8,128]{2,1,0:T(8,128)}, f32[16,8,128]{2,1,0:T(8,128)S(1)}, u32[]{:S(2)}, u32[]{:S(2)}) collective-permute-start(f32[16,8,128]{2,1,0:T(8,128)} %get-tuple-element.40), channel_id=1, source_target_pairs={{0,16},{8,24},{1,17},{9,25},{2,18},{10,26},{3,19},{11,27},{4,20},{... | collective-permute-start | bytes 196616 | tf_op jit(solution)/shard_map/ppermute | solution.py:645
  152.5 9.0 %collective-permute-start.3 = (f32[16,8,128]{2,1,0:T(8,128)}, f32[16,8,128]{2,1,0:T(8,128)S(1)}, u32[]{:S(2)}, u32[]{:S(2)}) collective-permute-start(f32[16,8,128]{2,1,0:T(8,128)} %get-tuple-element.40), channel_id=1, source_target_pairs={{0,24},{1,25},{2,26},{3,27},{4,28},{5,29},{6,30},{7,31}} | collective-permute-start | bytes 196616 | tf_op jit(solution)/shard_map/ppermute | solution.py:645
  163.7 43.8 %collective-permute-start.8 = (bf16[1024,1024]{1,0:T(8,128)(2,1)}, bf16[1024,1024]{1,0:T(8,128)(2,1)}, u32[]{:S(2)}, u32[]{:S(2)}) collective-permute-start(bf16[1024,1024]{1,0:T(8,128)(2,1)} %get-tuple-element.43), channel_id=1, source_target_pairs={{16,24},{17,25},{18,26},{19,27},{20,28},{21,29},{22,30},{23,31}} | collective-permute-start | bytes 6291464 | tf_op jit(solution)/shard_map/ppermute | solution.py:499
  165.7 48.2 %collective-permute-start.9 = (bf16[1024,1024]{1,0:T(8,128)(2,1)}, bf16[1024,1024]{1,0:T(8,128)(2,1)}, u32[]{:S(2)}, u32[]{:S(2)}) collective-permute-start(bf16[1024,1024]{1,0:T(8,128)(2,1)} %get-tuple-element.44), channel_id=1, source_target_pairs={{8,0},{9,1},{10,2},{11,3},{12,4},{13,5},{14,6},{15,7}} | collective-permute-start | bytes 6291464 | tf_op jit(solution)/shard_map/ppermute | solution.py:500
  202.8 4.7 copy-start.4
  261.1 44.4 %collective-permute-start.10 = (bf16[1024,1024]{1,0:T(8,128)(2,1)}, bf16[1024,1024]{1,0:T(8,128)(2,1)S(1)}, u32[]{:S(2)}, u32[]{:S(2)}) collective-permute-start(bf16[1024,1024]{1,0:T(8,128)(2,1)} %get-tuple-element.72.refs_2_), channel_id=1, source_target_pairs={{0,8},{1,9},{2,10},{3,11},{4,12},{5,13},{6,14},{7,15}} | collective-permute-start | bytes 6291464 | tf_op jit(solution)/shard_map/ppermute | solution.py:546
  262.6 42.9 %collective-permute-start.11 = (bf16[1024,1024]{1,0:T(8,128)(2,1)}, bf16[1024,1024]{1,0:T(8,128)(2,1)}, u32[]{:S(2)}, u32[]{:S(2)}) collective-permute-start(bf16[1024,1024]{1,0:T(8,128)(2,1)} %get-tuple-element.71.refs_3_), channel_id=1, source_target_pairs={{24,16},{25,17},{26,18},{27,19},{28,20},{29,21},{30,22},{31,23}} | collective-permute-start | bytes 6291464 | tf_op jit(solution)/shard_map/ppermute | solution.py:547
  305.5 1.3 copy-start.5
  306.8 9.0 %collective-permute-start.12 = (f32[384,128]{1,0:T(8,128)}, f32[384,128]{1,0:T(8,128)S(1)}, u32[]{:S(2)}, u32[]{:S(2)}) collective-permute-start(f32[384,128]{1,0:T(8,128)} %get-tuple-element.56), channel_id=1, source_target_pairs={{8,0},{16,8},{24,16},{9,1},{17,9},{25,17},{10,2},{18,10},{26,18},{... | collective-permute-start | bytes 589832 | tf_op jit(solution)/shard_map/ppermute | solution.py:645
  308.1 10.4 %collective-permute-start.13 = (f32[16,8,128]{2,1,0:T(8,128)}, f32[16,8,128]{2,1,0:T(8,128)S(1)}, u32[]{:S(2)}, u32[]{:S(2)}) collective-permute-start(f32[16,8,128]{2,1,0:T(8,128)} %get-tuple-element.57), channel_id=1, source_target_pairs={{16,0},{24,8},{17,1},{25,9},{18,2},{26,10},{19,3},{27,11},{20,4},{... | collective-permute-start | bytes 196616 | tf_op jit(solution)/shard_map/ppermute | solution.py:645
  309.4 9.8 %collective-permute-start.14 = (f32[16,8,128]{2,1,0:T(8,128)}, f32[16,8,128]{2,1,0:T(8,128)S(1)}, u32[]{:S(2)}, u32[]{:S(2)}) collective-permute-start(f32[16,8,128]{2,1,0:T(8,128)} %get-tuple-element.57), channel_id=1, source_target_pairs={{24,0},{25,1},{26,2},{27,3},{28,4},{29,5},{30,6},{31,7}} | collective-permute-start | bytes 196616 | tf_op jit(solution)/shard_map/ppermute | solution.py:645
  326.8 43.2 %collective-permute-start.15 = (bf16[1024,1024]{1,0:T(8,128)(2,1)}, bf16[1024,1024]{1,0:T(8,128)(2,1)}, u32[]{:S(2)}, u32[]{:S(2)}) collective-permute-start(bf16[1024,1024]{1,0:T(8,128)(2,1)} %get-tuple-element.70), channel_id=1, source_target_pairs={{0,8},{8,16},{1,9},{9,17},{2,10},{10,18},{3,11},{11,19},{4,12},{12... | collective-permute-start | bytes 6291464 | tf_op jit(solution)/shard_map/ppermute | solution.py:546
  330.0 40.1 %collective-permute-start.16 = (bf16[1024,1024]{1,0:T(8,128)(2,1)S(1)}, bf16[1024,1024]{1,0:T(8,128)(2,1)}, u32[]{:S(2)}, u32[]{:S(2)}) collective-permute-start(bf16[1024,1024]{1,0:T(8,128)(2,1)S(1)} %get-tuple-element.69), channel_id=1, source_target_pairs={{24,16},{16,8},{25,17},{17,9},{26,18},{18,10},{27,19},{19,11},{28,... | collective-permute-start | bytes 6291464 | tf_op jit(solution)/shard_map/ppermute | solution.py:547
  362.4 78.0 %all-to-all-start.3 = ((bf16[8,3,128,1024]{3,2,1,0:T(8,128)(2,1)}), bf16[8,3,128,1024]{3,2,1,0:T(8,128)(2,1)}, u32[]{:S(2)}, u32[]{:S(2)}) async-start(bf16[8,3,128,1024]{3,2,1,0:T(8,128)(2,1)} %get-tuple-element.58), calls=%async_computation.4 | async-start | bytes 12582912 | tf_op jit(solution)/shard_map/all_to_all | solution.py:760
  370.1 15.3 %copy-start.10 = (f32[3,7,8,128]{3,2,1,0:T(8,128)S(1)}, f32[3,7,8,128]{3,2,1,0:T(8,128)}, u32[]{:S(2)}) copy-start(f32[3,7,8,128]{3,2,1,0:T(8,128)} %get-tuple-element.61.refs_2_) | copy-start | bytes 258052
  370.1 15.8 %copy-start.11 = (f32[8,128]{1,0:T(8,128)S(1)}, f32[8,128]{1,0:T(8,128)}, u32[]{:S(2)}) copy-start(f32[8,128]{1,0:T(8,128)} %get-tuple-element.64) | copy-start | bytes 12292
  377.0 51.9 %collective-permute-start.18 = (bf16[1024,1024]{1,0:T(8,128)(2,1)}, bf16[1024,1024]{1,0:T(8,128)(2,1)}, u32[]{:S(2)}, u32[]{:S(2)}) collective-permute-start(bf16[1024,1024]{1,0:T(8,128)(2,1)} %get-tuple-element.68), channel_id=1, source_target_pairs={{24,16},{16,8},{8,0},{25,17},{17,9},{9,1},{26,18},{18,10},{10,2},{... | collective-permute-start | bytes 6291464 | tf_op jit(solution)/shard_map/ppermute | solution.py:547
  378.3 50.7 %collective-permute-start.17 = (bf16[1024,1024]{1,0:T(8,128)(2,1)S(1)}, bf16[1024,1024]{1,0:T(8,128)(2,1)}, u32[]{:S(2)}, u32[]{:S(2)}) collective-permute-start(bf16[1024,1024]{1,0:T(8,128)(2,1)S(1)} %get-tuple-element.67), channel_id=1, source_target_pairs={{0,8},{8,16},{16,24},{1,9},{9,17},{17,25},{2,10},{10,18},{18,26},{... | collective-permute-start | bytes 6291464 | tf_op jit(solution)/shard_map/ppermute | solution.py:546
  385.9 42.3 %collective-permute-start.21 = (f32[8,1024]{1,0:T(8,128)S(1)}, f32[8,1024]{1,0:T(8,128)S(1)}, u32[]{:S(2)}, u32[]{:S(2)}) collective-permute-start(f32[8,1024]{1,0:T(8,128)S(1)} %pad.9), channel_id=1, source_target_pairs={{0,24},{8,0},{16,8},{24,16},{1,25},{9,1},{17,9},{25,17},{2,26},{10... | collective-permute-start | bytes 98312 | tf_op jit(solution)/shard_map/ppermute | solution.py:768
  386.4 42.2 %collective-permute-start.20 = (f32[8,1024]{1,0:T(8,128)S(1)}, f32[8,1024]{1,0:T(8,128)S(1)}, u32[]{:S(2)}, u32[]{:S(2)}) collective-permute-start(f32[8,1024]{1,0:T(8,128)S(1)} %pad.9), channel_id=1, source_target_pairs={{0,16},{8,24},{16,0},{24,8},{1,17},{9,25},{17,1},{25,9},{2,18},{10... | collective-permute-start | bytes 98312 | tf_op jit(solution)/shard_map/ppermute | solution.py:768
  388.1 40.8 %collective-permute-start.19 = (f32[8,1024]{1,0:T(8,128)S(1)}, f32[8,1024]{1,0:T(8,128)S(1)}, u32[]{:S(2)}, u32[]{:S(2)}) collective-permute-start(f32[8,1024]{1,0:T(8,128)S(1)} %pad.9), channel_id=1, source_target_pairs={{0,8},{8,16},{16,24},{24,0},{1,9},{9,17},{17,25},{25,1},{2,10},{10... | collective-permute-start | bytes 98312 | tf_op jit(solution)/shard_map/ppermute | solution.py:768
  440.4 33.0 %all-to-all-start.4 = ((bf16[8,1,144,1024]{3,2,1,0:T(8,128)(2,1)}), bf16[8,1,144,1024]{3,2,1,0:T(8,128)(2,1)S(1)}, u32[]{:S(2)}, u32[]{:S(2)}) async-start(bf16[8,1,144,1024]{3,2,1,0:T(8,128)(2,1)} %tie.19), calls=%async_computation.5 | async-start | bytes 4718592 | tf_op jit(solution)/shard_map/all_to_all | solution.py:780
  473.4 2.0 copy-start.6
  474.8 6.6 %copy-start.1 = (f32[3,7,512]{2,1,0:T(8,128)S(1)}, f32[3,7,512]{2,1,0:T(8,128)}, u32[]{:S(2)}) copy-start(f32[3,7,512]{2,1,0:T(8,128)} %param.8) | copy-start | bytes 129028
Sparse Core Ops, SparseCore 0:
  110.7 76.1 all-gather.1
  261.2 73.2 reduce-scatter.1
